TPU v7x, 128 devices: a whole 4x4x4 slice. The times are simulated.
128 devices in a mesh: row: 16 (over z, y_hi, core), col: 8 (over x, y_lo).
Axes of the slice: x: 4, y: 4 (y_hi: 2, y_lo: 2; y = y_hi * 2 + y_lo), z: 4, core: 2. Of those that a mesh axis runs over, the one named last changes fastest.
Arguments:
- source_embed: bfloat16 [40, 24576], P(None, ('row', 'col')), may hold values from -4 to 4
- target_embed: bfloat16 [40, 24576], P(None, ('row', 'col')), may hold values from -4 to 4
- features: bfloat16 [24576, 128], P(('row', 'col')), may hold values from -6 to 6
- cotangent: bfloat16 [24576, 128], P(('row', 'col')), may hold values from -6 to 6
Outputs:
- hop_output: bfloat16 [24576, 128], P(('row', 'col'))
- grad_features: bfloat16 [24576, 128], P(('row', 'col'))
- grad_source: float32 [40, 24576], P(None, ('row', 'col'))
- grad_target: float32 [40, 24576], P(None, ('row', 'col'))
All inputs are finite; a program needn't handle non-finite values.
Results may differ from a plain program's by a relative error of at most 0.015.
Values may be sent and summed in bfloat16 or wider, within the bound.
No kernel may reach another device: no remote copies, remote signals or barrier semaphores. Data moves between devices by JAX's collectives and lax.ppermute only.
A program may use at most 64 MiB of HBM per device.

v0:
```python
import math

import jax
import jax.numpy as jnp
from jax import lax
from jax.sharding import PartitionSpec as P


def local(source_embed, target_embed, features, cotangent):
    src_rows, feat_rows, cot_rows = (
        lax.all_gather(source_embed, "col", axis=1, tiled=True),
        lax.all_gather(features, "col", axis=0, tiled=True),
        lax.all_gather(cotangent, "col", axis=0, tiled=True),
    )
    dst_cols, feat_cols, cot_cols = (
        lax.all_gather(target_embed, "row", axis=1, tiled=True),
        lax.all_gather(features, "row", axis=0, tiled=True),
        lax.all_gather(cotangent, "row", axis=0, tiled=True),
    )
    row_count = feat_rows.shape[0]
    col_count = feat_cols.shape[0]
    feat_count = feat_rows.shape[1]
    emb_count = src_rows.shape[0]
    block_width = math.gcd(col_count, 512)
    block_ids = jnp.arange(col_count // block_width, dtype=jnp.int32)
    pair_rows = jnp.concatenate([cot_rows, feat_rows], axis=1)
    pair_cols = jnp.concatenate([feat_cols, cot_cols], axis=1)

    def score_tile(block_index):
        first_col = block_index * block_width
        dst_block = lax.dynamic_slice_in_dim(dst_cols, first_col, block_width, 1)
        scores = lax.dot_general(
            src_rows, dst_block, (((0,), (0,)), ((), ())), preferred_element_type=jnp.float32
        )
        return (scores, dst_block, first_col)

    def outer_of(first_col):
        pair_block = lax.dynamic_slice_in_dim(pair_cols, first_col, block_width, 0)
        return lax.dot_general(
            pair_rows, pair_block, (((1,), (1,)), ((), ())), preferred_element_type=jnp.float32
        )

    zero_rows = jnp.zeros((row_count,), jnp.float32)

    def peak_step(row_peak, block_index):
        scores, dst_block, first_col = score_tile(block_index)
        return (jnp.maximum(row_peak, jnp.max(jnp.maximum(scores, 0.0), axis=1)), None)

    row_peak, unused = lax.scan(peak_step, zero_rows, block_ids)
    row_peak = lax.pmax(row_peak, "col")

    def total_step(row_total, block_index):
        scores, dst_block, first_col = score_tile(block_index)
        lifted = jnp.exp(jnp.maximum(scores, 0.0) - row_peak[:, None])
        return (row_total + jnp.sum(lifted, axis=1), None)

    row_total, unused = lax.scan(total_step, zero_rows, block_ids)
    row_total = lax.psum(row_total, "col")

    def soft_tile(block_index):
        scores, dst_block, first_col = score_tile(block_index)
        lifted = jnp.exp(jnp.maximum(scores, 0.0) - row_peak[:, None])
        soft = lifted / row_total[:, None]
        return (scores, dst_block, first_col, soft)

    def forward_step(fwd_rows, block_index):
        scores, dst_block, first_col, soft = soft_tile(block_index)
        soft_half = soft.astype(jnp.bfloat16)
        feat_block = lax.dynamic_slice_in_dim(feat_cols, first_col, block_width, 0)
        fwd_rows = fwd_rows + jnp.dot(soft_half, feat_block, preferred_element_type=jnp.float32)
        reverse_block = lax.dot_general(
            soft_half, feat_rows, (((0,), (0,)), ((), ())), preferred_element_type=jnp.float32
        )
        return (fwd_rows, reverse_block)

    fwd_rows, reverse_blocks = lax.scan(
        forward_step, jnp.zeros((row_count, feat_count), jnp.float32), block_ids
    )
    fwd_cols = reverse_blocks.reshape(col_count, feat_count)
    own_forward = lax.psum_scatter(fwd_rows, "col", scatter_dimension=0, tiled=True)
    own_reverse = lax.psum_scatter(
        fwd_cols.astype(jnp.bfloat16), "row", scatter_dimension=0, tiled=True
    ).astype(jnp.float32)
    hop_output = (own_forward + own_reverse).astype(jnp.bfloat16)

    def outer_tile(block_index):
        scores, dst_block, first_col, soft = soft_tile(block_index)
        return (scores, dst_block, first_col, soft, outer_of(first_col))

    def delta_step(row_delta, block_index):
        scores, dst_block, first_col, soft, outer_grad = outer_tile(block_index)
        return (row_delta + jnp.sum(soft * outer_grad, axis=1), None)

    row_delta, unused = lax.scan(delta_step, zero_rows, block_ids)
    row_delta = lax.psum(row_delta, "col")

    def backward_step(carry, block_index):
        back_rows, embed_rows = carry
        scores, dst_block, first_col, soft, outer_grad = outer_tile(block_index)
        score_grad = jnp.where(scores > 0.0, soft * (outer_grad - row_delta[:, None]), 0.0)
        score_half = score_grad.astype(jnp.bfloat16)
        soft_half = soft.astype(jnp.bfloat16)
        cot_block = lax.dynamic_slice_in_dim(cot_cols, first_col, block_width, 0)
        back_rows = back_rows + jnp.dot(soft_half, cot_block, preferred_element_type=jnp.float32)
        back_block = lax.dot_general(
            soft_half, cot_rows, (((0,), (0,)), ((), ())), preferred_element_type=jnp.float32
        )
        embed_rows = embed_rows + lax.dot_general(
            dst_block, score_half, (((1,), (1,)), ((), ())), preferred_element_type=jnp.float32
        )
        embed_block = jnp.dot(src_rows, score_half, preferred_element_type=jnp.float32)
        return ((back_rows, embed_rows), (back_block, embed_block))

    start_carry = (
        jnp.zeros((row_count, feat_count), jnp.float32),
        jnp.zeros((emb_count, row_count), jnp.float32),
    )
    (back_rows, embed_rows), (back_blocks, embed_blocks) = lax.scan(
        backward_step, start_carry, block_ids
    )
    back_cols = back_blocks.reshape(col_count, feat_count)
    embed_cols = jnp.transpose(embed_blocks, (1, 0, 2)).reshape(emb_count, col_count)
    grad_rows, grad_source = (
        lax.psum_scatter(back_rows, "col", scatter_dimension=0, tiled=True),
        lax.psum_scatter(embed_rows, "col", scatter_dimension=1, tiled=True),
    )
    grad_cols, grad_target = (
        lax.psum_scatter(back_cols, "row", scatter_dimension=0, tiled=True),
        lax.psum_scatter(embed_cols, "row", scatter_dimension=1, tiled=True),
    )
    grad_features = (grad_rows + grad_cols).astype(jnp.bfloat16)
    return (hop_output, grad_features, grad_source, grad_target)


def solution(mesh):
    in_specs = (
        P(None, ("row", "col")),
        P(None, ("row", "col")),
        P(("row", "col"), None),
        P(("row", "col"), None),
    )
    out_specs = (
        P(("row", "col"), None),
        P(("row", "col"), None),
        P(None, ("row", "col")),
        P(None, ("row", "col")),
    )
    return jax.shard_map(local, mesh=mesh, in_specs=in_specs, out_specs=out_specs, check_vma=False)
```

profile of v0, /device:TPU:0, one launch (start us, length us, event | category | flops | bytes accessed | tf_op | source)
XLA Modules:
  0.0 681.8 jit_solution(3920853521081071100)
XLA Ops:
  7.3 29.2 %all_gather.21 = bf16[1536,128]{1,0:T(8,128)(2,1)S(1)} all-gather(bf16[192,128]{1,0:T(8,128)(2,1)} %param.16), channel_id=1, replica_groups=mesh['row'=16,'col'=8] {'col'}, dimensions={0}, use_global_device_ids=true | all-gather | bytes 442368 | tf_op jit(solution)/shard_map/all_gather | solution.py:12
  36.4 29.4 %all_gather.20 = bf16[3072,128]{1,0:T(8,128)(2,1)S(1)} all-gather(bf16[192,128]{1,0:T(8,128)(2,1)} %param.16), channel_id=1, replica_groups=mesh['row'=16,'col'=8] {'row'}, dimensions={0}, use_global_device_ids=true | all-gather | bytes 835584 | tf_op jit(solution)/shard_map/all_gather | solution.py:17
  65.9 28.8 %all_gather.23 = bf16[1536,128]{1,0:T(8,128)(2,1)S(1)} all-gather(bf16[192,128]{1,0:T(8,128)(2,1)} %param.17), channel_id=1, replica_groups=mesh['row'=16,'col'=8] {'col'}, dimensions={0}, use_global_device_ids=true | all-gather | bytes 442368 | tf_op jit(solution)/shard_map/all_gather | solution.py:13
  94.7 24.0 %all_gather.22 = bf16[3072,128]{1,0:T(8,128)(2,1)S(1)} all-gather(bf16[192,128]{1,0:T(8,128)(2,1)} %param.17), channel_id=1, replica_groups=mesh['row'=16,'col'=8] {'row'}, dimensions={0}, use_global_device_ids=true | all-gather | bytes 835584 | tf_op jit(solution)/shard_map/all_gather | solution.py:18
  118.6 28.4 %all-gather.1 = bf16[8,192,40]{1,2,0:T(8,128)(2,1)S(1)} all-gather(bf16[1,192,40]{1,2,0:T(8,128)(2,1)} %bitcast.137), channel_id=1, replica_groups=mesh['row'=16,'col'=8] {'col'}, dimensions={0}, use_global_device_ids=true | all-gather | bytes 138240 | tf_op jit(solution)/shard_map/all_gather | solution.py:11
  148.8 22.6 %all-gather = bf16[16,192,40]{1,2,0:T(8,128)(2,1)S(1)} all-gather(bf16[1,192,40]{1,2,0:T(8,128)(2,1)} %bitcast.138), channel_id=1, replica_groups=mesh['row'=16,'col'=8] {'row'}, dimensions={0}, use_global_device_ids=true | all-gather | bytes 261120 | tf_op jit(solution)/shard_map/all_gather | solution.py:16
  172.3 2.0 reshape.37
  174.3 15.9 %while.68 = (s32[]{:T(128)}, f32[1536]{0:T(1024)S(1)}, s32[6]{0:T(128)S(1)}, bf16[40,3072]{1,0:T(8,128)(2,1)}, bf16[40,1536]{1,0:T(8,128)(2,1)S(1)}, /*index=5*/s32[1]{0:T(128)}) while((s32[]{:T(128)}, f32[1536]{0:T(1024)S(1)}, s32[6]{0:T(128)S(1)}, bf16[40,3072]{1,0:T(8,128)(2,1)}, bf16[40,1536]{1,0:T(8,128)(2,1)S(1)}, ...), condition=%wide.region_2.3_spmd.clone.clone, body=%wide.region_0.2_spmd.clone.sunk.clone | while | flops 64488964 | bytes 188565 | solution.py:49
  190.2 19.0 %pmax.7 = f32[1536]{0:T(1024)S(1)} all-reduce(f32[1536]{0:T(1024)S(1)} %get-tuple-element.243), channel_id=1, replica_groups=mesh['row'=16,'col'=8] {'col'}, use_global_device_ids=true, to_apply=%region_3.4 | all-reduce | flops 1536 | bytes 12288 | tf_op jit(solution)/shard_map/pmax | solution.py:50
  209.2 16.6 %while.69 = (s32[]{:T(128)}, f32[1536]{0:T(1024)S(1)}, s32[6]{0:T(128)S(1)}, bf16[40,3072]{1,0:T(8,128)(2,1)}, bf16[40,1536]{1,0:T(8,128)(2,1)S(1)}, /*index=5*/f32[1536]{0:T(1024)S(1)}, s32[1]{0:T(128)}) while((s32[]{:T(128)}, f32[1536]{0:T(1024)S(1)}, s32[6]{0:T(128)S(1)}, bf16[40,3072]{1,0:T(8,128)(2,1)}, ...), condition=%wide.region_6.7_spmd.clone.clone, body=%wide.region_4.6_spmd.clone.sunk.clone | while | flops 65275396 | bytes 194717 | solution.py:57
  225.8 16.2 %psum.14 = f32[1536]{0:T(1024)S(1)} all-reduce(f32[1536]{0:T(1024)S(1)} %get-tuple-element.244), channel_id=1, replica_groups=mesh['row'=16,'col'=8] {'col'}, use_global_device_ids=true, to_apply=%region_7.8 | all-reduce | flops 1536 | bytes 12288 | tf_op jit(solution)/shard_map/psum | solution.py:58
  243.7 26.1 %while.71 = (s32[]{:T(128)}, f32[1536]{0:T(1024)S(1)}, s32[6]{0:T(128)S(1)}, bf16[40,3072]{1,0:T(8,128)(2,1)}, bf16[40,1536]{1,0:T(8,128)(2,1)S(1)}, /*index=5*/...) while((s32[]{:T(128)}, f32[1536]{0:T(1024)S(1)}, ...), condition=%wide.region_14.15_spmd.clone.clone, body=%wide.region_12.14_spmd.clone.sunk.clone | while | flops 469501440 | bytes 10686677 | solution.py:94
  246.4 1.6 fusion.139
  250.8 1.6 fusion.139
  255.1 1.6 fusion.139
  259.5 1.6 fusion.139
  263.9 1.6 fusion.139
  268.2 1.6 fusion.139
  269.8 18.2 %psum.15 = f32[1536]{0:T(1024)S(1)} all-reduce(f32[1536]{0:T(1024)S(1)} %get-tuple-element.247), channel_id=1, replica_groups=mesh['row'=16,'col'=8] {'col'}, use_global_device_ids=true, to_apply=%region_15.16 | all-reduce | flops 1536 | bytes 12288 | tf_op jit(solution)/shard_map/psum | solution.py:95
  288.1 58.0 %while.72 = (s32[]{:T(128)}, f32[1536,128]{1,0:T(8,128)S(1)}, f32[40,1536]{1,0:T(8,128)S(1)}, f32[6,512,128]{2,1,0:T(8,128)}, f32[6,40,512]{2,1,0:T(8,128)}, /*i...) while((s32[]{:T(128)}, f32[1536,128]{1,0:T(8,128)S(1)}, ...), condition=%wide.region_17.18_spmd.clone.clone, body=%wide.region_16.17_spmd.clone.sunk.clone | while | flops 1004003328 | bytes 23214356 | solution.py:118
  289.3 1.6 fusion.151
  291.0 2.2 fusion.152
  299.0 1.6 fusion.151
  300.6 2.1 fusion.152
  308.6 1.6 fusion.151
  310.3 2.2 fusion.152
  318.3 1.6 fusion.151
  319.9 2.2 fusion.152
  328.0 1.6 fusion.151
  329.6 2.1 fusion.152
  337.6 1.6 fusion.151
  339.2 2.2 fusion.152
  347.3 2.7 copy.22
  351.0 29.8 %while.70 = (s32[]{:T(128)}, f32[1536,128]{1,0:T(8,128)S(1)}, bf16[6,512,128]{2,1,0:T(8,128)(2,1)}, s32[6]{0:T(128)S(1)}, bf16[40,3072]{1,0:T(8,128)(2,1)}, /*in...) while((s32[]{:T(128)}, f32[1536,128]{1,0:T(8,128)S(1)}, ...), condition=%wide.region_9.10_spmd.clone.clone, body=%wide.region_8.9_spmd.clone.sunk.clone | while | flops 469106688 | bytes 7254213 | solution.py:76
  352.3 1.5 divide_convert_fusion.3
  357.3 1.5 divide_convert_fusion.3
  362.2 1.5 divide_convert_fusion.3
  367.2 1.5 divide_convert_fusion.3
  372.2 1.5 divide_convert_fusion.3
  377.1 1.5 divide_convert_fusion.3
  383.0 1.6 copy.19
  384.6 68.7 %reduce-scatter.21.cloned.1.call-done = f32[192,40]{1,0:T(8,128)} async-done(((f32[3072,40]{1,0:T(8,128)}), f32[192,40]{1,0:T(8,128)}) %reduce-scatter.21.cloned.1.call-update) | async-done | bytes 30736
  453.3 1.6 copy.21
  454.9 67.3 %reduce-scatter.13.cloned.1.call-done = bf16[192,128]{1,0:T(8,128)(2,1)} async-done(((bf16[3072,128]{1,0:T(8,128)(2,1)}), bf16[192,128]{1,0:T(8,128)(2,1)}) %reduce-scatter.13.cloned.1.call-update) | async-done | bytes 49168 | tf_op jit(solution)/shard_map/reduce_scatter | solution.py:81
  522.2 39.8 %reduce-scatter.11.cloned.1.call-done = f32[192,128]{1,0:T(8,128)} async-done(((f32[1536,128]{1,0:T(8,128)}), f32[192,128]{1,0:T(8,128)}) %reduce-scatter.11.cloned.1.call-update) | async-done | bytes 98320 | tf_op jit(solution)/shard_map/reduce_scatter | solution.py:80
  563.5 37.8 %reduce-scatter.15.cloned.1.call-done = f32[192,128]{1,0:T(8,128)} async-done(((f32[1536,128]{1,0:T(8,128)}), f32[192,128]{1,0:T(8,128)}) %reduce-scatter.15.cloned.1.call-update) | async-done | bytes 98320 | tf_op jit(solution)/shard_map/reduce_scatter | solution.py:124
  601.4 72.0 %reduce-scatter.17.cloned.1.call-done = f32[192,128]{1,0:T(8,128)} async-done(((f32[3072,128]{1,0:T(8,128)}), f32[192,128]{1,0:T(8,128)}) %reduce-scatter.17.cloned.1.call-update) | async-done | bytes 98320 | tf_op jit(solution)/shard_map/reduce_scatter | solution.py:128
  673.4 1.6 add_convert_fusion
  (170 shorter events, 94.9 us)
Async XLA Ops:
  7.2 375.8 %reduce-scatter.19.cloned.1.call-start = ((), (), s32[]{:S(2)}) async-start(), calls=%async_computation.10 | async-start | bytes 884736
  242.3 0.9 copy-start.3
  242.5 1.2 copy-start.2
  244.9 1.5 copy-start.4
  249.3 1.5 copy-start.4
  253.7 1.5 copy-start.4
  258.0 1.5 copy-start.4
  262.4 1.5 copy-start.4
  266.7 1.5 copy-start.4
  289.3 1.6 copy-start.5
  299.0 1.6 copy-start.5
  308.6 1.6 copy-start.5
  318.3 1.6 copy-start.5
  327.9 1.6 copy-start.5
  337.6 1.6 copy-start.5
  346.0 5.0 copy-start
  347.2 106.1 %reduce-scatter.21.cloned.1.call-start = ((), (), s32[]{:S(2)}) async-start(), calls=%async_computation.11 | async-start | bytes 1671168
  350.0 172.2 %reduce-scatter.13.cloned.1.call-start = ((), (), s32[]{:S(2)}) async-start(), calls=%async_computation.7 | async-start | bytes 835584 | tf_op jit(solution)/shard_map/reduce_scatter | solution.py:81
  380.9 0.9 copy-start.1
  380.9 181.1 %reduce-scatter.11.cloned.1.call-start = ((), (), s32[]{:S(2)}) async-start(), calls=%async_computation.6 | async-start | bytes 884736 | tf_op jit(solution)/shard_map/reduce_scatter | solution.py:80
  381.8 219.6 %reduce-scatter.15.cloned.1.call-start = ((), (), s32[]{:S(2)}) async-start(), calls=%async_computation.8 | async-start | bytes 884736 | tf_op jit(solution)/shard_map/reduce_scatter | solution.py:124
  382.4 291.0 %reduce-scatter.17.cloned.1.call-start = ((), (), s32[]{:S(2)}) async-start(), calls=%async_computation.9 | async-start | bytes 1671168 | tf_op jit(solution)/shard_map/reduce_scatter | solution.py:128
Sparse Core Ops, SparseCore 0:
  347.3 33.7 reduce-scatter.18
  385.5 67.6 reduce-scatter.20
  457.1 65.0 reduce-scatter.12
  524.6 37.3 reduce-scatter.10
  564.2 37.0 reduce-scatter.14
  605.6 67.6 reduce-scatter.16
where the time goes:
time: 685 us; the launch traced here: 682 us
  waiting for transfers between devices  287 us (42%)
  blocking collectives  216 us (32%)
  matrix products  108 us (16%)
  local copies, waits for them, and re-layouts  32 us (5%)
  loops' own time  20.3 us (3%)
  between operations  14.3 us (2%)
    reduce_scatter x1, waiting for transfers between devices, local(): lax.psum_scatter(back_cols, 'row', scatter_dimension=0, tiled=True)  72 us
    unnamed x8, waiting for transfers between devices  69.9 us
    reduce_scatter x1, waiting for transfers between devices, local(): lax.psum_scatter(fwd_cols.astype(jnp.bfloat16), 'row', scatter_dimension=...  67.3 us
    dot_general x30, matrix products, score_tile(): lax.dot_general(src_rows, dst_block, (((0,), (0,)), ((), ())), preferred_...  45 us
    reduce_scatter x1, waiting for transfers between devices, local(): lax.psum_scatter(fwd_rows, 'col', scatter_dimension=0, tiled=True)  39.8 us
    reduce_scatter x1, waiting for transfers between devices, local(): lax.psum_scatter(back_rows, 'col', scatter_dimension=0, tiled=True)  37.8 us
    all_gather x1, blocking collectives, local(): lax.all_gather(features, 'row', axis=0, tiled=True)  29.4 us
    all_gather x1, blocking collectives, local(): lax.all_gather(features, 'col', axis=0, tiled=True)  29.2 us
  transfers between devices with their start and end apart: 6, of which 5 were waited for; matrix products, arithmetic and copies ran while one was open for 5% of the time, Pallas kernels for 0%

commit v1 on v0

v1 whole, which is shorter than its diff:
```python
import functools

import jax
import jax.numpy as jnp
import numpy as np
from jax import lax
from jax.experimental import pallas as pl
from jax.experimental.pallas import tpu as pltpu
from jax.sharding import PartitionSpec as P

F32 = jnp.float32
BF16 = jnp.bfloat16
LANES = 128
VMEM_MIB = 24
SMEM = pl.BlockSpec(memory_space=pltpu.SMEM)
MOVES = (0, 1, 2, -1)


def pick(total, unit, most):
    size = total
    while size > most or total % size or size % unit:
        size -= unit
    return size


def whole(shape):
    return pl.BlockSpec(shape, lambda *i: (0,) * len(shape))


def shapes(*pairs):
    return [jax.ShapeDtypeStruct(shape, kind) for shape, kind in pairs]


def params(mib=VMEM_MIB):
    return pltpu.CompilerParams(vmem_limit_bytes=mib * 1024 * 1024)


def places(row_size, col_size):
    depth, width = row_size // 4, col_size // 2
    table = np.zeros((row_size * col_size, 16), np.int32)
    for index in range(row_size * col_size):
        row, col = divmod(index, col_size)
        slots = [(col // 2 + move) % width for move in MOVES] + [(row // 4 + move) % depth for move in MOVES]
        table[index, :12] = slots + [col % 2, row // 2 % 2, col, col // 2]
    return table


def assemble(own, chunk_refs, place_ref, base, parity, pair_ref, turned_ref, nodes_ref):
    extra = chunk_refs[0].shape[1] - own
    even = parity == 0
    blank = jnp.zeros((extra, 2 * own - chunk_refs[0].shape[2]), F32)
    for slot, chunk_ref in enumerate(chunk_refs):
        start = place_ref[base + slot] * 2 * own
        for flip in range(2):
            rows = pl.ds(pl.multiple_of(start + (parity ^ flip) * own, 64), own)
            pair_ref[rows, :] = chunk_ref[flip, :own, :]
        first = chunk_ref[0, own:, :].astype(F32)
        second = chunk_ref[1, own:, :].astype(F32)
        left = jnp.concatenate([jnp.where(even, first, second), blank], axis=1)
        right = jnp.concatenate([blank, jnp.where(even, second, first)], axis=1)
        both = left + pltpu.roll(right, own - blank.shape[1], 1)
        turned_ref[:extra, pl.ds(pl.multiple_of(start, LANES), 2 * own)] = both.astype(BF16)
    turned_ref[extra:, :] = jnp.zeros((LANES - extra, turned_ref.shape[1]), BF16)
    nodes_ref[...] = jnp.transpose(turned_ref[...])


def stats_kernel(own, feat, place_ref, *rest):
    parts = len(MOVES)
    a_refs, b0_refs, b1_refs = rest[0 : 2 * parts : 2], rest[1 : 2 * parts : 2], rest[2 * parts : 3 * parts]
    scaled_ref, stats_ref, a_pair, a_pair_t, a_src, a_src_t, b_pair, b_dst, b_dst_t, scores, peaks = rest[3 * parts :]
    step = pl.program_id(0)
    last = pl.num_programs(0) - 1
    count, cols = scores.shape
    span = pick(cols, LANES, 1024)
    repeat = span // LANES

    def tiles(array):
        return [array[:, lane : lane + LANES] for lane in range(0, span, LANES)]

    def work(ahead, behind):
        block = step - 1 if behind else step
        here = pl.ds(pl.multiple_of(block * count, count), count)
        there = pl.ds(pl.multiple_of(step * count, count), count)
        total = jnp.zeros((count, LANES), F32)
        peak = jnp.zeros((count, LANES), F32)
        sums = jnp.zeros((count, 2 * feat), F32)
        for start in range(0, cols, span):
            part = slice(start, start + span)
            if behind:
                before = peaks[...]
                half = jnp.exp(scores[:, part] - jnp.concatenate([before] * repeat, axis=1)).astype(BF16)
                total = total + sum(tiles(half.astype(F32)))
                sums = sums + jnp.dot(half, b_pair[part, :], preferred_element_type=F32)
            if ahead:
                fresh = jnp.maximum(jnp.dot(a_src[there, :], b_dst_t[:, part], preferred_element_type=F32), 0.0)
                scores[:, part] = fresh
                peak = functools.reduce(jnp.maximum, tiles(fresh), peak)
        if behind:
            total = jnp.sum(total, axis=1, keepdims=True)
            sums = sums / total
            scaled_ref[...] = sums.astype(BF16)
            mates = a_pair[here, :].astype(F32)
            inner = jnp.sum(sums[:, :feat] * mates[:, feat:] + sums[:, feat:] * mates[:, :feat], axis=1, keepdims=True)
            lane = lax.broadcasted_iota(jnp.int32, (count, LANES), 1)
            table = jnp.where(lane == 0, peaks[...], jnp.where(lane == 1, total, inner))
            stats_ref[...] = jnp.broadcast_to(jnp.transpose(table)[:4][None], stats_ref.shape)
        if ahead:
            peaks[...] = jnp.broadcast_to(jnp.max(peak, axis=1, keepdims=True), peaks.shape)

    @pl.when(step == 0)
    def _():
        assemble(own, a_refs, place_ref, 0, place_ref[8], a_pair, a_src_t, a_src)
        half = b_pair.shape[0] // 2
        for index, b_refs in enumerate((b0_refs, b1_refs)):
            part = pl.ds(index * half, half)
            outs = (b_pair.at[part, :], b_dst_t.at[:, part], b_dst.at[part, :])
            assemble(own, b_refs, place_ref, 4, place_ref[9], *outs)
        a_pair_t[:feat] = jnp.transpose(a_pair[:, feat:])
        a_pair_t[feat:] = jnp.transpose(a_pair[:, :feat])
        work(True, False)

    @pl.when((step > 0) & (step < last))
    def _():
        work(True, True)

    @pl.when(step == last)
    def _():
        work(False, True)


def row_stats(place, a_parts, b0_parts, b1_parts, own, feat):
    mates = sum(part.shape[0] for part in a_parts)
    rows = mates * own
    cols = 2 * own * sum(part.shape[0] for part in b0_parts)
    pair = 2 * feat
    step = pick(rows, LANES, 256)
    kept = [((rows, pair), BF16), ((pair, rows), BF16), ((rows, LANES), BF16), ((LANES, rows), BF16)]
    kept += [((cols, pair), BF16), ((cols, LANES), BF16), ((LANES, cols), BF16)]
    parts = [part for both in zip(a_parts, b0_parts) for part in both] + b1_parts
    scaled, stats, *kept = pl.pallas_call(
        functools.partial(stats_kernel, own, feat),
        grid=(rows // step + 1,),
        in_specs=[SMEM] + [whole(x.shape) for x in parts],
        out_specs=[
            pl.BlockSpec((step, pair), lambda i: (jnp.maximum(i - 1, 0), 0)),
            pl.BlockSpec((mates, 4, step), lambda i: (0, 0, jnp.maximum(i - 1, 0))),
        ]
        + [whole(shape) for shape, kind in kept],
        out_shape=shapes(((rows, pair), BF16), ((mates, 4, rows), F32), *kept),
        scratch_shapes=[pltpu.VMEM((step, cols), F32), pltpu.VMEM((step, LANES), F32)],
        compiler_params=params(),
        cost_estimate=pl.CostEstimate(flops=2 * rows * cols * 512, bytes_accessed=8 << 20, transcendentals=rows * cols),
        name="row_stats",
    )(place, *parts)
    return scaled, stats, kept


def tile_kernel(
    own, feat, last, place_ref, a_pair, a_pair_t, a_src, a_src_t, b_pair, b_dst, b_dst_t, stats_ref, *rest
):
    pair = 2 * feat
    step = pl.program_id(0)
    if last:
        start_ref, mine_ref, cols_ref, source_ref, *piece_refs, twin_ref, table, slots = rest
    else:
        scaled_ref, cols_ref, source_ref, mine_ref, given_ref, table, weights_ref = rest
    extra = cols_ref.shape[1] - own

    @pl.when(step == 0)
    def _():
        source_ref[...] = start_ref[...] if last else jnp.zeros_like(source_ref)
        stats = stats_ref[...]
        peaks = stats[:, 0:1]
        peak = jnp.max(peaks, axis=0)
        weights = jnp.exp(peaks - peak[None]) * stats[:, 1:2]
        total = jnp.sum(weights, axis=0)
        table[0:1, :] = peak + jnp.log(total)
        table[1:2, :] = jnp.sum(weights * stats[:, 2:3], axis=0) / total
        if not last:
            at = place_ref[10]
            weight = jnp.exp(stats_ref[at, 0:1] - peak) * stats_ref[at, 1:2] / total
            weights_ref[...] = jnp.transpose(jnp.broadcast_to(weight, (LANES, weight.shape[1])))
            for slot in range(mine_ref.shape[0]):
                for flip, out_ref in enumerate((mine_ref, given_ref)):
                    chunk = 2 * (place_ref[11] ^ slot) + (place_ref[8] ^ flip)
                    rows = pl.ds(pl.multiple_of(chunk * own, 64), own)
                    out_ref[slot] = (weights_ref[rows, 0:1] * scaled_ref[rows, :].astype(F32)).astype(BF16)

    scores = jnp.dot(b_dst[...], a_src_t[...], preferred_element_type=F32)
    outer = jnp.dot(b_pair[...], a_pair_t[...], preferred_element_type=F32)
    soft = jnp.exp(jnp.maximum(scores, 0.0) - table[0:1, :])
    grad = jnp.where(scores > 0.0, soft * (outer - table[1:2, :]), 0.0)
    soft_half = soft.astype(BF16)
    grad_half = grad.astype(BF16)
    col_sums = jnp.dot(soft_half, a_pair[...], preferred_element_type=F32).astype(BF16)
    target_sums = jnp.dot(grad_half, a_src[...], preferred_element_type=F32)
    for slot in range(cols_ref.shape[0]):
        rows = slice(slot * own, (slot + 1) * own)
        cols_ref[slot, :own, :] = col_sums[rows]
        wide = jnp.concatenate([target_sums[rows], jnp.zeros((pair - own, LANES), F32)], axis=0)
        cols_ref[slot, own:, :] = jnp.transpose(wide)[:extra].astype(BF16)
    source_ref[...] += jnp.dot(b_dst_t[:extra], grad_half, preferred_element_type=F32)

    if last:

        @pl.when(step == pl.num_programs(0) - 1)
        def _():
            fill = jnp.zeros((extra, pair - own), F32)
            for chunk in range(slots.shape[0]):
                part = source_ref[:, chunk * own : (chunk + 1) * own]
                slots[place_ref[10] ^ chunk] = jnp.concatenate([part, fill], axis=1)
            for slot, piece_ref in enumerate(piece_refs):
                piece_ref[:own, :] = mine_ref[slot]
                piece_ref[own:, :] = slots[2 * slot].astype(BF16)
                twin_ref[slot] = slots[2 * slot + 1].astype(BF16)


def tile_sums(place, kept, half, stats, late, own, feat, extra, last, name):
    rows, pair = kept[0].shape
    cols = kept[4].shape[0] // 2
    mates = stats.shape[0]
    step = pick(cols, 2 * own, 2 * own)
    base = half * (cols // step)
    scratch = [pltpu.VMEM((8, rows), F32)]
    if last:
        kinds = [((own + extra, pair), BF16)] * (mates // 2) + [((mates // 2, extra, pair), BF16)]
        scratch += [pltpu.VMEM((mates, extra, pair), F32)]
    else:
        kinds = [((mates // 2, own, pair), BF16)] * 2
        scratch += [pltpu.VMEM((rows, LANES), F32)]
    return pl.pallas_call(
        functools.partial(tile_kernel, own, feat, last),
        grid=(cols // step,),
        in_specs=[
            SMEM,
            *[whole(x.shape) for x in kept[:4]],
            pl.BlockSpec((step, pair), lambda i: (i + base, 0)),
            pl.BlockSpec((step, LANES), lambda i: (i + base, 0)),
            pl.BlockSpec((LANES, step), lambda i: (0, i + base)),
            *[whole(x.shape) for x in (stats, *late)],
        ],
        out_specs=[pl.BlockSpec((step // own, own + extra, pair), lambda i: (i, 0, 0)), whole((extra, rows))]
        + [whole(shape) for shape, kind in kinds],
        out_shape=shapes(((cols // own, own + extra, pair), BF16), ((extra, rows), F32), *kinds),
        scratch_shapes=scratch,
        compiler_params=params(),
        cost_estimate=pl.CostEstimate(flops=2 * rows * cols * 1280, bytes_accessed=8 << 20, transcendentals=rows * cols),
        name=name,
    )(place, *kept, stats, *late)


def join_cols_kernel(own_ref, other_ref, out_ref):
    out_ref[...] = (own_ref[...].astype(F32) + other_ref[...].astype(F32)).astype(BF16)


def join_rows_kernel(given_ref, twin_ref, *rest):
    count, own = given_ref.shape[:2]
    for slot, (piece_ref, out_ref) in enumerate(zip(rest[:count], rest[count:])):
        out_ref[:own, :] = (piece_ref[:own, :].astype(F32) + given_ref[slot].astype(F32)).astype(BF16)
        out_ref[own:, :] = (piece_ref[own:, :].astype(F32) + twin_ref[slot].astype(F32)).astype(BF16)


def join(kernel, name, outs, *arrays):
    return pl.pallas_call(
        kernel,
        out_shape=[jax.ShapeDtypeStruct(out.shape, out.dtype) for out in outs],
        compiler_params=params(8),
        name=name,
    )(*arrays)


def finish_kernel(own, feat, emb_count, cols_ref, *rest):
    piece_refs, (hop_ref, grad_ref, source_ref, target_ref) = rest[:-4], rest[-4:]
    total = jnp.zeros((own, 2 * feat), F32)
    extra = jnp.zeros((cols_ref.shape[1] - own, 2 * feat), F32)
    source = extra
    for piece_ref in piece_refs:
        total = total + piece_ref[:own, :].astype(F32)
        source = source + piece_ref[own:, :].astype(F32)
    for slot in range(cols_ref.shape[0]):
        total = total + cols_ref[slot, :own, :].astype(F32)
        extra = extra + cols_ref[slot, own:, :].astype(F32)
    hop_ref[...] = total[:, :feat].astype(BF16)
    grad_ref[...] = total[:, feat:].astype(BF16)
    source_ref[...] = source[:emb_count, :own]
    target_ref[...] = extra[:emb_count, :own]


def finish(cols, pieces, own, feat, emb_count):
    return pl.pallas_call(
        functools.partial(finish_kernel, own, feat, emb_count),
        out_shape=shapes(
            ((own, feat), BF16), ((own, feat), BF16), ((emb_count, own), F32), ((emb_count, own), F32)
        ),
        compiler_params=params(8),
        name="finish",
    )(cols, *pieces)


def local(sizes, source_embed, target_embed, features, cotangent):
    row_size, col_size = sizes
    emb_count, own = source_embed.shape
    feat = features.shape[1]
    pair = 2 * feat
    extra = -(-emb_count // 16) * 16
    depth, width = row_size // 4, col_size // 2
    both = ("row", "col")

    def device(z, y, core, x, skew):
        return (((z % depth) * 2 + y) * 2 + core) * col_size + (x % width) * 2 + (skew ^ y)

    groups = [
        [device(z, y, core, x, skew) for z in range(depth) for y in range(2)]
        for core in range(2) for x in range(width) for skew in range(2)
    ]

    def mate(array, bits):
        return lax.ppermute(array, "col", [(c, c ^ bits) for c in range(col_size)])

    def swap(array):
        return lax.ppermute(array, "row", [(r, r ^ 1) for r in range(row_size)])

    def along_x(array, move, flip):
        pairs = [(x * 2 + y, ((x + move) % width) * 2 + (y ^ flip)) for x in range(width) for y in range(2)]
        return lax.ppermute(array, "col", pairs)

    def along_z(array, move, flip):
        pairs = [
            (device(z, y, core, x, skew), device(z + move, y ^ flip, core, x, skew))
            for z in range(depth) for y in range(2) for core in range(2) for x in range(width) for skew in range(2)
        ]
        return lax.ppermute(array, both, pairs)

    def pack(embed):
        left = jnp.pad(features, ((0, extra), (0, feat)))
        right = jnp.pad(cotangent, ((0, extra), (feat, 0)))
        return left + right + jnp.pad(embed, ((own, extra - emb_count), (0, pair - own)))

    index = lax.axis_index(both)
    place = lax.dynamic_index_in_dim(jnp.asarray(places(row_size, col_size)), index, 0, keepdims=False)
    chunks, alongs = (pack(target_embed), pack(source_embed)), (along_z, along_x)
    near = [jnp.stack([chunk, along(chunk, 0, 1)]) for chunk, along in zip(chunks, alongs)]
    near, place = lax.optimization_barrier((near, place))
    moved = [[along(array, -move, 0) for array, along in zip(near, alongs)] for move in MOVES[1:]]
    b_parts, a_parts = [[array, *[pair[index] for pair in moved]] for index, array in enumerate(near)]
    others = [swap(part) for part in b_parts]
    scaled, stats, kept = row_stats(place, a_parts, b_parts, others, own, feat)
    stats = lax.all_to_all(stats, "col", 0, 0)

    sizes = (own, feat, extra)
    other_cols, start, mine, given = tile_sums(place, kept, 1, stats, (scaled,), *sizes, False, "other_tile")
    other_cols = swap(other_cols)
    given = mate(given, 1)
    own_cols, unused, *pieces, twin = tile_sums(place, kept, 0, stats, (start, mine), *sizes, True, "own_tile")
    twin = mate(twin, 1)
    (cols,) = join(join_cols_kernel, "join_cols", [own_cols], own_cols, other_cols)
    cols = lax.all_to_all(cols, both, 0, 0, axis_index_groups=groups)
    pieces = join(join_rows_kernel, "join_rows", pieces, given, twin, *pieces)
    pieces = [mate(piece, 2 * slot) if slot else piece for slot, piece in enumerate(pieces)]
    return tuple(finish(cols, pieces, own, feat, emb_count))


def solution(mesh):
    nodes = P(("row", "col"), None)
    embeds = P(None, ("row", "col"))
    sizes = (mesh.shape["row"], mesh.shape["col"])
    return jax.shard_map(
        functools.partial(local, sizes),
        mesh=mesh,
        in_specs=(embeds, embeds, nodes, nodes),
        out_specs=(nodes, nodes, embeds, embeds),
        check_vma=False,
    )
```

time: 685 us -> 97.2 us (0.14)
  waiting for transfers between devices: 287 us -> 27.3 us
  blocking collectives: 216 us -> 9.42 us
  matrix products: 108 us -> 0 us
  local copies, waits for them, and re-layouts: 32 us -> 0.69 us
  Pallas kernels: 0 us -> 29.2 us
  starting transfers between devices: 0.24 us -> 28.6 us
  loops' own time: 20.3 us -> 0 us
  between operations: 14.3 us -> 0.69 us
    reduce_scatter x4 -> x0, waiting for transfers between devices: 217 us -> none  [the longest x1 72 us: local(): lax.psum_scatter(back_cols, 'row', scatter_dimension=0, tiled=True)]
    all_gather x6 -> x0, blocking collectives: 162 us -> none  [the longest x1 29.4 us: local(): lax.all_gather(features, 'row', axis=0, tiled=True)]
    dot_general x78 -> x0, matrix products: 108 us -> none  [the longest x30 45 us: score_tile(): lax.dot_general(src_rows, dst_block, (((0,), (0,)), ((), ())), preferred_...]
    unnamed x8 -> x0, waiting for transfers between devices: 69.9 us -> none
    psum x2 -> x0, blocking collectives: 34.4 us -> none  [the longest x1 18.2 us: local(): row_delta = lax.psum(row_delta, 'col')]
    pallas_call x0 -> x6, Pallas kernels: none -> 29.2 us  [the longest x2 17.4 us: tile_sums(): pl.pallas_call(functools.partial(tile_kernel, own, feat, last), grid=(col...]
    ppermute x0 -> x18, waiting for transfers between devices: none -> 27.3 us  [the longest x5 16.2 us: mate(): return lax.ppermute(array, 'col', [(c, c ^ bits) for c in range(col_size)])]
    ppermute x0 -> x18, starting transfers between devices: none -> 23.6 us  [the longest x4 8.69 us: along_z(): return lax.ppermute(array, both, pairs)]
  transfers between devices with their start and end apart: 6 -> 19, of which waited for: 5 -> 11; matrix products, arithmetic and copies ran while one was open for 5% -> 1% of each run, Pallas kernels for 0% -> 9%
where the time goes in v1:
time: 97.2 us; the launch traced here: 96.9 us
  Pallas kernels  29.2 us (30%)
  starting transfers between devices  28.6 us (29%)
  waiting for transfers between devices  27.3 us (28%)
  blocking collectives  9.42 us (10%)
    pallas_call x2, Pallas kernels, tile_sums(): pl.pallas_call(functools.partial(tile_kernel, own, feat, last), grid=(col...  17.4 us
    ppermute x5, waiting for transfers between devices, mate(): return lax.ppermute(array, 'col', [(c, c ^ bits) for c in range(col_size)])  16.2 us
    pallas_call x1, Pallas kernels, row_stats(): pl.pallas_call(functools.partial(stats_kernel, own, feat), grid=(rows //...  9.67 us
    all_to_all x1, blocking collectives, local(): stats = lax.all_to_all(stats, 'col', 0, 0)  9.42 us
    ppermute x4, starting transfers between devices, along_z(): return lax.ppermute(array, both, pairs)  8.69 us
    ppermute x4, waiting for transfers between devices, along_z(): return lax.ppermute(array, both, pairs)  7.68 us
    ppermute x4, starting transfers between devices, along_x(): return lax.ppermute(array, 'col', pairs)  7.46 us
    ppermute x5, starting transfers between devices, mate(): return lax.ppermute(array, 'col', [(c, c ^ bits) for c in range(col_size)])  6.8 us
  transfers between devices with their start and end apart: 19, of which 11 were waited for; matrix products, arithmetic and copies ran while one was open for 1% of the time, Pallas kernels for 9%

profile of v1, /device:TPU:0, one launch (start us, length us, event | category | flops | bytes accessed | tf_op | source)
XLA Modules:
  0.0 96.9 jit_solution(12215231219443824525)
XLA Ops:
  0.6 0.9 fusion.1
  1.5 1.7 %collective-permute-start.1 = (bf16[240,256]{1,0:T(8,128)(2,1)S(1)}, bf16[240,256]{1,0:T(8,128)(2,1)S(1)}, u32[]{:S(2)}, u32[]{:S(2)}) collective-permute-start(bf16[240,256]{1,0:T(8,128)(2,1)S(1)} %get-tuple-element.57), channel_id=1, source_target_pairs={{0,1},{1,0},{2,3},{3,2},{4,5},{5,4},{6,7},{7,6},{8,9},{9,8},{10,11... | collective-permute-start | bytes 368648 | tf_op jit(solution)/shard_map/ppermute | solution.py:325
  3.3 2.2 %collective-permute-start = (bf16[240,256]{1,0:T(8,128)(2,1)S(1)}, bf16[240,256]{1,0:T(8,128)(2,1)S(1)}, u32[]{:S(2)}, u32[]{:S(2)}) collective-permute-start(bf16[240,256]{1,0:T(8,128)(2,1)S(1)} %get-tuple-element.60), channel_id=1, source_target_pairs={{0,17},{1,16},{2,19},{3,18},{4,21},{5,20},{6,23},{7,22},{8,25},{9,... | collective-permute-start | bytes 368648 | tf_op jit(solution)/shard_map/ppermute | solution.py:332
  5.4 0.7 dynamic-slice_bitcast_fusion.place_ref
  6.1 0.4 collective-permute-done.1
  6.6 2.7 %collective-permute-done = bf16[240,256]{1,0:T(8,128)(2,1)S(1)} collective-permute-done((bf16[240,256]{1,0:T(8,128)(2,1)S(1)}, bf16[240,256]{1,0:T(8,128)(2,1)S(1)}, u32[]{:S(2)}, u32[]{:S(2)}) %collective-permute-start) | collective-permute-done | bytes 122912 | tf_op jit(solution)/shard_map/ppermute | solution.py:332
  9.4 1.6 %collective-permute-start.6 = (bf16[2,240,256]{2,1,0:T(8,128)(2,1)S(1)}, bf16[2,240,256]{2,1,0:T(8,128)(2,1)S(1)}, u32[]{:S(2)}, u32[]{:S(2)}) collective-permute-start(bf16[2,240,256]{2,1,0:T(8,128)(2,1)S(1)} %pad_maximum_fusion.1.rest_0_), channel_id=1, source_target_pairs={{0,2},{1,3},{2,4},{3,5},{4,6},{5,7},{6,0},{7,1},{8,10},{9,11},{10,... | collective-permute-start | bytes 737288 | tf_op jit(solution)/shard_map/ppermute | solution.py:325
  10.9 2.7 %collective-permute-start.4 = (bf16[2,240,256]{2,1,0:T(8,128)(2,1)S(1)}, bf16[2,240,256]{2,1,0:T(8,128)(2,1)S(1)}, u32[]{:S(2)}, u32[]{:S(2)}) collective-permute-start(bf16[2,240,256]{2,1,0:T(8,128)(2,1)S(1)} %pad_maximum_fusion.1.rest_0_), channel_id=1, source_target_pairs={{0,4},{1,5},{2,6},{3,7},{4,0},{5,1},{6,2},{7,3},{8,12},{9,13},{10,... | collective-permute-start | bytes 737288 | tf_op jit(solution)/shard_map/ppermute | solution.py:325
  13.7 1.9 %collective-permute-start.7 = (bf16[2,240,256]{2,1,0:T(8,128)(2,1)S(1)}, bf16[2,240,256]{2,1,0:T(8,128)(2,1)S(1)}, u32[]{:S(2)}, u32[]{:S(2)}) collective-permute-start(bf16[2,240,256]{2,1,0:T(8,128)(2,1)S(1)} %pad_maximum_fusion.rest_1_), channel_id=1, source_target_pairs={{0,32},{1,33},{2,34},{3,35},{4,36},{5,37},{6,38},{7,39},{8,40},{9,... | collective-permute-start | bytes 737288 | tf_op jit(solution)/shard_map/ppermute | solution.py:332
  15.6 3.6 %collective-permute-start.5 = (bf16[2,240,256]{2,1,0:T(8,128)(2,1)S(1)}, bf16[2,240,256]{2,1,0:T(8,128)(2,1)S(1)}, u32[]{:S(2)}, u32[]{:S(2)}) collective-permute-start(bf16[2,240,256]{2,1,0:T(8,128)(2,1)S(1)} %pad_maximum_fusion.rest_1_), channel_id=1, source_target_pairs={{0,64},{1,65},{2,66},{3,67},{4,68},{5,69},{6,70},{7,71},{8,72},{9,... | collective-permute-start | bytes 737288 | tf_op jit(solution)/shard_map/ppermute | solution.py:332
  19.2 1.0 %collective-permute-start.3 = (bf16[2,240,256]{2,1,0:T(8,128)(2,1)S(1)}, bf16[2,240,256]{2,1,0:T(8,128)(2,1)S(1)}, u32[]{:S(2)}, u32[]{:S(2)}) collective-permute-start(bf16[2,240,256]{2,1,0:T(8,128)(2,1)S(1)} %pad_maximum_fusion.rest_1_), channel_id=1, source_target_pairs={{0,96},{1,97},{2,98},{3,99},{4,100},{5,101},{6,102},{7,103},{8,104... | collective-permute-start | bytes 737288 | tf_op jit(solution)/shard_map/ppermute | solution.py:332
  20.2 0.0 collective-permute-done.6.rest_6_
  20.2 1.4 %collective-permute-start.2 = (bf16[2,240,256]{2,1,0:T(8,128)(2,1)S(1)}, bf16[2,240,256]{2,1,0:T(8,128)(2,1)S(1)}, u32[]{:S(2)}, u32[]{:S(2)}) collective-permute-start(bf16[2,240,256]{2,1,0:T(8,128)(2,1)S(1)} %pad_maximum_fusion.1.rest_0_), channel_id=1, source_target_pairs={{0,6},{1,7},{2,0},{3,1},{4,2},{5,3},{6,4},{7,5},{8,14},{9,15},{10,... | collective-permute-start | bytes 737288 | tf_op jit(solution)/shard_map/ppermute | solution.py:325
  21.6 1.6 %collective-permute-done.4.rest_4_ = bf16[2,240,256]{2,1,0:T(8,128)(2,1)S(1)} collective-permute-done((bf16[2,240,256]{2,1,0:T(8,128)(2,1)S(1)}, bf16[2,240,256]{2,1,0:T(8,128)(2,1)S(1)}, u32[]{:S(2)}, u32[]{:S(2)}) %collective-permute-start.4) | collective-permute-done | bytes 245792 | tf_op jit(solution)/shard_map/ppermute | solution.py:325
  23.2 0.0 collective-permute-start.8
  23.2 0.9 collective-permute-done.7.rest_7_
  24.1 0.0 collective-permute-start.11
  24.1 4.0 %collective-permute-done.5.rest_5_ = bf16[2,240,256]{2,1,0:T(8,128)(2,1)S(1)} collective-permute-done((bf16[2,240,256]{2,1,0:T(8,128)(2,1)S(1)}, bf16[2,240,256]{2,1,0:T(8,128)(2,1)S(1)}, u32[]{:S(2)}, u32[]{:S(2)}) %collective-permute-start.5) | collective-permute-done | bytes 245792 | tf_op jit(solution)/shard_map/ppermute | solution.py:332
  28.1 0.0 collective-permute-start.10
  28.1 0.0 collective-permute-done.3.rest_3_
  28.1 0.5 collective-permute-start.9
  28.6 0.0 collective-permute-done.2.rest_2_
  28.6 0.0 collective-permute-done.8.rest_8_
  28.6 0.0 collective-permute-done.11.rest_11_
  28.6 1.0 %collective-permute-done.10.rest_10_ = bf16[2,240,256]{2,1,0:T(8,128)(2,1)S(1)} collective-permute-done((bf16[2,240,256]{2,1,0:T(8,128)(2,1)S(1)}, bf16[2,240,256]{2,1,0:T(8,128)(2,1)S(1)}, u32[]{:S(2)}, u32[]{:S(2)}) %collective-permute-start.10) | collective-permute-done | bytes 245792 | tf_op jit(solution)/shard_map/ppermute | solution.py:321
  29.6 0.4 collective-permute-done.9.rest_9_
  30.0 9.7 %row_stats.1 = (bf16[1536,256]{1,0:T(8,128)(2,1)S(1)}, f32[8,4,1536]{2,1,0:T(4,128)S(1)}, bf16[1536,256]{1,0:T(8,128)(2,1)S(1)}, bf16[256,1536]{1,0:T(8,128)(2,1...) custom-call(s32[16]{0:T(128)S(1)} %dynamic-slice_bitcast_fusion.plac, ...), custom_call_target="tpu_custom_call" | custom-call | flops 4831838208 | bytes 8388608 | tf_op jit(solution)/shard_map/row_stats/pallas_call | solution.py:140
  39.6 9.4 %all_to_all.10.stats_ref = f32[8,4,1536]{2,1,0:T(4,128)S(1)} all-to-all(f32[8,4,1536]{2,1,0:T(4,128)S(1)} %get-tuple-element.40), channel_id=1, replica_groups=mesh['row'=16,'col'=8] {'col'}, dimensions={0} | all-to-all | bytes 393216 | tf_op jit(solution)/shard_map/all_to_all | solution.py:348
  49.1 8.5 %other_tile.1 = (bf16[8,240,256]{2,1,0:T(8,128)(2,1)S(1)}, f32[48,1536]{1,0:T(8,128)S(1)}, bf16[4,192,256]{2,1,0:T(8,128)(2,1)S(1)}, bf16[4,192,256]{2,1,0:T(8,128)(2,1)S(1)}) custom-call(s32[16]{0:T(128)S(1)} %dynamic-slice_bitcast_fusion.place_ref, bf16[1536,256]{1,0:T(8,128)(2,1)S(1)} %get-tuple-element.33.a_pair, ...), custom_call_target="tpu_custom_call" | custom-call | flops 6039797760 | bytes 8388608 | tf_op jit(solution)/shard_map/other_tile/pallas_call | solution.py:231
  57.6 0.1 collective-permute-start.12
  57.7 8.9 %own_tile.1 = (bf16[8,240,256]{2,1,0:T(8,128)(2,1)S(1)}, f32[48,1536]{1,0:T(8,128)}, bf16[240,256]{1,0:T(8,128)(2,1)S(1)}, bf16[240,256]{1,0:T(8,128)(2,1)S(1)},...) custom-call(s32[16]{0:T(128)S(1)} %dynamic-slice_bitcast_fusion.place_ref, ...), custom_call_target="tpu_custom_call" | custom-call | flops 6039797760 | bytes 8388608 | tf_op jit(solution)/shard_map/own_tile/pallas_call | solution.py:231
  66.6 0.0 collective-permute-done.12.other_ref
  66.6 1.2 %join_cols.1 = bf16[8,240,256]{2,1,0:T(8,128)(2,1)} custom-call(bf16[8,240,256]{2,1,0:T(8,128)(2,1)S(1)} %get-tuple-element.44.own_ref, bf16[8,240,256]{2,1,0:T(8,128)(2,1)S(1)} %collective-permute-done.12.other_ref), custom_call_target="tpu_custom_call" | custom-call | tf_op jit(solution)/shard_map/join_cols/pallas_call | solution.py:264
  67.8 5.1 %all-to-all-start.1 = ((bf16[8,240,256]{2,1,0:T(8,128)(2,1)}), bf16[8,240,256]{2,1,0:T(8,128)(2,1)S(1)}, u32[]{:S(2)}, u32[]{:S(2)}) async-start(bf16[8,240,256]{2,1,0:T(8,128)(2,1)} %join_cols.1), calls=%async_computation.1 | async-start | bytes 1966080 | tf_op jit(solution)/shard_map/all_to_all | solution.py:357
  72.9 0.6 collective-permute-start.13
  73.4 1.5 %collective-permute-start.14 = (bf16[4,48,256]{2,1,0:T(8,128)(2,1)S(1)}, bf16[4,48,256]{2,1,0:T(8,128)(2,1)S(1)}, u32[]{:S(2)}, u32[]{:S(2)}) collective-permute-start(bf16[4,48,256]{2,1,0:T(8,128)(2,1)S(1)} %get-tuple-element.47), channel_id=1, source_target_pairs={{0,1},{1,0},{2,3},{3,2},{4,5},{5,4},{6,7},{7,6},{8,9},{9,8},{10,11... | collective-permute-start | bytes 294920 | tf_op jit(solution)/shard_map/ppermute | solution.py:318
  74.9 11.3 %collective-permute-done.14.twin_ref = bf16[4,48,256]{2,1,0:T(8,128)(2,1)S(1)} collective-permute-done((bf16[4,48,256]{2,1,0:T(8,128)(2,1)S(1)}, bf16[4,48,256]{2,1,0:T(8,128)(2,1)S(1)}, u32[]{:S(2)}, u32[]{:S(2)}) %collective-permute-start.14) | collective-permute-done | bytes 98336 | tf_op jit(solution)/shard_map/ppermute | solution.py:318
  86.2 0.0 collective-permute-done.13.given_ref
  86.2 0.1 join_rows.1
  86.3 0.6 collective-permute-start.15
  87.0 2.1 %collective-permute-start.16 = (bf16[240,256]{1,0:T(8,128)(2,1)S(1)}, bf16[240,256]{1,0:T(8,128)(2,1)S(1)}, u32[]{:S(2)}, u32[]{:S(2)}) collective-permute-start(bf16[240,256]{1,0:T(8,128)(2,1)S(1)} %get-tuple-element.54), channel_id=1, source_target_pairs={{0,4},{1,5},{2,6},{3,7},{4,0},{5,1},{6,2},{7,3},{8,12},{9,13},{10,... | collective-permute-start | bytes 368648 | tf_op jit(solution)/shard_map/ppermute | solution.py:318
  89.0 2.1 %collective-permute-start.17 = (bf16[240,256]{1,0:T(8,128)(2,1)S(1)}, bf16[240,256]{1,0:T(8,128)(2,1)S(1)}, u32[]{:S(2)}, u32[]{:S(2)}) collective-permute-start(bf16[240,256]{1,0:T(8,128)(2,1)S(1)} %get-tuple-element.55), channel_id=1, source_target_pairs={{0,6},{1,7},{2,4},{3,5},{4,2},{5,3},{6,0},{7,1},{8,14},{9,15},{10,... | collective-permute-start | bytes 368648 | tf_op jit(solution)/shard_map/ppermute | solution.py:318
  91.1 1.2 %collective-permute-done.15.rest_1_ = bf16[240,256]{1,0:T(8,128)(2,1)S(1)} collective-permute-done((bf16[240,256]{1,0:T(8,128)(2,1)S(1)}, bf16[240,256]{1,0:T(8,128)(2,1)S(1)}, u32[]{:S(2)}, u32[]{:S(2)}) %collective-permute-start.15) | collective-permute-done | bytes 122912 | tf_op jit(solution)/shard_map/ppermute | solution.py:318
  92.3 2.0 %collective-permute-done.16.rest_2_ = bf16[240,256]{1,0:T(8,128)(2,1)S(1)} collective-permute-done((bf16[240,256]{1,0:T(8,128)(2,1)S(1)}, bf16[240,256]{1,0:T(8,128)(2,1)S(1)}, u32[]{:S(2)}, u32[]{:S(2)}) %collective-permute-start.16) | collective-permute-done | bytes 122912 | tf_op jit(solution)/shard_map/ppermute | solution.py:318
  94.3 1.7 %collective-permute-done.17.rest_3_ = bf16[240,256]{1,0:T(8,128)(2,1)S(1)} collective-permute-done((bf16[240,256]{1,0:T(8,128)(2,1)S(1)}, bf16[240,256]{1,0:T(8,128)(2,1)S(1)}, u32[]{:S(2)}, u32[]{:S(2)}) %collective-permute-start.17) | collective-permute-done | bytes 122912 | tf_op jit(solution)/shard_map/ppermute | solution.py:318
  96.1 0.0 all-to-all-done.1.cols_ref
  96.1 0.8 finish.1
  (2 shorter events, 0.1 us)
Async XLA Ops:
  1.5 5.1 %collective-permute-start.1 = (bf16[240,256]{1,0:T(8,128)(2,1)S(1)}, bf16[240,256]{1,0:T(8,128)(2,1)S(1)}, u32[]{:S(2)}, u32[]{:S(2)}) collective-permute-start(bf16[240,256]{1,0:T(8,128)(2,1)S(1)} %get-tuple-element.57), channel_id=1, source_target_pairs={{0,1},{1,0},{2,3},{3,2},{4,5},{5,4},{6,7},{7,6},{8,9},{9,8},{10,11... | collective-permute-start | bytes 368648 | tf_op jit(solution)/shard_map/ppermute | solution.py:325
  3.3 6.1 %collective-permute-start = (bf16[240,256]{1,0:T(8,128)(2,1)S(1)}, bf16[240,256]{1,0:T(8,128)(2,1)S(1)}, u32[]{:S(2)}, u32[]{:S(2)}) collective-permute-start(bf16[240,256]{1,0:T(8,128)(2,1)S(1)} %get-tuple-element.60), channel_id=1, source_target_pairs={{0,17},{1,16},{2,19},{3,18},{4,21},{5,20},{6,23},{7,22},{8,25},{9,... | collective-permute-start | bytes 368648 | tf_op jit(solution)/shard_map/ppermute | solution.py:332
  9.4 10.8 %collective-permute-start.6 = (bf16[2,240,256]{2,1,0:T(8,128)(2,1)S(1)}, bf16[2,240,256]{2,1,0:T(8,128)(2,1)S(1)}, u32[]{:S(2)}, u32[]{:S(2)}) collective-permute-start(bf16[2,240,256]{2,1,0:T(8,128)(2,1)S(1)} %pad_maximum_fusion.1.rest_0_), channel_id=1, source_target_pairs={{0,2},{1,3},{2,4},{3,5},{4,6},{5,7},{6,0},{7,1},{8,10},{9,11},{10,... | collective-permute-start | bytes 737288 | tf_op jit(solution)/shard_map/ppermute | solution.py:325
  10.9 12.2 %collective-permute-start.4 = (bf16[2,240,256]{2,1,0:T(8,128)(2,1)S(1)}, bf16[2,240,256]{2,1,0:T(8,128)(2,1)S(1)}, u32[]{:S(2)}, u32[]{:S(2)}) collective-permute-start(bf16[2,240,256]{2,1,0:T(8,128)(2,1)S(1)} %pad_maximum_fusion.1.rest_0_), channel_id=1, source_target_pairs={{0,4},{1,5},{2,6},{3,7},{4,0},{5,1},{6,2},{7,3},{8,12},{9,13},{10,... | collective-permute-start | bytes 737288 | tf_op jit(solution)/shard_map/ppermute | solution.py:325
  13.7 10.4 %collective-permute-start.7 = (bf16[2,240,256]{2,1,0:T(8,128)(2,1)S(1)}, bf16[2,240,256]{2,1,0:T(8,128)(2,1)S(1)}, u32[]{:S(2)}, u32[]{:S(2)}) collective-permute-start(bf16[2,240,256]{2,1,0:T(8,128)(2,1)S(1)} %pad_maximum_fusion.rest_1_), channel_id=1, source_target_pairs={{0,32},{1,33},{2,34},{3,35},{4,36},{5,37},{6,38},{7,39},{8,40},{9,... | collective-permute-start | bytes 737288 | tf_op jit(solution)/shard_map/ppermute | solution.py:332
  15.6 12.5 %collective-permute-start.5 = (bf16[2,240,256]{2,1,0:T(8,128)(2,1)S(1)}, bf16[2,240,256]{2,1,0:T(8,128)(2,1)S(1)}, u32[]{:S(2)}, u32[]{:S(2)}) collective-permute-start(bf16[2,240,256]{2,1,0:T(8,128)(2,1)S(1)} %pad_maximum_fusion.rest_1_), channel_id=1, source_target_pairs={{0,64},{1,65},{2,66},{3,67},{4,68},{5,69},{6,70},{7,71},{8,72},{9,... | collective-permute-start | bytes 737288 | tf_op jit(solution)/shard_map/ppermute | solution.py:332
  19.2 9.0 %collective-permute-start.3 = (bf16[2,240,256]{2,1,0:T(8,128)(2,1)S(1)}, bf16[2,240,256]{2,1,0:T(8,128)(2,1)S(1)}, u32[]{:S(2)}, u32[]{:S(2)}) collective-permute-start(bf16[2,240,256]{2,1,0:T(8,128)(2,1)S(1)} %pad_maximum_fusion.rest_1_), channel_id=1, source_target_pairs={{0,96},{1,97},{2,98},{3,99},{4,100},{5,101},{6,102},{7,103},{8,104... | collective-permute-start | bytes 737288 | tf_op jit(solution)/shard_map/ppermute | solution.py:332
  20.2 8.5 %collective-permute-start.2 = (bf16[2,240,256]{2,1,0:T(8,128)(2,1)S(1)}, bf16[2,240,256]{2,1,0:T(8,128)(2,1)S(1)}, u32[]{:S(2)}, u32[]{:S(2)}) collective-permute-start(bf16[2,240,256]{2,1,0:T(8,128)(2,1)S(1)} %pad_maximum_fusion.1.rest_0_), channel_id=1, source_target_pairs={{0,6},{1,7},{2,0},{3,1},{4,2},{5,3},{6,4},{7,5},{8,14},{9,15},{10,... | collective-permute-start | bytes 737288 | tf_op jit(solution)/shard_map/ppermute | solution.py:325
  23.2 5.5 %collective-permute-start.8 = (bf16[2,240,256]{2,1,0:T(8,128)(2,1)S(1)}, bf16[2,240,256]{2,1,0:T(8,128)(2,1)S(1)}, u32[]{:S(2)}, u32[]{:S(2)}) collective-permute-start(bf16[2,240,256]{2,1,0:T(8,128)(2,1)S(1)} %pad_maximum_fusion.rest_1_), channel_id=1, source_target_pairs={{0,8},{8,0},{16,24},{24,16},{32,40},{40,32},{48,56},{56,48},{64,72... | collective-permute-start | bytes 737288 | tf_op jit(solution)/shard_map/ppermute | solution.py:321
  24.1 4.5 %collective-permute-start.11 = (bf16[2,240,256]{2,1,0:T(8,128)(2,1)S(1)}, bf16[2,240,256]{2,1,0:T(8,128)(2,1)S(1)}, u32[]{:S(2)}, u32[]{:S(2)}) collective-permute-start(bf16[2,240,256]{2,1,0:T(8,128)(2,1)S(1)} %collective-permute-done.7.rest_7_), channel_id=1, source_target_pairs={{0,8},{8,0},{16,24},{24,16},{32,40},{40,32},{48,56},{56,48},{64,72... | collective-permute-start | bytes 737288 | tf_op jit(solution)/shard_map/ppermute | solution.py:321
  28.1 1.5 %collective-permute-start.10 = (bf16[2,240,256]{2,1,0:T(8,128)(2,1)S(1)}, bf16[2,240,256]{2,1,0:T(8,128)(2,1)S(1)}, u32[]{:S(2)}, u32[]{:S(2)}) collective-permute-start(bf16[2,240,256]{2,1,0:T(8,128)(2,1)S(1)} %collective-permute-done.5.rest_5_), channel_id=1, source_target_pairs={{0,8},{8,0},{16,24},{24,16},{32,40},{40,32},{48,56},{56,48},{64,72... | collective-permute-start | bytes 737288 | tf_op jit(solution)/shard_map/ppermute | solution.py:321
  28.1 1.9 %collective-permute-start.9 = (bf16[2,240,256]{2,1,0:T(8,128)(2,1)S(1)}, bf16[2,240,256]{2,1,0:T(8,128)(2,1)S(1)}, u32[]{:S(2)}, u32[]{:S(2)}) collective-permute-start(bf16[2,240,256]{2,1,0:T(8,128)(2,1)S(1)} %collective-permute-done.3.rest_3_), channel_id=1, source_target_pairs={{0,8},{8,0},{16,24},{24,16},{32,40},{40,32},{48,56},{56,48},{64,72... | collective-permute-start | bytes 737288 | tf_op jit(solution)/shard_map/ppermute | solution.py:321
  57.6 9.0 %collective-permute-start.12 = (bf16[8,240,256]{2,1,0:T(8,128)(2,1)S(1)}, bf16[8,240,256]{2,1,0:T(8,128)(2,1)S(1)}, u32[]{:S(2)}, u32[]{:S(2)}) collective-permute-start(bf16[8,240,256]{2,1,0:T(8,128)(2,1)S(1)} %get-tuple-element.45), channel_id=1, source_target_pairs={{0,8},{8,0},{16,24},{24,16},{32,40},{40,32},{48,56},{56,48},{64,72... | collective-permute-start | bytes 2949128 | tf_op jit(solution)/shard_map/ppermute | solution.py:321
  67.8 28.3 %all-to-all-start.1 = ((bf16[8,240,256]{2,1,0:T(8,128)(2,1)}), bf16[8,240,256]{2,1,0:T(8,128)(2,1)S(1)}, u32[]{:S(2)}, u32[]{:S(2)}) async-start(bf16[8,240,256]{2,1,0:T(8,128)(2,1)} %join_cols.1), calls=%async_computation.1 | async-start | bytes 1966080 | tf_op jit(solution)/shard_map/all_to_all | solution.py:357
  72.9 13.3 %collective-permute-start.13 = (bf16[4,192,256]{2,1,0:T(8,128)(2,1)S(1)}, bf16[4,192,256]{2,1,0:T(8,128)(2,1)S(1)}, u32[]{:S(2)}, u32[]{:S(2)}) collective-permute-start(bf16[4,192,256]{2,1,0:T(8,128)(2,1)S(1)} %get-tuple-element.46), channel_id=1, source_target_pairs={{0,1},{1,0},{2,3},{3,2},{4,5},{5,4},{6,7},{7,6},{8,9},{9,8},{10,11... | collective-permute-start | bytes 1179656 | tf_op jit(solution)/shard_map/ppermute | solution.py:318
  73.4 12.8 %collective-permute-start.14 = (bf16[4,48,256]{2,1,0:T(8,128)(2,1)S(1)}, bf16[4,48,256]{2,1,0:T(8,128)(2,1)S(1)}, u32[]{:S(2)}, u32[]{:S(2)}) collective-permute-start(bf16[4,48,256]{2,1,0:T(8,128)(2,1)S(1)} %get-tuple-element.47), channel_id=1, source_target_pairs={{0,1},{1,0},{2,3},{3,2},{4,5},{5,4},{6,7},{7,6},{8,9},{9,8},{10,11... | collective-permute-start | bytes 294920 | tf_op jit(solution)/shard_map/ppermute | solution.py:318
  86.3 6.0 %collective-permute-start.15 = (bf16[240,256]{1,0:T(8,128)(2,1)S(1)}, bf16[240,256]{1,0:T(8,128)(2,1)S(1)}, u32[]{:S(2)}, u32[]{:S(2)}) collective-permute-start(bf16[240,256]{1,0:T(8,128)(2,1)S(1)} %get-tuple-element.53), channel_id=1, source_target_pairs={{0,2},{1,3},{2,0},{3,1},{4,6},{5,7},{6,4},{7,5},{8,10},{9,11},{10,... | collective-permute-start | bytes 368648 | tf_op jit(solution)/shard_map/ppermute | solution.py:318
  87.0 7.4 %collective-permute-start.16 = (bf16[240,256]{1,0:T(8,128)(2,1)S(1)}, bf16[240,256]{1,0:T(8,128)(2,1)S(1)}, u32[]{:S(2)}, u32[]{:S(2)}) collective-permute-start(bf16[240,256]{1,0:T(8,128)(2,1)S(1)} %get-tuple-element.54), channel_id=1, source_target_pairs={{0,4},{1,5},{2,6},{3,7},{4,0},{5,1},{6,2},{7,3},{8,12},{9,13},{10,... | collective-permute-start | bytes 368648 | tf_op jit(solution)/shard_map/ppermute | solution.py:318
  89.0 7.0 %collective-permute-start.17 = (bf16[240,256]{1,0:T(8,128)(2,1)S(1)}, bf16[240,256]{1,0:T(8,128)(2,1)S(1)}, u32[]{:S(2)}, u32[]{:S(2)}) collective-permute-start(bf16[240,256]{1,0:T(8,128)(2,1)S(1)} %get-tuple-element.55), channel_id=1, source_target_pairs={{0,6},{1,7},{2,4},{3,5},{4,2},{5,3},{6,0},{7,1},{8,14},{9,15},{10,... | collective-permute-start | bytes 368648 | tf_op jit(solution)/shard_map/ppermute | solution.py:318

commit v2 on v1

--- a/solution.py
+++ b/solution.py
@@ -71,7 +71,7 @@
     step = pl.program_id(0)
     last = pl.num_programs(0) - 1
     count, cols = scores.shape
-    span = pick(cols, LANES, 1024)
+    span = pick(cols, LANES, 512)
     repeat = span // LANES
 
     def tiles(array):
@@ -133,7 +133,7 @@
     rows = mates * own
     cols = 2 * own * sum(part.shape[0] for part in b0_parts)
     pair = 2 * feat
-    step = pick(rows, LANES, 256)
+    step = pick(rows, LANES, 512)
     kept = [((rows, pair), BF16), ((pair, rows), BF16), ((rows, LANES), BF16), ((LANES, rows), BF16)]
     kept += [((cols, pair), BF16), ((cols, LANES), BF16), ((LANES, cols), BF16)]
     parts = [part for both in zip(a_parts, b0_parts) for part in both] + b1_parts
@@ -155,56 +155,89 @@
     return scaled, stats, kept
 
 
+def weigh_kernel(own, place_ref, stats_ref, scaled_ref, table_ref, mine_ref, given_ref, weights_ref):
+    stats = stats_ref[...]
+    peaks = stats[:, 0:1]
+    peak = jnp.max(peaks, axis=0)
+    weights = jnp.exp(peaks - peak[None]) * stats[:, 1:2]
+    total = jnp.sum(weights, axis=0)
+    table_ref[0:1, :] = peak + jnp.log(total)
+    table_ref[1:2, :] = jnp.sum(weights * stats[:, 2:3], axis=0) / total
+    table_ref[2:, :] = jnp.zeros((table_ref.shape[0] - 2, table_ref.shape[1]), F32)
+    at = place_ref[10]
+    weight = jnp.exp(stats_ref[at, 0:1] - peak) * stats_ref[at, 1:2] / total
+    weights_ref[...] = jnp.transpose(jnp.broadcast_to(weight, (LANES, weight.shape[1])))
+    for slot in range(mine_ref.shape[0]):
+        for flip, out_ref in enumerate((mine_ref, given_ref)):
+            chunk = 2 * (place_ref[11] ^ slot) + (place_ref[8] ^ flip)
+            rows = pl.ds(pl.multiple_of(chunk * own, 64), own)
+            out_ref[slot] = (weights_ref[rows, 0:1] * scaled_ref[rows, :].astype(F32)).astype(BF16)
+
+
+def weigh(place, stats, scaled, own):
+    rows, pair = scaled.shape
+    part = ((stats.shape[0] // 2, own, pair), BF16)
+    return pl.pallas_call(
+        functools.partial(weigh_kernel, own),
+        in_specs=[SMEM] + [pl.BlockSpec(memory_space=pltpu.VMEM)] * 2,
+        out_shape=shapes(((8, rows), F32), part, part),
+        scratch_shapes=[pltpu.VMEM((rows, LANES), F32)],
+        compiler_params=params(8),
+        name="weigh",
+    )(place, stats, scaled)
+
+
 def tile_kernel(
-    own, feat, last, place_ref, a_pair, a_pair_t, a_src, a_src_t, b_pair, b_dst, b_dst_t, stats_ref, *rest
+    own, feat, last, place_ref, a_pair, a_pair_t, a_src, a_src_t, b_pair, b_dst, b_dst_t, table, *rest
 ):
     pair = 2 * feat
     step = pl.program_id(0)
+    end = pl.num_programs(0) - 1
     if last:
-        start_ref, mine_ref, cols_ref, source_ref, *piece_refs, twin_ref, table, slots = rest
+        start_ref, mine_ref, cols_ref, source_ref, *piece_refs, twin_ref, scores, outer, slots = rest
     else:
-        scaled_ref, cols_ref, source_ref, mine_ref, given_ref, table, weights_ref = rest
+        cols_ref, source_ref, scores, outer = rest
     extra = cols_ref.shape[1] - own
+    count, rows = scores.shape
+    span = pick(rows, LANES, 256)
+
+    def work(ahead, behind):
+        col_sums = jnp.zeros((count, pair), F32)
+        target_sums = jnp.zeros((count, LANES), F32)
+        for start in range(0, rows, span):
+            part = slice(start, start + span)
+            if behind:
+                score = scores[:, part]
+                soft = jnp.exp(jnp.maximum(score, 0.0) - table[0:1, part])
+                grad = jnp.where(score > 0.0, soft * (outer[:, part] - table[1:2, part]), 0.0)
+                soft_half = soft.astype(BF16)
+                grad_half = grad.astype(BF16)
+                col_sums = col_sums + jnp.dot(soft_half, a_pair[part, :], preferred_element_type=F32)
+                target_sums = target_sums + jnp.dot(grad_half, a_src[part, :], preferred_element_type=F32)
+                source_ref[:, part] += jnp.dot(b_dst_t[:extra], grad_half, preferred_element_type=F32)
+            if ahead:
+                scores[:, part] = jnp.dot(b_dst[...], a_src_t[:, part], preferred_element_type=F32)
+                outer[:, part] = jnp.dot(b_pair[...], a_pair_t[:, part], preferred_element_type=F32)
+        if behind:
+            for slot in range(cols_ref.shape[0]):
+                here = slice(slot * own, (slot + 1) * own)
+                cols_ref[slot, :own, :] = col_sums[here].astype(BF16)
+                wide = jnp.concatenate([target_sums[here], jnp.zeros((pair - own, LANES), F32)], axis=0)
+                cols_ref[slot, own:, :] = jnp.transpose(wide)[:extra].astype(BF16)
 
     @pl.when(step == 0)
     def _():
         source_ref[...] = start_ref[...] if last else jnp.zeros_like(source_ref)
-        stats = stats_ref[...]
-        peaks = stats[:, 0:1]
-        peak = jnp.max(peaks, axis=0)
-        weights = jnp.exp(peaks - peak[None]) * stats[:, 1:2]
-        total = jnp.sum(weights, axis=0)
-        table[0:1, :] = peak + jnp.log(total)
-        table[1:2, :] = jnp.sum(weights * stats[:, 2:3], axis=0) / total
-        if not last:
-            at = place_ref[10]
-            weight = jnp.exp(stats_ref[at, 0:1] - peak) * stats_ref[at, 1:2] / total
-            weights_ref[...] = jnp.transpose(jnp.broadcast_to(weight, (LANES, weight.shape[1])))
-            for slot in range(mine_ref.shape[0]):
-                for flip, out_ref in enumerate((mine_ref, given_ref)):
-                    chunk = 2 * (place_ref[11] ^ slot) + (place_ref[8] ^ flip)
-                    rows = pl.ds(pl.multiple_of(chunk * own, 64), own)
-                    out_ref[slot] = (weights_ref[rows, 0:1] * scaled_ref[rows, :].astype(F32)).astype(BF16)
-
-    scores = jnp.dot(b_dst[...], a_src_t[...], preferred_element_type=F32)
-    outer = jnp.dot(b_pair[...], a_pair_t[...], preferred_element_type=F32)
-    soft = jnp.exp(jnp.maximum(scores, 0.0) - table[0:1, :])
-    grad = jnp.where(scores > 0.0, soft * (outer - table[1:2, :]), 0.0)
-    soft_half = soft.astype(BF16)
-    grad_half = grad.astype(BF16)
-    col_sums = jnp.dot(soft_half, a_pair[...], preferred_element_type=F32).astype(BF16)
-    target_sums = jnp.dot(grad_half, a_src[...], preferred_element_type=F32)
-    for slot in range(cols_ref.shape[0]):
-        rows = slice(slot * own, (slot + 1) * own)
-        cols_ref[slot, :own, :] = col_sums[rows]
-        wide = jnp.concatenate([target_sums[rows], jnp.zeros((pair - own, LANES), F32)], axis=0)
-        cols_ref[slot, own:, :] = jnp.transpose(wide)[:extra].astype(BF16)
-    source_ref[...] += jnp.dot(b_dst_t[:extra], grad_half, preferred_element_type=F32)
-
-    if last:
-
-        @pl.when(step == pl.num_programs(0) - 1)
-        def _():
+        work(True, False)
+
+    @pl.when((step > 0) & (step < end))
+    def _():
+        work(True, True)
+
+    @pl.when(step == end)
+    def _():
+        work(False, True)
+        if last:
             fill = jnp.zeros((extra, pair - own), F32)
             for chunk in range(slots.shape[0]):
                 part = source_ref[:, chunk * own : (chunk + 1) * own]
@@ -215,58 +248,67 @@
                 twin_ref[slot] = slots[2 * slot + 1].astype(BF16)
 
 
-def tile_sums(place, kept, half, stats, late, own, feat, extra, last, name):
+def tile_sums(place, kept, half, table, late, own, feat, extra, last, name):
     rows, pair = kept[0].shape
     cols = kept[4].shape[0] // 2
-    mates = stats.shape[0]
-    step = pick(cols, 2 * own, 2 * own)
-    base = half * (cols // step)
-    scratch = [pltpu.VMEM((8, rows), F32)]
+    mates = rows // own
+    step = pick(cols, 2 * own, 4 * own)
+    tiles = cols // step
+    base = half * tiles
+
+    def now(i):
+        return jnp.minimum(i, tiles - 1) + base
+
+    def then(i):
+        return jnp.maximum(i - 1, 0)
+
+    scratch = [pltpu.VMEM((step, rows), F32)] * 2
+    kinds = []
     if last:
         kinds = [((own + extra, pair), BF16)] * (mates // 2) + [((mates // 2, extra, pair), BF16)]
         scratch += [pltpu.VMEM((mates, extra, pair), F32)]
-    else:
-        kinds = [((mates // 2, own, pair), BF16)] * 2
-        scratch += [pltpu.VMEM((rows, LANES), F32)]
+    work = 1 << 20 if last else 2 * rows * cols * 1280
     return pl.pallas_call(
         functools.partial(tile_kernel, own, feat, last),
-        grid=(cols // step,),
+        grid=(tiles + 1,),
         in_specs=[
             SMEM,
             *[whole(x.shape) for x in kept[:4]],
-            pl.BlockSpec((step, pair), lambda i: (i + base, 0)),
-            pl.BlockSpec((step, LANES), lambda i: (i + base, 0)),
-            pl.BlockSpec((LANES, step), lambda i: (0, i + base)),
-            *[whole(x.shape) for x in (stats, *late)],
+            pl.BlockSpec((step, pair), lambda i: (now(i), 0)),
+            pl.BlockSpec((step, LANES), lambda i: (now(i), 0)),
+            pl.BlockSpec((LANES, step), lambda i: (0, then(i) + base)),
+            *[whole(x.shape) for x in (table, *late)],
         ],
-        out_specs=[pl.BlockSpec((step // own, own + extra, pair), lambda i: (i, 0, 0)), whole((extra, rows))]
+        out_specs=[pl.BlockSpec((step // own, own + extra, pair), lambda i: (then(i), 0, 0)), whole((extra, rows))]
         + [whole(shape) for shape, kind in kinds],
         out_shape=shapes(((cols // own, own + extra, pair), BF16), ((extra, rows), F32), *kinds),
         scratch_shapes=scratch,
         compiler_params=params(),
-        cost_estimate=pl.CostEstimate(flops=2 * rows * cols * 1280, bytes_accessed=8 << 20, transcendentals=rows * cols),
+        cost_estimate=pl.CostEstimate(flops=work, bytes_accessed=1 << 20, transcendentals=work >> 11),
         name=name,
-    )(place, *kept, stats, *late)
-
-
-def join_cols_kernel(own_ref, other_ref, out_ref):
+    )(place, *kept, table, *late)
+
+
+def join_cols_kernel(own_ref, other_ref, unused_ref, out_ref):
     out_ref[...] = (own_ref[...].astype(F32) + other_ref[...].astype(F32)).astype(BF16)
 
 
 def join_rows_kernel(given_ref, twin_ref, *rest):
     count, own = given_ref.shape[:2]
-    for slot, (piece_ref, out_ref) in enumerate(zip(rest[:count], rest[count:])):
+    for slot, (piece_ref, out_ref) in enumerate(zip(rest[:count], rest[count + 1 :])):
         out_ref[:own, :] = (piece_ref[:own, :].astype(F32) + given_ref[slot].astype(F32)).astype(BF16)
         out_ref[own:, :] = (piece_ref[own:, :].astype(F32) + twin_ref[slot].astype(F32)).astype(BF16)
 
 
-def join(kernel, name, outs, *arrays):
+def join(kernel, name, outs, *arrays, unread=()):
+    vmem, anywhere = pl.BlockSpec(memory_space=pltpu.VMEM), pl.BlockSpec(memory_space=pl.ANY)
     return pl.pallas_call(
         kernel,
+        in_specs=[vmem] * len(arrays) + [anywhere] * len(unread),
         out_shape=[jax.ShapeDtypeStruct(out.shape, out.dtype) for out in outs],
         compiler_params=params(8),
         name=name,
-    )(*arrays)
+    )(*arrays, *unread)
 
 
 def finish_kernel(own, feat, emb_count, cols_ref, *rest):
@@ -348,14 +390,15 @@
     stats = lax.all_to_all(stats, "col", 0, 0)
 
     sizes = (own, feat, extra)
-    other_cols, start, mine, given = tile_sums(place, kept, 1, stats, (scaled,), *sizes, False, "other_tile")
+    table, mine, given = weigh(place, stats, scaled, own)
+    given = mate(given, 1)
+    other_cols, start = tile_sums(place, kept, 1, table, (), *sizes, False, "other_tile")
     other_cols = swap(other_cols)
-    given = mate(given, 1)
-    own_cols, unused, *pieces, twin = tile_sums(place, kept, 0, stats, (start, mine), *sizes, True, "own_tile")
+    own_cols, unused, *pieces, twin = tile_sums(place, kept, 0, table, (start, mine), *sizes, True, "own_tile")
     twin = mate(twin, 1)
-    (cols,) = join(join_cols_kernel, "join_cols", [own_cols], own_cols, other_cols)
+    (cols,) = join(join_cols_kernel, "join_cols", [own_cols], own_cols, other_cols, unread=(given,))
+    pieces = join(join_rows_kernel, "join_rows", pieces, given, twin, *pieces, unread=(cols,))
     cols = lax.all_to_all(cols, both, 0, 0, axis_index_groups=groups)
-    pieces = join(join_rows_kernel, "join_rows", pieces, given, twin, *pieces)
     pieces = [mate(piece, 2 * slot) if slot else piece for slot, piece in enumerate(pieces)]
     return tuple(finish(cols, pieces, own, feat, emb_count))
 

time: 97.2 us -> 91.6 us (0.942)
  waiting for transfers between devices: 27.3 us -> 23.2 us
  Pallas kernels: 29.2 us -> 27.9 us
    ppermute x5, waiting for transfers between devices: 16.2 us -> 9.98 us  [mate(): return lax.ppermute(array, 'col', [(c, c ^ bits) for c in range(col_size)])]
    all_to_all x1, waiting for transfers between devices: 0.01 us -> 2.21 us  [local(): cols = lax.all_to_all(cols, both, 0, 0, axis_index_groups=groups)]
    pallas_call x1, Pallas kernels: 9.67 us -> 8.69 us  [row_stats(): pl.pallas_call(functools.partial(stats_kernel, own, feat), grid=(rows //...]
    pallas_call x4 -> x5, Pallas kernels: 18.8 us -> 18.4 us  [the longest x2 15.9 us: tile_sums(): pl.pallas_call(functools.partial(tile_kernel, own, feat, last), grid=(til...]
  transfers between devices with their start and end apart: 19 -> 19, of which waited for: 11 -> 13; matrix products, arithmetic and copies ran while one was open for 1% -> 1% of each run, Pallas kernels for 9% -> 9%
where the time goes in v2:
time: 91.6 us; the launch traced here: 91.3 us
  starting transfers between devices  28.4 us (31%)
  Pallas kernels  27.9 us (30%)
  waiting for transfers between devices  23.2 us (25%)
  blocking collectives  9.44 us (10%)
  other arithmetic  0.93 us (1%)
    pallas_call x2, Pallas kernels, tile_sums(): pl.pallas_call(functools.partial(tile_kernel, own, feat, last), grid=(til...  15.9 us
    ppermute x5, waiting for transfers between devices, mate(): return lax.ppermute(array, 'col', [(c, c ^ bits) for c in range(col_size)])  9.98 us
    all_to_all x1, blocking collectives, local(): stats = lax.all_to_all(stats, 'col', 0, 0)  9.44 us
    ppermute x4, starting transfers between devices, along_z(): return lax.ppermute(array, both, pairs)  8.69 us
    pallas_call x1, Pallas kernels, row_stats(): pl.pallas_call(functools.partial(stats_kernel, own, feat), grid=(rows //...  8.69 us
    ppermute x4, waiting for transfers between devices, along_z(): return lax.ppermute(array, both, pairs)  7.68 us
    ppermute x4, starting transfers between devices, along_x(): return lax.ppermute(array, 'col', pairs)  7.46 us
    ppermute x5, starting transfers between devices, mate(): return lax.ppermute(array, 'col', [(c, c ^ bits) for c in range(col_size)])  6.61 us
  transfers between devices with their start and end apart: 19, of which 13 were waited for; matrix products, arithmetic and copies ran while one was open for 1% of the time, Pallas kernels for 9%

profile of v2, /device:TPU:0, one launch (start us, length us, event | category | flops | bytes accessed | tf_op | source)
XLA Modules:
  0.0 91.3 jit_solution(11704680836256976688)
XLA Ops:
  0.6 0.9 fusion.1
  1.5 1.7 %collective-permute-start.1 = (bf16[240,256]{1,0:T(8,128)(2,1)S(1)}, bf16[240,256]{1,0:T(8,128)(2,1)S(1)}, u32[]{:S(2)}, u32[]{:S(2)}) collective-permute-start(bf16[240,256]{1,0:T(8,128)(2,1)S(1)} %get-tuple-element.59), channel_id=1, source_target_pairs={{0,1},{1,0},{2,3},{3,2},{4,5},{5,4},{6,7},{7,6},{8,9},{9,8},{10,11... | collective-permute-start | bytes 368648 | tf_op jit(solution)/shard_map/ppermute | solution.py:367
  3.3 2.2 %collective-permute-start = (bf16[240,256]{1,0:T(8,128)(2,1)S(1)}, bf16[240,256]{1,0:T(8,128)(2,1)S(1)}, u32[]{:S(2)}, u32[]{:S(2)}) collective-permute-start(bf16[240,256]{1,0:T(8,128)(2,1)S(1)} %get-tuple-element.62), channel_id=1, source_target_pairs={{0,17},{1,16},{2,19},{3,18},{4,21},{5,20},{6,23},{7,22},{8,25},{9,... | collective-permute-start | bytes 368648 | tf_op jit(solution)/shard_map/ppermute | solution.py:374
  5.4 0.7 dynamic-slice_bitcast_fusion.place_ref
  6.1 0.4 collective-permute-done.1
  6.6 2.7 %collective-permute-done = bf16[240,256]{1,0:T(8,128)(2,1)S(1)} collective-permute-done((bf16[240,256]{1,0:T(8,128)(2,1)S(1)}, bf16[240,256]{1,0:T(8,128)(2,1)S(1)}, u32[]{:S(2)}, u32[]{:S(2)}) %collective-permute-start) | collective-permute-done | bytes 122912 | tf_op jit(solution)/shard_map/ppermute | solution.py:374
  9.4 1.6 %collective-permute-start.6 = (bf16[2,240,256]{2,1,0:T(8,128)(2,1)S(1)}, bf16[2,240,256]{2,1,0:T(8,128)(2,1)S(1)}, u32[]{:S(2)}, u32[]{:S(2)}) collective-permute-start(bf16[2,240,256]{2,1,0:T(8,128)(2,1)S(1)} %pad_maximum_fusion.1.rest_0_), channel_id=1, source_target_pairs={{0,2},{1,3},{2,4},{3,5},{4,6},{5,7},{6,0},{7,1},{8,10},{9,11},{10,... | collective-permute-start | bytes 737288 | tf_op jit(solution)/shard_map/ppermute | solution.py:367
  10.9 2.7 %collective-permute-start.4 = (bf16[2,240,256]{2,1,0:T(8,128)(2,1)S(1)}, bf16[2,240,256]{2,1,0:T(8,128)(2,1)S(1)}, u32[]{:S(2)}, u32[]{:S(2)}) collective-permute-start(bf16[2,240,256]{2,1,0:T(8,128)(2,1)S(1)} %pad_maximum_fusion.1.rest_0_), channel_id=1, source_target_pairs={{0,4},{1,5},{2,6},{3,7},{4,0},{5,1},{6,2},{7,3},{8,12},{9,13},{10,... | collective-permute-start | bytes 737288 | tf_op jit(solution)/shard_map/ppermute | solution.py:367
  13.7 1.9 %collective-permute-start.7 = (bf16[2,240,256]{2,1,0:T(8,128)(2,1)S(1)}, bf16[2,240,256]{2,1,0:T(8,128)(2,1)S(1)}, u32[]{:S(2)}, u32[]{:S(2)}) collective-permute-start(bf16[2,240,256]{2,1,0:T(8,128)(2,1)S(1)} %pad_maximum_fusion.rest_1_), channel_id=1, source_target_pairs={{0,32},{1,33},{2,34},{3,35},{4,36},{5,37},{6,38},{7,39},{8,40},{9,... | collective-permute-start | bytes 737288 | tf_op jit(solution)/shard_map/ppermute | solution.py:374
  15.6 3.6 %collective-permute-start.5 = (bf16[2,240,256]{2,1,0:T(8,128)(2,1)S(1)}, bf16[2,240,256]{2,1,0:T(8,128)(2,1)S(1)}, u32[]{:S(2)}, u32[]{:S(2)}) collective-permute-start(bf16[2,240,256]{2,1,0:T(8,128)(2,1)S(1)} %pad_maximum_fusion.rest_1_), channel_id=1, source_target_pairs={{0,64},{1,65},{2,66},{3,67},{4,68},{5,69},{6,70},{7,71},{8,72},{9,... | collective-permute-start | bytes 737288 | tf_op jit(solution)/shard_map/ppermute | solution.py:374
  19.2 1.0 %collective-permute-start.3 = (bf16[2,240,256]{2,1,0:T(8,128)(2,1)S(1)}, bf16[2,240,256]{2,1,0:T(8,128)(2,1)S(1)}, u32[]{:S(2)}, u32[]{:S(2)}) collective-permute-start(bf16[2,240,256]{2,1,0:T(8,128)(2,1)S(1)} %pad_maximum_fusion.rest_1_), channel_id=1, source_target_pairs={{0,96},{1,97},{2,98},{3,99},{4,100},{5,101},{6,102},{7,103},{8,104... | collective-permute-start | bytes 737288 | tf_op jit(solution)/shard_map/ppermute | solution.py:374
  20.2 0.0 collective-permute-done.6.rest_6_
  20.2 1.4 %collective-permute-start.2 = (bf16[2,240,256]{2,1,0:T(8,128)(2,1)S(1)}, bf16[2,240,256]{2,1,0:T(8,128)(2,1)S(1)}, u32[]{:S(2)}, u32[]{:S(2)}) collective-permute-start(bf16[2,240,256]{2,1,0:T(8,128)(2,1)S(1)} %pad_maximum_fusion.1.rest_0_), channel_id=1, source_target_pairs={{0,6},{1,7},{2,0},{3,1},{4,2},{5,3},{6,4},{7,5},{8,14},{9,15},{10,... | collective-permute-start | bytes 737288 | tf_op jit(solution)/shard_map/ppermute | solution.py:367
  21.6 1.6 %collective-permute-done.4.rest_4_ = bf16[2,240,256]{2,1,0:T(8,128)(2,1)S(1)} collective-permute-done((bf16[2,240,256]{2,1,0:T(8,128)(2,1)S(1)}, bf16[2,240,256]{2,1,0:T(8,128)(2,1)S(1)}, u32[]{:S(2)}, u32[]{:S(2)}) %collective-permute-start.4) | collective-permute-done | bytes 245792 | tf_op jit(solution)/shard_map/ppermute | solution.py:367
  23.2 0.0 collective-permute-start.8
  23.2 0.9 %collective-permute-done.7.rest_7_ = bf16[2,240,256]{2,1,0:T(8,128)(2,1)S(1)} collective-permute-done((bf16[2,240,256]{2,1,0:T(8,128)(2,1)S(1)}, bf16[2,240,256]{2,1,0:T(8,128)(2,1)S(1)}, u32[]{:S(2)}, u32[]{:S(2)}) %collective-permute-start.7) | collective-permute-done | bytes 245792 | tf_op jit(solution)/shard_map/ppermute | solution.py:374
  24.1 0.0 collective-permute-start.11
  24.1 4.0 %collective-permute-done.5.rest_5_ = bf16[2,240,256]{2,1,0:T(8,128)(2,1)S(1)} collective-permute-done((bf16[2,240,256]{2,1,0:T(8,128)(2,1)S(1)}, bf16[2,240,256]{2,1,0:T(8,128)(2,1)S(1)}, u32[]{:S(2)}, u32[]{:S(2)}) %collective-permute-start.5) | collective-permute-done | bytes 245792 | tf_op jit(solution)/shard_map/ppermute | solution.py:374
  28.1 0.0 collective-permute-start.10
  28.1 0.0 collective-permute-done.3.rest_3_
  28.1 0.5 collective-permute-start.9
  28.6 0.0 collective-permute-done.2.rest_2_
  28.6 0.0 collective-permute-done.8.rest_8_
  28.6 0.0 collective-permute-done.11.rest_11_
  28.6 1.0 %collective-permute-done.10.rest_10_ = bf16[2,240,256]{2,1,0:T(8,128)(2,1)S(1)} collective-permute-done((bf16[2,240,256]{2,1,0:T(8,128)(2,1)S(1)}, bf16[2,240,256]{2,1,0:T(8,128)(2,1)S(1)}, u32[]{:S(2)}, u32[]{:S(2)}) %collective-permute-start.10) | collective-permute-done | bytes 245792 | tf_op jit(solution)/shard_map/ppermute | solution.py:363
  29.6 0.4 collective-permute-done.9.rest_9_
  30.0 8.7 %row_stats.1 = (bf16[1536,256]{1,0:T(8,128)(2,1)S(1)}, f32[8,4,1536]{2,1,0:T(4,128)S(1)}, bf16[1536,256]{1,0:T(8,128)(2,1)S(1)}, bf16[256,1536]{1,0:T(8,128)(2,1...) custom-call(s32[16]{0:T(128)S(1)} %dynamic-slice_bitcast_fusion.plac, ...), custom_call_target="tpu_custom_call" | custom-call | flops 4831838208 | bytes 8388608 | tf_op jit(solution)/shard_map/row_stats/pallas_call | solution.py:140
  38.7 9.4 %all_to_all.10.stats_ref = f32[8,4,1536]{2,1,0:T(4,128)S(1)} all-to-all(f32[8,4,1536]{2,1,0:T(4,128)S(1)} %get-tuple-element.41), channel_id=1, replica_groups=mesh['row'=16,'col'=8] {'col'}, dimensions={0} | all-to-all | bytes 393216 | tf_op jit(solution)/shard_map/all_to_all | solution.py:390
  48.1 1.2 %weigh.1 = (f32[8,1536]{1,0:T(8,128)S(1)}, bf16[4,192,256]{2,1,0:T(8,128)(2,1)S(1)}, bf16[4,192,256]{2,1,0:T(8,128)(2,1)S(1)}) custom-call(s32[16]{0:T(128)S(1)} %dynamic-slice_bitcast_fusion.place_ref, f32[8,4,1536]{2,1,0:T(4,128)S(1)} %all_to_all.10.stats_ref, bf16[1536,256]{1,0:T(8,128)(2,1)S(1)} %get-tuple-element.42.scaled_ref), custom_call_target="tpu_custom_call" | custom-call | tf_op jit(solution)/shard_map/weigh/pallas_call | solution.py:180
  49.3 7.5 %other_tile.1 = (bf16[8,240,256]{2,1,0:T(8,128)(2,1)S(1)}, f32[48,1536]{1,0:T(8,128)S(1)}) custom-call(s32[16]{0:T(128)S(1)} %dynamic-slice_bitcast_fusion.place_ref, bf16[1536,256]{1,0:T(8,128)(2,1)S(1)} %get-tuple-element.34.a_pair, bf16[256,1536]{1,0:T(8,128)(2,1)S(1)} %get-tuple-element.35.a_pair_t, bf16[1536,128]{1,0:T(8,128)(2,1)S(1)} %get-tuple-element.36.a_src, ...), custom_call_target="tpu_custom_call" | custom-call | flops 6039797760 | bytes 1048576 | tf_op jit(solution)/shard_map/other_tile/pallas_call | solution.py:271
  56.9 0.1 collective-permute-start.12
  57.0 1.3 %collective-permute-start.13 = (bf16[4,192,256]{2,1,0:T(8,128)(2,1)S(1)}, bf16[4,192,256]{2,1,0:T(8,128)(2,1)S(1)}, u32[]{:S(2)}, u32[]{:S(2)}) collective-permute-start(bf16[4,192,256]{2,1,0:T(8,128)(2,1)S(1)} %get-tuple-element.48), channel_id=1, source_target_pairs={{0,1},{1,0},{2,3},{3,2},{4,5},{5,4},{6,7},{7,6},{8,9},{9,8},{10,11... | collective-permute-start | bytes 1179656 | tf_op jit(solution)/shard_map/ppermute | solution.py:360
  58.3 8.3 %own_tile.1 = (bf16[8,240,256]{2,1,0:T(8,128)(2,1)S(1)}, f32[48,1536]{1,0:T(8,128)}, bf16[240,256]{1,0:T(8,128)(2,1)S(1)}, bf16[240,256]{1,0:T(8,128)(2,1)S(1)},...) custom-call(s32[16]{0:T(128)S(1)} %dynamic-slice_bitcast_fusion.place_ref, ...), custom_call_target="tpu_custom_call" | custom-call | flops 1048576 | bytes 1048576 | tf_op jit(solution)/shard_map/own_tile/pallas_call | solution.py:271
  66.6 1.9 %collective-permute-done.13.unused_ref.given_ref = bf16[4,192,256]{2,1,0:T(8,128)(2,1)S(1)} collective-permute-done((bf16[4,192,256]{2,1,0:T(8,128)(2,1)S(1)}, bf16[4,192,256]{2,1,0:T(8,128)(2,1)S(1)}, u32[]{:S(2)}, u32[]{:S(2)}) %collective-permute-start.13) | collective-permute-done | bytes 393248 | tf_op jit(solution)/shard_map/ppermute | solution.py:360
  68.5 0.0 collective-permute-done.12.other_ref
  68.5 1.2 %join_cols.1.rest_4_ = bf16[8,240,256]{2,1,0:T(8,128)(2,1)} custom-call(bf16[8,240,256]{2,1,0:T(8,128)(2,1)S(1)} %get-tuple-element.46.own_ref, bf16[8,240,256]{2,1,0:T(8,128)(2,1)S(1)} %collective-permute-done.12.other_ref, bf16[4,192,256]{2,1,0:T(8,128)(2,1)S(1)} %collective-permute-done.13.unused_ref.given_ref), custom_call_target="tpu_custom_call" | custom-call | tf_op jit(solution)/shard_map/join_cols/pallas_call | solution.py:305
  69.7 5.1 %all-to-all-start.1 = ((bf16[8,240,256]{2,1,0:T(8,128)(2,1)}), bf16[8,240,256]{2,1,0:T(8,128)(2,1)S(1)}, u32[]{:S(2)}, u32[]{:S(2)}) async-start(bf16[8,240,256]{2,1,0:T(8,128)(2,1)} %join_cols.1.rest_4_), calls=%async_computation.1 | async-start | bytes 1966080 | tf_op jit(solution)/shard_map/all_to_all | solution.py:401
  74.8 0.5 collective-permute-start.14
  75.3 4.1 %collective-permute-done.14.twin_ref = bf16[4,48,256]{2,1,0:T(8,128)(2,1)S(1)} collective-permute-done((bf16[4,48,256]{2,1,0:T(8,128)(2,1)S(1)}, bf16[4,48,256]{2,1,0:T(8,128)(2,1)S(1)}, u32[]{:S(2)}, u32[]{:S(2)}) %collective-permute-start.14) | collective-permute-done | bytes 98336 | tf_op jit(solution)/shard_map/ppermute | solution.py:360
  79.4 0.1 join_rows.1
  79.5 0.7 collective-permute-start.15
  80.1 2.1 %collective-permute-start.16 = (bf16[240,256]{1,0:T(8,128)(2,1)S(1)}, bf16[240,256]{1,0:T(8,128)(2,1)S(1)}, u32[]{:S(2)}, u32[]{:S(2)}) collective-permute-start(bf16[240,256]{1,0:T(8,128)(2,1)S(1)} %get-tuple-element.56), channel_id=1, source_target_pairs={{0,4},{1,5},{2,6},{3,7},{4,0},{5,1},{6,2},{7,3},{8,12},{9,13},{10,... | collective-permute-start | bytes 368648 | tf_op jit(solution)/shard_map/ppermute | solution.py:360
  82.2 2.1 %collective-permute-start.17 = (bf16[240,256]{1,0:T(8,128)(2,1)S(1)}, bf16[240,256]{1,0:T(8,128)(2,1)S(1)}, u32[]{:S(2)}, u32[]{:S(2)}) collective-permute-start(bf16[240,256]{1,0:T(8,128)(2,1)S(1)} %get-tuple-element.57), channel_id=1, source_target_pairs={{0,6},{1,7},{2,4},{3,5},{4,2},{5,3},{6,0},{7,1},{8,14},{9,15},{10,... | collective-permute-start | bytes 368648 | tf_op jit(solution)/shard_map/ppermute | solution.py:360
  84.3 0.2 collective-permute-done.15.rest_1_
  84.4 2.1 %collective-permute-done.16.rest_2_ = bf16[240,256]{1,0:T(8,128)(2,1)S(1)} collective-permute-done((bf16[240,256]{1,0:T(8,128)(2,1)S(1)}, bf16[240,256]{1,0:T(8,128)(2,1)S(1)}, u32[]{:S(2)}, u32[]{:S(2)}) %collective-permute-start.16) | collective-permute-done | bytes 122912 | tf_op jit(solution)/shard_map/ppermute | solution.py:360
  86.5 1.8 %collective-permute-done.17.rest_3_ = bf16[240,256]{1,0:T(8,128)(2,1)S(1)} collective-permute-done((bf16[240,256]{1,0:T(8,128)(2,1)S(1)}, bf16[240,256]{1,0:T(8,128)(2,1)S(1)}, u32[]{:S(2)}, u32[]{:S(2)}) %collective-permute-start.17) | collective-permute-done | bytes 122912 | tf_op jit(solution)/shard_map/ppermute | solution.py:360
  88.3 2.2 %all-to-all-done.1.cols_ref = bf16[8,240,256]{2,1,0:T(8,128)(2,1)S(1)} async-done(((bf16[8,240,256]{2,1,0:T(8,128)(2,1)}), bf16[8,240,256]{2,1,0:T(8,128)(2,1)S(1)}, u32[]{:S(2)}, u32[]{:S(2)}) %all-to-all-start.1) | async-done | bytes 983072 | tf_op jit(solution)/shard_map/all_to_all | solution.py:401
  90.5 0.8 finish.1
  (2 shorter events, 0.1 us)
Async XLA Ops:
  1.5 5.1 %collective-permute-start.1 = (bf16[240,256]{1,0:T(8,128)(2,1)S(1)}, bf16[240,256]{1,0:T(8,128)(2,1)S(1)}, u32[]{:S(2)}, u32[]{:S(2)}) collective-permute-start(bf16[240,256]{1,0:T(8,128)(2,1)S(1)} %get-tuple-element.59), channel_id=1, source_target_pairs={{0,1},{1,0},{2,3},{3,2},{4,5},{5,4},{6,7},{7,6},{8,9},{9,8},{10,11... | collective-permute-start | bytes 368648 | tf_op jit(solution)/shard_map/ppermute | solution.py:367
  3.3 6.1 %collective-permute-start = (bf16[240,256]{1,0:T(8,128)(2,1)S(1)}, bf16[240,256]{1,0:T(8,128)(2,1)S(1)}, u32[]{:S(2)}, u32[]{:S(2)}) collective-permute-start(bf16[240,256]{1,0:T(8,128)(2,1)S(1)} %get-tuple-element.62), channel_id=1, source_target_pairs={{0,17},{1,16},{2,19},{3,18},{4,21},{5,20},{6,23},{7,22},{8,25},{9,... | collective-permute-start | bytes 368648 | tf_op jit(solution)/shard_map/ppermute | solution.py:374
  9.4 10.8 %collective-permute-start.6 = (bf16[2,240,256]{2,1,0:T(8,128)(2,1)S(1)}, bf16[2,240,256]{2,1,0:T(8,128)(2,1)S(1)}, u32[]{:S(2)}, u32[]{:S(2)}) collective-permute-start(bf16[2,240,256]{2,1,0:T(8,128)(2,1)S(1)} %pad_maximum_fusion.1.rest_0_), channel_id=1, source_target_pairs={{0,2},{1,3},{2,4},{3,5},{4,6},{5,7},{6,0},{7,1},{8,10},{9,11},{10,... | collective-permute-start | bytes 737288 | tf_op jit(solution)/shard_map/ppermute | solution.py:367
  10.9 12.2 %collective-permute-start.4 = (bf16[2,240,256]{2,1,0:T(8,128)(2,1)S(1)}, bf16[2,240,256]{2,1,0:T(8,128)(2,1)S(1)}, u32[]{:S(2)}, u32[]{:S(2)}) collective-permute-start(bf16[2,240,256]{2,1,0:T(8,128)(2,1)S(1)} %pad_maximum_fusion.1.rest_0_), channel_id=1, source_target_pairs={{0,4},{1,5},{2,6},{3,7},{4,0},{5,1},{6,2},{7,3},{8,12},{9,13},{10,... | collective-permute-start | bytes 737288 | tf_op jit(solution)/shard_map/ppermute | solution.py:367
  13.7 10.4 %collective-permute-start.7 = (bf16[2,240,256]{2,1,0:T(8,128)(2,1)S(1)}, bf16[2,240,256]{2,1,0:T(8,128)(2,1)S(1)}, u32[]{:S(2)}, u32[]{:S(2)}) collective-permute-start(bf16[2,240,256]{2,1,0:T(8,128)(2,1)S(1)} %pad_maximum_fusion.rest_1_), channel_id=1, source_target_pairs={{0,32},{1,33},{2,34},{3,35},{4,36},{5,37},{6,38},{7,39},{8,40},{9,... | collective-permute-start | bytes 737288 | tf_op jit(solution)/shard_map/ppermute | solution.py:374
  15.6 12.5 %collective-permute-start.5 = (bf16[2,240,256]{2,1,0:T(8,128)(2,1)S(1)}, bf16[2,240,256]{2,1,0:T(8,128)(2,1)S(1)}, u32[]{:S(2)}, u32[]{:S(2)}) collective-permute-start(bf16[2,240,256]{2,1,0:T(8,128)(2,1)S(1)} %pad_maximum_fusion.rest_1_), channel_id=1, source_target_pairs={{0,64},{1,65},{2,66},{3,67},{4,68},{5,69},{6,70},{7,71},{8,72},{9,... | collective-permute-start | bytes 737288 | tf_op jit(solution)/shard_map/ppermute | solution.py:374
  19.2 9.0 %collective-permute-start.3 = (bf16[2,240,256]{2,1,0:T(8,128)(2,1)S(1)}, bf16[2,240,256]{2,1,0:T(8,128)(2,1)S(1)}, u32[]{:S(2)}, u32[]{:S(2)}) collective-permute-start(bf16[2,240,256]{2,1,0:T(8,128)(2,1)S(1)} %pad_maximum_fusion.rest_1_), channel_id=1, source_target_pairs={{0,96},{1,97},{2,98},{3,99},{4,100},{5,101},{6,102},{7,103},{8,104... | collective-permute-start | bytes 737288 | tf_op jit(solution)/shard_map/ppermute | solution.py:374
  20.2 8.5 %collective-permute-start.2 = (bf16[2,240,256]{2,1,0:T(8,128)(2,1)S(1)}, bf16[2,240,256]{2,1,0:T(8,128)(2,1)S(1)}, u32[]{:S(2)}, u32[]{:S(2)}) collective-permute-start(bf16[2,240,256]{2,1,0:T(8,128)(2,1)S(1)} %pad_maximum_fusion.1.rest_0_), channel_id=1, source_target_pairs={{0,6},{1,7},{2,0},{3,1},{4,2},{5,3},{6,4},{7,5},{8,14},{9,15},{10,... | collective-permute-start | bytes 737288 | tf_op jit(solution)/shard_map/ppermute | solution.py:367
  23.2 5.5 %collective-permute-start.8 = (bf16[2,240,256]{2,1,0:T(8,128)(2,1)S(1)}, bf16[2,240,256]{2,1,0:T(8,128)(2,1)S(1)}, u32[]{:S(2)}, u32[]{:S(2)}) collective-permute-start(bf16[2,240,256]{2,1,0:T(8,128)(2,1)S(1)} %pad_maximum_fusion.rest_1_), channel_id=1, source_target_pairs={{0,8},{8,0},{16,24},{24,16},{32,40},{40,32},{48,56},{56,48},{64,72... | collective-permute-start | bytes 737288 | tf_op jit(solution)/shard_map/ppermute | solution.py:363
  24.1 4.5 %collective-permute-start.11 = (bf16[2,240,256]{2,1,0:T(8,128)(2,1)S(1)}, bf16[2,240,256]{2,1,0:T(8,128)(2,1)S(1)}, u32[]{:S(2)}, u32[]{:S(2)}) collective-permute-start(bf16[2,240,256]{2,1,0:T(8,128)(2,1)S(1)} %collective-permute-done.7.rest_7_), channel_id=1, source_target_pairs={{0,8},{8,0},{16,24},{24,16},{32,40},{40,32},{48,56},{56,48},{64,72... | collective-permute-start | bytes 737288 | tf_op jit(solution)/shard_map/ppermute | solution.py:363
  28.1 1.5 %collective-permute-start.10 = (bf16[2,240,256]{2,1,0:T(8,128)(2,1)S(1)}, bf16[2,240,256]{2,1,0:T(8,128)(2,1)S(1)}, u32[]{:S(2)}, u32[]{:S(2)}) collective-permute-start(bf16[2,240,256]{2,1,0:T(8,128)(2,1)S(1)} %collective-permute-done.5.rest_5_), channel_id=1, source_target_pairs={{0,8},{8,0},{16,24},{24,16},{32,40},{40,32},{48,56},{56,48},{64,72... | collective-permute-start | bytes 737288 | tf_op jit(solution)/shard_map/ppermute | solution.py:363
  28.1 1.9 %collective-permute-start.9 = (bf16[2,240,256]{2,1,0:T(8,128)(2,1)S(1)}, bf16[2,240,256]{2,1,0:T(8,128)(2,1)S(1)}, u32[]{:S(2)}, u32[]{:S(2)}) collective-permute-start(bf16[2,240,256]{2,1,0:T(8,128)(2,1)S(1)} %collective-permute-done.3.rest_3_), channel_id=1, source_target_pairs={{0,8},{8,0},{16,24},{24,16},{32,40},{40,32},{48,56},{56,48},{64,72... | collective-permute-start | bytes 737288 | tf_op jit(solution)/shard_map/ppermute | solution.py:363
  56.9 11.6 %collective-permute-start.12 = (bf16[8,240,256]{2,1,0:T(8,128)(2,1)S(1)}, bf16[8,240,256]{2,1,0:T(8,128)(2,1)S(1)}, u32[]{:S(2)}, u32[]{:S(2)}) collective-permute-start(bf16[8,240,256]{2,1,0:T(8,128)(2,1)S(1)} %get-tuple-element.47), channel_id=1, source_target_pairs={{0,8},{8,0},{16,24},{24,16},{32,40},{40,32},{48,56},{56,48},{64,72... | collective-permute-start | bytes 2949128 | tf_op jit(solution)/shard_map/ppermute | solution.py:363
  57.0 11.5 %collective-permute-start.13 = (bf16[4,192,256]{2,1,0:T(8,128)(2,1)S(1)}, bf16[4,192,256]{2,1,0:T(8,128)(2,1)S(1)}, u32[]{:S(2)}, u32[]{:S(2)}) collective-permute-start(bf16[4,192,256]{2,1,0:T(8,128)(2,1)S(1)} %get-tuple-element.48), channel_id=1, source_target_pairs={{0,1},{1,0},{2,3},{3,2},{4,5},{5,4},{6,7},{7,6},{8,9},{9,8},{10,11... | collective-permute-start | bytes 1179656 | tf_op jit(solution)/shard_map/ppermute | solution.py:360
  69.7 20.8 %all-to-all-start.1 = ((bf16[8,240,256]{2,1,0:T(8,128)(2,1)}), bf16[8,240,256]{2,1,0:T(8,128)(2,1)S(1)}, u32[]{:S(2)}, u32[]{:S(2)}) async-start(bf16[8,240,256]{2,1,0:T(8,128)(2,1)} %join_cols.1.rest_4_), calls=%async_computation.1 | async-start | bytes 1966080 | tf_op jit(solution)/shard_map/all_to_all | solution.py:401
  74.8 4.6 %collective-permute-start.14 = (bf16[4,48,256]{2,1,0:T(8,128)(2,1)S(1)}, bf16[4,48,256]{2,1,0:T(8,128)(2,1)S(1)}, u32[]{:S(2)}, u32[]{:S(2)}) collective-permute-start(bf16[4,48,256]{2,1,0:T(8,128)(2,1)S(1)} %get-tuple-element.49), channel_id=1, source_target_pairs={{0,1},{1,0},{2,3},{3,2},{4,5},{5,4},{6,7},{7,6},{8,9},{9,8},{10,11... | collective-permute-start | bytes 294920 | tf_op jit(solution)/shard_map/ppermute | solution.py:360
  79.5 5.0 %collective-permute-start.15 = (bf16[240,256]{1,0:T(8,128)(2,1)S(1)}, bf16[240,256]{1,0:T(8,128)(2,1)S(1)}, u32[]{:S(2)}, u32[]{:S(2)}) collective-permute-start(bf16[240,256]{1,0:T(8,128)(2,1)S(1)} %get-tuple-element.55), channel_id=1, source_target_pairs={{0,2},{1,3},{2,0},{3,1},{4,6},{5,7},{6,4},{7,5},{8,10},{9,11},{10,... | collective-permute-start | bytes 368648 | tf_op jit(solution)/shard_map/ppermute | solution.py:360
  80.1 6.4 %collective-permute-start.16 = (bf16[240,256]{1,0:T(8,128)(2,1)S(1)}, bf16[240,256]{1,0:T(8,128)(2,1)S(1)}, u32[]{:S(2)}, u32[]{:S(2)}) collective-permute-start(bf16[240,256]{1,0:T(8,128)(2,1)S(1)} %get-tuple-element.56), channel_id=1, source_target_pairs={{0,4},{1,5},{2,6},{3,7},{4,0},{5,1},{6,2},{7,3},{8,12},{9,13},{10,... | collective-permute-start | bytes 368648 | tf_op jit(solution)/shard_map/ppermute | solution.py:360
  82.2 6.1 %collective-permute-start.17 = (bf16[240,256]{1,0:T(8,128)(2,1)S(1)}, bf16[240,256]{1,0:T(8,128)(2,1)S(1)}, u32[]{:S(2)}, u32[]{:S(2)}) collective-permute-start(bf16[240,256]{1,0:T(8,128)(2,1)S(1)} %get-tuple-element.57), channel_id=1, source_target_pairs={{0,6},{1,7},{2,4},{3,5},{4,2},{5,3},{6,0},{7,1},{8,14},{9,15},{10,... | collective-permute-start | bytes 368648 | tf_op jit(solution)/shard_map/ppermute | solution.py:360

commit v3 on v2

--- a/solution.py
+++ b/solution.py
@@ -176,7 +176,8 @@
 
 def weigh(place, stats, scaled, own):
     rows, pair = scaled.shape
-    part = ((stats.shape[0] // 2, own, pair), BF16)
+    count = stats.shape[0] // 2
+    part = ((count, own, pair), BF16)
     return pl.pallas_call(
         functools.partial(weigh_kernel, own),
         in_specs=[SMEM] + [pl.BlockSpec(memory_space=pltpu.VMEM)] * 2,
@@ -187,109 +188,85 @@
     )(place, stats, scaled)
 
 
-def tile_kernel(
-    own, feat, last, place_ref, a_pair, a_pair_t, a_src, a_src_t, b_pair, b_dst, b_dst_t, table, *rest
-):
+def tile_kernel(own, feat, half, place_ref, a_pair, a_pair_t, a_src, a_src_t, b_pair, b_dst, b_dst_t, table, *rest):
     pair = 2 * feat
-    step = pl.program_id(0)
-    end = pl.num_programs(0) - 1
+    last = half == 0
     if last:
-        start_ref, mine_ref, cols_ref, source_ref, *piece_refs, twin_ref, scores, outer, slots = rest
+        start_ref, mine_ref, cols_ref, source_ref, *piece_refs, twin_ref = rest[:-5]
+        col_sums, target_sums, scores, outer, slots = rest[-5:]
     else:
-        cols_ref, source_ref, scores, outer = rest
+        cols_ref, source_ref, col_sums, target_sums, scores, outer = rest
     extra = cols_ref.shape[1] - own
-    count, rows = scores.shape
-    span = pick(rows, LANES, 256)
-
-    def work(ahead, behind):
-        col_sums = jnp.zeros((count, pair), F32)
-        target_sums = jnp.zeros((count, LANES), F32)
-        for start in range(0, rows, span):
-            part = slice(start, start + span)
-            if behind:
-                score = scores[:, part]
-                soft = jnp.exp(jnp.maximum(score, 0.0) - table[0:1, part])
-                grad = jnp.where(score > 0.0, soft * (outer[:, part] - table[1:2, part]), 0.0)
-                soft_half = soft.astype(BF16)
-                grad_half = grad.astype(BF16)
-                col_sums = col_sums + jnp.dot(soft_half, a_pair[part, :], preferred_element_type=F32)
-                target_sums = target_sums + jnp.dot(grad_half, a_src[part, :], preferred_element_type=F32)
-                source_ref[:, part] += jnp.dot(b_dst_t[:extra], grad_half, preferred_element_type=F32)
-            if ahead:
-                scores[:, part] = jnp.dot(b_dst[...], a_src_t[:, part], preferred_element_type=F32)
-                outer[:, part] = jnp.dot(b_pair[...], a_pair_t[:, part], preferred_element_type=F32)
-        if behind:
-            for slot in range(cols_ref.shape[0]):
-                here = slice(slot * own, (slot + 1) * own)
-                cols_ref[slot, :own, :] = col_sums[here].astype(BF16)
-                wide = jnp.concatenate([target_sums[here], jnp.zeros((pair - own, LANES), F32)], axis=0)
-                cols_ref[slot, own:, :] = jnp.transpose(wide)[:extra].astype(BF16)
-
-    @pl.when(step == 0)
-    def _():
-        source_ref[...] = start_ref[...] if last else jnp.zeros_like(source_ref)
-        work(True, False)
-
-    @pl.when((step > 0) & (step < end))
-    def _():
-        work(True, True)
-
-    @pl.when(step == end)
-    def _():
-        work(False, True)
-        if last:
-            fill = jnp.zeros((extra, pair - own), F32)
-            for chunk in range(slots.shape[0]):
-                part = source_ref[:, chunk * own : (chunk + 1) * own]
-                slots[place_ref[10] ^ chunk] = jnp.concatenate([part, fill], axis=1)
-            for slot, piece_ref in enumerate(piece_refs):
-                piece_ref[:own, :] = mine_ref[slot]
-                piece_ref[own:, :] = slots[2 * slot].astype(BF16)
-                twin_ref[slot] = slots[2 * slot + 1].astype(BF16)
-
-
-def tile_sums(place, kept, half, table, late, own, feat, extra, last, name):
+    rows = a_pair.shape[0]
+    cols = col_sums.shape[0]
+    span = scores.shape[2]
+    here = slice(half * cols, (half + 1) * cols)
+
+    def ahead(index):
+        part = slice(index * span, (index + 1) * span)
+        scores[index % 2] = jnp.dot(b_dst[here, :], a_src_t[:, part], preferred_element_type=F32)
+        outer[index % 2] = jnp.dot(b_pair[here, :], a_pair_t[:, part], preferred_element_type=F32)
+
+    def behind(index):
+        part = slice(index * span, (index + 1) * span)
+        score = scores[index % 2]
+        soft = jnp.exp(jnp.maximum(score, 0.0) - table[0:1, part])
+        grad = jnp.where(score > 0.0, soft * (outer[index % 2] - table[1:2, part]), 0.0)
+        soft_half = soft.astype(BF16)
+        grad_half = grad.astype(BF16)
+        more_cols = jnp.dot(soft_half, a_pair[part, :], preferred_element_type=F32)
+        more_target = jnp.dot(grad_half, a_src[part, :], preferred_element_type=F32)
+        more_source = jnp.dot(b_dst_t[:extra, here], grad_half, preferred_element_type=F32)
+        col_sums[...] = col_sums[...] + more_cols if index else more_cols
+        target_sums[...] = target_sums[...] + more_target if index else more_target
+        source_ref[:, part] = start_ref[:, part] + more_source if last else more_source
+
+    count = rows // span
+    ahead(0)
+    for index in range(count):
+        if index + 1 < count:
+            ahead(index + 1)
+        behind(index)
+    for slot in range(cols_ref.shape[0]):
+        chunk = slice(slot * own, (slot + 1) * own)
+        cols_ref[slot, :own, :] = col_sums[chunk, :].astype(BF16)
+        wide = jnp.concatenate([target_sums[chunk, :], jnp.zeros((pair - own, LANES), F32)], axis=0)
+        cols_ref[slot, own:, :] = jnp.transpose(wide)[:extra].astype(BF16)
+    if last:
+        fill = jnp.zeros((extra, pair - own), F32)
+        for chunk in range(slots.shape[0]):
+            part = source_ref[:, chunk * own : (chunk + 1) * own]
+            slots[place_ref[10] ^ chunk] = jnp.concatenate([part, fill], axis=1)
+        for slot, piece_ref in enumerate(piece_refs):
+            piece_ref[:own, :] = mine_ref[slot]
+            piece_ref[own:, :] = slots[2 * slot].astype(BF16)
+            twin_ref[slot] = slots[2 * slot + 1].astype(BF16)
+
+
+def tile_sums(place, kept, half, table, late, unread, own, feat, extra, name):
     rows, pair = kept[0].shape
     cols = kept[4].shape[0] // 2
     mates = rows // own
-    step = pick(cols, 2 * own, 4 * own)
-    tiles = cols // step
-    base = half * tiles
-
-    def now(i):
-        return jnp.minimum(i, tiles - 1) + base
-
-    def then(i):
-        return jnp.maximum(i - 1, 0)
-
-    scratch = [pltpu.VMEM((step, rows), F32)] * 2
+    span = pick(rows, LANES, 256)
+    scratch = [pltpu.VMEM((cols, pair), F32), pltpu.VMEM((cols, LANES), F32)] + [pltpu.VMEM((2, cols, span), F32)] * 2
     kinds = []
-    if last:
+    if half == 0:
         kinds = [((own + extra, pair), BF16)] * (mates // 2) + [((mates // 2, extra, pair), BF16)]
         scratch += [pltpu.VMEM((mates, extra, pair), F32)]
-    work = 1 << 20 if last else 2 * rows * cols * 1280
+    vmem, anywhere = pl.BlockSpec(memory_space=pltpu.VMEM), pl.BlockSpec(memory_space=pl.ANY)
+    work = 1 << 20 if half == 0 else 2 * rows * cols * 1280
     return pl.pallas_call(
-        functools.partial(tile_kernel, own, feat, last),
-        grid=(tiles + 1,),
-        in_specs=[
-            SMEM,
-            *[whole(x.shape) for x in kept[:4]],
-            pl.BlockSpec((step, pair), lambda i: (now(i), 0)),
-            pl.BlockSpec((step, LANES), lambda i: (now(i), 0)),
-            pl.BlockSpec((LANES, step), lambda i: (0, then(i) + base)),
-            *[whole(x.shape) for x in (table, *late)],
-        ],
-        out_specs=[pl.BlockSpec((step // own, own + extra, pair), lambda i: (then(i), 0, 0)), whole((extra, rows))]
-        + [whole(shape) for shape, kind in kinds],
+        functools.partial(tile_kernel, own, feat, half),
+        in_specs=[SMEM] + [vmem] * (len(kept) + 1 + len(late)) + [anywhere] * len(unread),
         out_shape=shapes(((cols // own, own + extra, pair), BF16), ((extra, rows), F32), *kinds),
         scratch_shapes=scratch,
         compiler_params=params(),
         cost_estimate=pl.CostEstimate(flops=work, bytes_accessed=1 << 20, transcendentals=work >> 11),
         name=name,
-    )(place, *kept, table, *late)
-
-
-def join_cols_kernel(own_ref, other_ref, unused_ref, out_ref):
+    )(place, *kept, table, *late, *unread)
+
+
+def join_cols_kernel(own_ref, other_ref, unread_ref, out_ref):
     out_ref[...] = (own_ref[...].astype(F32) + other_ref[...].astype(F32)).astype(BF16)
 
 
@@ -390,14 +367,14 @@
     stats = lax.all_to_all(stats, "col", 0, 0)
 
     sizes = (own, feat, extra)
-    table, mine, given = weigh(place, stats, scaled, own)
-    given = mate(given, 1)
-    other_cols, start = tile_sums(place, kept, 1, table, (), *sizes, False, "other_tile")
+    table, mine, *given = weigh(place, stats, scaled, own)
+    given = [mate(part, 1) for part in given]
+    other_cols, start = tile_sums(place, kept, 1, table, (), (), *sizes, "other_tile")
     other_cols = swap(other_cols)
-    own_cols, unused, *pieces, twin = tile_sums(place, kept, 0, table, (start, mine), *sizes, True, "own_tile")
+    own_cols, unused, *pieces, twin = tile_sums(place, kept, 0, table, (start, mine), (), *sizes, "own_tile")
     twin = mate(twin, 1)
-    (cols,) = join(join_cols_kernel, "join_cols", [own_cols], own_cols, other_cols, unread=(given,))
-    pieces = join(join_rows_kernel, "join_rows", pieces, given, twin, *pieces, unread=(cols,))
+    (cols,) = join(join_cols_kernel, "join_cols", [own_cols], own_cols, other_cols, unread=given)
+    pieces = join(join_rows_kernel, "join_rows", pieces, *given, twin, *pieces, unread=(cols,))
     cols = lax.all_to_all(cols, both, 0, 0, axis_index_groups=groups)
     pieces = [mate(piece, 2 * slot) if slot else piece for slot, piece in enumerate(pieces)]
     return tuple(finish(cols, pieces, own, feat, emb_count))

time: 91.6 us -> 90.7 us (level)
  Pallas kernels: 27.9 us -> 26.1 us
  waiting for transfers between devices: 23.2 us -> 24.2 us
    pallas_call x2, Pallas kernels: 15.9 us -> 14.1 us  [tile_sums(): pl.pallas_call(functools.partial(tile_kernel, own, feat, half), in_specs=...]
    ppermute x5, waiting for transfers between devices: 9.98 us -> 11 us  [mate(): return lax.ppermute(array, 'col', [(c, c ^ bits) for c in range(col_size)])]
  transfers between devices with their start and end apart: 19 -> 19, of which waited for: 13 -> 13; matrix products, arithmetic and copies ran while one was open for 1% -> 1% of each run, Pallas kernels for 9% -> 8%
where the time goes in v3:
time: 90.7 us; the launch traced here: 90.4 us
  starting transfers between devices  28.4 us (31%)
  Pallas kernels  26.1 us (29%)
  waiting for transfers between devices  24.2 us (27%)
  blocking collectives  9.44 us (10%)
  other arithmetic  0.93 us (1%)
    pallas_call x2, Pallas kernels, tile_sums(): pl.pallas_call(functools.partial(tile_kernel, own, feat, half), in_specs=...  14.1 us
    ppermute x5, waiting for transfers between devices, mate(): return lax.ppermute(array, 'col', [(c, c ^ bits) for c in range(col_size)])  11 us
    all_to_all x1, blocking collectives, local(): stats = lax.all_to_all(stats, 'col', 0, 0)  9.44 us
    ppermute x4, starting transfers between devices, along_z(): return lax.ppermute(array, both, pairs)  8.69 us
    pallas_call x1, Pallas kernels, row_stats(): pl.pallas_call(functools.partial(stats_kernel, own, feat), grid=(rows //...  8.69 us
    ppermute x4, waiting for transfers between devices, along_z(): return lax.ppermute(array, both, pairs)  7.68 us
    ppermute x4, starting transfers between devices, along_x(): return lax.ppermute(array, 'col', pairs)  7.46 us
    ppermute x5, starting transfers between devices, mate(): return lax.ppermute(array, 'col', [(c, c ^ bits) for c in range(col_size)])  6.59 us
  transfers between devices with their start and end apart: 19, of which 13 were waited for; matrix products, arithmetic and copies ran while one was open for 1% of the time, Pallas kernels for 8%

profile of v3, /device:TPU:0, one launch (start us, length us, event | category | flops | bytes accessed | tf_op | source)
XLA Modules:
  0.0 90.4 jit_solution(17215308984246072263)
XLA Ops:
  0.6 0.9 fusion.1
  1.5 1.7 %collective-permute-start.1 = (bf16[240,256]{1,0:T(8,128)(2,1)S(1)}, bf16[240,256]{1,0:T(8,128)(2,1)S(1)}, u32[]{:S(2)}, u32[]{:S(2)}) collective-permute-start(bf16[240,256]{1,0:T(8,128)(2,1)S(1)} %get-tuple-element.59), channel_id=1, source_target_pairs={{0,1},{1,0},{2,3},{3,2},{4,5},{5,4},{6,7},{7,6},{8,9},{9,8},{10,11... | collective-permute-start | bytes 368648 | tf_op jit(solution)/shard_map/ppermute | solution.py:344
  3.3 2.2 %collective-permute-start = (bf16[240,256]{1,0:T(8,128)(2,1)S(1)}, bf16[240,256]{1,0:T(8,128)(2,1)S(1)}, u32[]{:S(2)}, u32[]{:S(2)}) collective-permute-start(bf16[240,256]{1,0:T(8,128)(2,1)S(1)} %get-tuple-element.62), channel_id=1, source_target_pairs={{0,17},{1,16},{2,19},{3,18},{4,21},{5,20},{6,23},{7,22},{8,25},{9,... | collective-permute-start | bytes 368648 | tf_op jit(solution)/shard_map/ppermute | solution.py:351
  5.4 0.7 dynamic-slice_bitcast_fusion.place_ref
  6.1 0.4 collective-permute-done.1
  6.6 2.7 %collective-permute-done = bf16[240,256]{1,0:T(8,128)(2,1)S(1)} collective-permute-done((bf16[240,256]{1,0:T(8,128)(2,1)S(1)}, bf16[240,256]{1,0:T(8,128)(2,1)S(1)}, u32[]{:S(2)}, u32[]{:S(2)}) %collective-permute-start) | collective-permute-done | bytes 122912 | tf_op jit(solution)/shard_map/ppermute | solution.py:351
  9.4 1.6 %collective-permute-start.6 = (bf16[2,240,256]{2,1,0:T(8,128)(2,1)S(1)}, bf16[2,240,256]{2,1,0:T(8,128)(2,1)S(1)}, u32[]{:S(2)}, u32[]{:S(2)}) collective-permute-start(bf16[2,240,256]{2,1,0:T(8,128)(2,1)S(1)} %pad_maximum_fusion.1.rest_0_), channel_id=1, source_target_pairs={{0,2},{1,3},{2,4},{3,5},{4,6},{5,7},{6,0},{7,1},{8,10},{9,11},{10,... | collective-permute-start | bytes 737288 | tf_op jit(solution)/shard_map/ppermute | solution.py:344
  10.9 2.7 %collective-permute-start.4 = (bf16[2,240,256]{2,1,0:T(8,128)(2,1)S(1)}, bf16[2,240,256]{2,1,0:T(8,128)(2,1)S(1)}, u32[]{:S(2)}, u32[]{:S(2)}) collective-permute-start(bf16[2,240,256]{2,1,0:T(8,128)(2,1)S(1)} %pad_maximum_fusion.1.rest_0_), channel_id=1, source_target_pairs={{0,4},{1,5},{2,6},{3,7},{4,0},{5,1},{6,2},{7,3},{8,12},{9,13},{10,... | collective-permute-start | bytes 737288 | tf_op jit(solution)/shard_map/ppermute | solution.py:344
  13.7 1.9 %collective-permute-start.7 = (bf16[2,240,256]{2,1,0:T(8,128)(2,1)S(1)}, bf16[2,240,256]{2,1,0:T(8,128)(2,1)S(1)}, u32[]{:S(2)}, u32[]{:S(2)}) collective-permute-start(bf16[2,240,256]{2,1,0:T(8,128)(2,1)S(1)} %pad_maximum_fusion.rest_1_), channel_id=1, source_target_pairs={{0,32},{1,33},{2,34},{3,35},{4,36},{5,37},{6,38},{7,39},{8,40},{9,... | collective-permute-start | bytes 737288 | tf_op jit(solution)/shard_map/ppermute | solution.py:351
  15.6 3.6 %collective-permute-start.5 = (bf16[2,240,256]{2,1,0:T(8,128)(2,1)S(1)}, bf16[2,240,256]{2,1,0:T(8,128)(2,1)S(1)}, u32[]{:S(2)}, u32[]{:S(2)}) collective-permute-start(bf16[2,240,256]{2,1,0:T(8,128)(2,1)S(1)} %pad_maximum_fusion.rest_1_), channel_id=1, source_target_pairs={{0,64},{1,65},{2,66},{3,67},{4,68},{5,69},{6,70},{7,71},{8,72},{9,... | collective-permute-start | bytes 737288 | tf_op jit(solution)/shard_map/ppermute | solution.py:351
  19.2 1.0 %collective-permute-start.3 = (bf16[2,240,256]{2,1,0:T(8,128)(2,1)S(1)}, bf16[2,240,256]{2,1,0:T(8,128)(2,1)S(1)}, u32[]{:S(2)}, u32[]{:S(2)}) collective-permute-start(bf16[2,240,256]{2,1,0:T(8,128)(2,1)S(1)} %pad_maximum_fusion.rest_1_), channel_id=1, source_target_pairs={{0,96},{1,97},{2,98},{3,99},{4,100},{5,101},{6,102},{7,103},{8,104... | collective-permute-start | bytes 737288 | tf_op jit(solution)/shard_map/ppermute | solution.py:351
  20.2 0.0 collective-permute-done.6.rest_6_
  20.2 1.4 %collective-permute-start.2 = (bf16[2,240,256]{2,1,0:T(8,128)(2,1)S(1)}, bf16[2,240,256]{2,1,0:T(8,128)(2,1)S(1)}, u32[]{:S(2)}, u32[]{:S(2)}) collective-permute-start(bf16[2,240,256]{2,1,0:T(8,128)(2,1)S(1)} %pad_maximum_fusion.1.rest_0_), channel_id=1, source_target_pairs={{0,6},{1,7},{2,0},{3,1},{4,2},{5,3},{6,4},{7,5},{8,14},{9,15},{10,... | collective-permute-start | bytes 737288 | tf_op jit(solution)/shard_map/ppermute | solution.py:344
  21.6 1.6 %collective-permute-done.4.rest_4_ = bf16[2,240,256]{2,1,0:T(8,128)(2,1)S(1)} collective-permute-done((bf16[2,240,256]{2,1,0:T(8,128)(2,1)S(1)}, bf16[2,240,256]{2,1,0:T(8,128)(2,1)S(1)}, u32[]{:S(2)}, u32[]{:S(2)}) %collective-permute-start.4) | collective-permute-done | bytes 245792 | tf_op jit(solution)/shard_map/ppermute | solution.py:344
  23.2 0.0 collective-permute-start.8
  23.2 0.9 %collective-permute-done.7.rest_7_ = bf16[2,240,256]{2,1,0:T(8,128)(2,1)S(1)} collective-permute-done((bf16[2,240,256]{2,1,0:T(8,128)(2,1)S(1)}, bf16[2,240,256]{2,1,0:T(8,128)(2,1)S(1)}, u32[]{:S(2)}, u32[]{:S(2)}) %collective-permute-start.7) | collective-permute-done | bytes 245792 | tf_op jit(solution)/shard_map/ppermute | solution.py:351
  24.1 0.0 collective-permute-start.11
  24.1 4.0 %collective-permute-done.5.rest_5_ = bf16[2,240,256]{2,1,0:T(8,128)(2,1)S(1)} collective-permute-done((bf16[2,240,256]{2,1,0:T(8,128)(2,1)S(1)}, bf16[2,240,256]{2,1,0:T(8,128)(2,1)S(1)}, u32[]{:S(2)}, u32[]{:S(2)}) %collective-permute-start.5) | collective-permute-done | bytes 245792 | tf_op jit(solution)/shard_map/ppermute | solution.py:351
  28.1 0.0 collective-permute-start.10
  28.1 0.0 collective-permute-done.3.rest_3_
  28.1 0.5 collective-permute-start.9
  28.6 0.0 collective-permute-done.2.rest_2_
  28.6 0.0 collective-permute-done.8.rest_8_
  28.6 0.0 collective-permute-done.11.rest_11_
  28.6 1.0 %collective-permute-done.10.rest_10_ = bf16[2,240,256]{2,1,0:T(8,128)(2,1)S(1)} collective-permute-done((bf16[2,240,256]{2,1,0:T(8,128)(2,1)S(1)}, bf16[2,240,256]{2,1,0:T(8,128)(2,1)S(1)}, u32[]{:S(2)}, u32[]{:S(2)}) %collective-permute-start.10) | collective-permute-done | bytes 245792 | tf_op jit(solution)/shard_map/ppermute | solution.py:340
  29.6 0.4 collective-permute-done.9.rest_9_
  30.0 8.7 %row_stats.1 = (bf16[1536,256]{1,0:T(8,128)(2,1)S(1)}, f32[8,4,1536]{2,1,0:T(4,128)S(1)}, bf16[1536,256]{1,0:T(8,128)(2,1)S(1)}, bf16[256,1536]{1,0:T(8,128)(2,1...) custom-call(s32[16]{0:T(128)S(1)} %dynamic-slice_bitcast_fusion.plac, ...), custom_call_target="tpu_custom_call" | custom-call | flops 4831838208 | bytes 8388608 | tf_op jit(solution)/shard_map/row_stats/pallas_call | solution.py:140
  38.7 9.4 %all_to_all.10.stats_ref = f32[8,4,1536]{2,1,0:T(4,128)S(1)} all-to-all(f32[8,4,1536]{2,1,0:T(4,128)S(1)} %get-tuple-element.41), channel_id=1, replica_groups=mesh['row'=16,'col'=8] {'col'}, dimensions={0} | all-to-all | bytes 393216 | tf_op jit(solution)/shard_map/all_to_all | solution.py:367
  48.1 1.2 %weigh.1 = (f32[8,1536]{1,0:T(8,128)S(1)}, bf16[4,192,256]{2,1,0:T(8,128)(2,1)S(1)}, bf16[4,192,256]{2,1,0:T(8,128)(2,1)S(1)}) custom-call(s32[16]{0:T(128)S(1)} %dynamic-slice_bitcast_fusion.place_ref, f32[8,4,1536]{2,1,0:T(4,128)S(1)} %all_to_all.10.stats_ref, bf16[1536,256]{1,0:T(8,128)(2,1)S(1)} %get-tuple-element.42.scaled_ref), custom_call_target="tpu_custom_call" | custom-call | tf_op jit(solution)/shard_map/weigh/pallas_call | solution.py:181
  49.3 6.7 %other_tile.1 = (bf16[8,240,256]{2,1,0:T(8,128)(2,1)S(1)}, f32[48,1536]{1,0:T(8,128)S(1)}) custom-call(s32[16]{0:T(128)S(1)} %dynamic-slice_bitcast_fusion.place_ref, bf16[1536,256]{1,0:T(8,128)(2,1)S(1)} %get-tuple-element.34.a_pair, bf16[256,1536]{1,0:T(8,128)(2,1)S(1)} %get-tuple-element.35.a_pair_t, bf16[1536,128]{1,0:T(8,128)(2,1)S(1)} %get-tuple-element.36.a_src, ...), custom_call_target="tpu_custom_call" | custom-call | flops 6039797760 | bytes 1048576 | tf_op jit(solution)/shard_map/other_tile/pallas_call | solution.py:258
  56.0 0.1 collective-permute-start.12
  56.1 1.3 %collective-permute-start.13 = (bf16[4,192,256]{2,1,0:T(8,128)(2,1)S(1)}, bf16[4,192,256]{2,1,0:T(8,128)(2,1)S(1)}, u32[]{:S(2)}, u32[]{:S(2)}) collective-permute-start(bf16[4,192,256]{2,1,0:T(8,128)(2,1)S(1)} %get-tuple-element.48), channel_id=1, source_target_pairs={{0,1},{1,0},{2,3},{3,2},{4,5},{5,4},{6,7},{7,6},{8,9},{9,8},{10,11... | collective-permute-start | bytes 1179656 | tf_op jit(solution)/shard_map/ppermute | solution.py:337
  57.4 7.4 %own_tile.1 = (bf16[8,240,256]{2,1,0:T(8,128)(2,1)S(1)}, f32[48,1536]{1,0:T(8,128)}, bf16[240,256]{1,0:T(8,128)(2,1)S(1)}, bf16[240,256]{1,0:T(8,128)(2,1)S(1)},...) custom-call(s32[16]{0:T(128)S(1)} %dynamic-slice_bitcast_fusion.place_ref, ...), custom_call_target="tpu_custom_call" | custom-call | flops 1048576 | bytes 1048576 | tf_op jit(solution)/shard_map/own_tile/pallas_call | solution.py:258
  64.8 2.8 %collective-permute-done.13.unread_ref.given_ref = bf16[4,192,256]{2,1,0:T(8,128)(2,1)S(1)} collective-permute-done((bf16[4,192,256]{2,1,0:T(8,128)(2,1)S(1)}, bf16[4,192,256]{2,1,0:T(8,128)(2,1)S(1)}, u32[]{:S(2)}, u32[]{:S(2)}) %collective-permute-start.13) | collective-permute-done | bytes 393248 | tf_op jit(solution)/shard_map/ppermute | solution.py:337
  67.6 0.0 collective-permute-done.12.other_ref
  67.6 1.2 %join_cols.1.rest_4_ = bf16[8,240,256]{2,1,0:T(8,128)(2,1)} custom-call(bf16[8,240,256]{2,1,0:T(8,128)(2,1)S(1)} %get-tuple-element.46.own_ref, bf16[8,240,256]{2,1,0:T(8,128)(2,1)S(1)} %collective-permute-done.12.other_ref, bf16[4,192,256]{2,1,0:T(8,128)(2,1)S(1)} %collective-permute-done.13.unread_ref.given_ref), custom_call_target="tpu_custom_call" | custom-call | tf_op jit(solution)/shard_map/join_cols/pallas_call | solution.py:282
  68.8 5.1 %all-to-all-start.1 = ((bf16[8,240,256]{2,1,0:T(8,128)(2,1)}), bf16[8,240,256]{2,1,0:T(8,128)(2,1)S(1)}, u32[]{:S(2)}, u32[]{:S(2)}) async-start(bf16[8,240,256]{2,1,0:T(8,128)(2,1)} %join_cols.1.rest_4_), calls=%async_computation.1 | async-start | bytes 1966080 | tf_op jit(solution)/shard_map/all_to_all | solution.py:378
  73.9 0.5 collective-permute-start.14
  74.4 4.1 %collective-permute-done.14.twin_ref = bf16[4,48,256]{2,1,0:T(8,128)(2,1)S(1)} collective-permute-done((bf16[4,48,256]{2,1,0:T(8,128)(2,1)S(1)}, bf16[4,48,256]{2,1,0:T(8,128)(2,1)S(1)}, u32[]{:S(2)}, u32[]{:S(2)}) %collective-permute-start.14) | collective-permute-done | bytes 98336 | tf_op jit(solution)/shard_map/ppermute | solution.py:337
  78.5 0.1 join_rows.1
  78.6 0.6 collective-permute-start.15
  79.3 2.1 %collective-permute-start.16 = (bf16[240,256]{1,0:T(8,128)(2,1)S(1)}, bf16[240,256]{1,0:T(8,128)(2,1)S(1)}, u32[]{:S(2)}, u32[]{:S(2)}) collective-permute-start(bf16[240,256]{1,0:T(8,128)(2,1)S(1)} %get-tuple-element.56), channel_id=1, source_target_pairs={{0,4},{1,5},{2,6},{3,7},{4,0},{5,1},{6,2},{7,3},{8,12},{9,13},{10,... | collective-permute-start | bytes 368648 | tf_op jit(solution)/shard_map/ppermute | solution.py:337
  81.3 2.1 %collective-permute-start.17 = (bf16[240,256]{1,0:T(8,128)(2,1)S(1)}, bf16[240,256]{1,0:T(8,128)(2,1)S(1)}, u32[]{:S(2)}, u32[]{:S(2)}) collective-permute-start(bf16[240,256]{1,0:T(8,128)(2,1)S(1)} %get-tuple-element.57), channel_id=1, source_target_pairs={{0,6},{1,7},{2,4},{3,5},{4,2},{5,3},{6,0},{7,1},{8,14},{9,15},{10,... | collective-permute-start | bytes 368648 | tf_op jit(solution)/shard_map/ppermute | solution.py:337
  83.4 0.2 collective-permute-done.15.rest_1_
  83.6 2.1 %collective-permute-done.16.rest_2_ = bf16[240,256]{1,0:T(8,128)(2,1)S(1)} collective-permute-done((bf16[240,256]{1,0:T(8,128)(2,1)S(1)}, bf16[240,256]{1,0:T(8,128)(2,1)S(1)}, u32[]{:S(2)}, u32[]{:S(2)}) %collective-permute-start.16) | collective-permute-done | bytes 122912 | tf_op jit(solution)/shard_map/ppermute | solution.py:337
  85.6 1.8 %collective-permute-done.17.rest_3_ = bf16[240,256]{1,0:T(8,128)(2,1)S(1)} collective-permute-done((bf16[240,256]{1,0:T(8,128)(2,1)S(1)}, bf16[240,256]{1,0:T(8,128)(2,1)S(1)}, u32[]{:S(2)}, u32[]{:S(2)}) %collective-permute-start.17) | collective-permute-done | bytes 122912 | tf_op jit(solution)/shard_map/ppermute | solution.py:337
  87.4 2.2 %all-to-all-done.1.cols_ref = bf16[8,240,256]{2,1,0:T(8,128)(2,1)S(1)} async-done(((bf16[8,240,256]{2,1,0:T(8,128)(2,1)}), bf16[8,240,256]{2,1,0:T(8,128)(2,1)S(1)}, u32[]{:S(2)}, u32[]{:S(2)}) %all-to-all-start.1) | async-done | bytes 983072 | tf_op jit(solution)/shard_map/all_to_all | solution.py:378
  89.6 0.8 finish.1
  (2 shorter events, 0.1 us)
Async XLA Ops:
  1.5 5.1 %collective-permute-start.1 = (bf16[240,256]{1,0:T(8,128)(2,1)S(1)}, bf16[240,256]{1,0:T(8,128)(2,1)S(1)}, u32[]{:S(2)}, u32[]{:S(2)}) collective-permute-start(bf16[240,256]{1,0:T(8,128)(2,1)S(1)} %get-tuple-element.59), channel_id=1, source_target_pairs={{0,1},{1,0},{2,3},{3,2},{4,5},{5,4},{6,7},{7,6},{8,9},{9,8},{10,11... | collective-permute-start | bytes 368648 | tf_op jit(solution)/shard_map/ppermute | solution.py:344
  3.3 6.1 %collective-permute-start = (bf16[240,256]{1,0:T(8,128)(2,1)S(1)}, bf16[240,256]{1,0:T(8,128)(2,1)S(1)}, u32[]{:S(2)}, u32[]{:S(2)}) collective-permute-start(bf16[240,256]{1,0:T(8,128)(2,1)S(1)} %get-tuple-element.62), channel_id=1, source_target_pairs={{0,17},{1,16},{2,19},{3,18},{4,21},{5,20},{6,23},{7,22},{8,25},{9,... | collective-permute-start | bytes 368648 | tf_op jit(solution)/shard_map/ppermute | solution.py:351
  9.4 10.8 %collective-permute-start.6 = (bf16[2,240,256]{2,1,0:T(8,128)(2,1)S(1)}, bf16[2,240,256]{2,1,0:T(8,128)(2,1)S(1)}, u32[]{:S(2)}, u32[]{:S(2)}) collective-permute-start(bf16[2,240,256]{2,1,0:T(8,128)(2,1)S(1)} %pad_maximum_fusion.1.rest_0_), channel_id=1, source_target_pairs={{0,2},{1,3},{2,4},{3,5},{4,6},{5,7},{6,0},{7,1},{8,10},{9,11},{10,... | collective-permute-start | bytes 737288 | tf_op jit(solution)/shard_map/ppermute | solution.py:344
  10.9 12.2 %collective-permute-start.4 = (bf16[2,240,256]{2,1,0:T(8,128)(2,1)S(1)}, bf16[2,240,256]{2,1,0:T(8,128)(2,1)S(1)}, u32[]{:S(2)}, u32[]{:S(2)}) collective-permute-start(bf16[2,240,256]{2,1,0:T(8,128)(2,1)S(1)} %pad_maximum_fusion.1.rest_0_), channel_id=1, source_target_pairs={{0,4},{1,5},{2,6},{3,7},{4,0},{5,1},{6,2},{7,3},{8,12},{9,13},{10,... | collective-permute-start | bytes 737288 | tf_op jit(solution)/shard_map/ppermute | solution.py:344
  13.7 10.4 %collective-permute-start.7 = (bf16[2,240,256]{2,1,0:T(8,128)(2,1)S(1)}, bf16[2,240,256]{2,1,0:T(8,128)(2,1)S(1)}, u32[]{:S(2)}, u32[]{:S(2)}) collective-permute-start(bf16[2,240,256]{2,1,0:T(8,128)(2,1)S(1)} %pad_maximum_fusion.rest_1_), channel_id=1, source_target_pairs={{0,32},{1,33},{2,34},{3,35},{4,36},{5,37},{6,38},{7,39},{8,40},{9,... | collective-permute-start | bytes 737288 | tf_op jit(solution)/shard_map/ppermute | solution.py:351
  15.6 12.5 %collective-permute-start.5 = (bf16[2,240,256]{2,1,0:T(8,128)(2,1)S(1)}, bf16[2,240,256]{2,1,0:T(8,128)(2,1)S(1)}, u32[]{:S(2)}, u32[]{:S(2)}) collective-permute-start(bf16[2,240,256]{2,1,0:T(8,128)(2,1)S(1)} %pad_maximum_fusion.rest_1_), channel_id=1, source_target_pairs={{0,64},{1,65},{2,66},{3,67},{4,68},{5,69},{6,70},{7,71},{8,72},{9,... | collective-permute-start | bytes 737288 | tf_op jit(solution)/shard_map/ppermute | solution.py:351
  19.2 9.0 %collective-permute-start.3 = (bf16[2,240,256]{2,1,0:T(8,128)(2,1)S(1)}, bf16[2,240,256]{2,1,0:T(8,128)(2,1)S(1)}, u32[]{:S(2)}, u32[]{:S(2)}) collective-permute-start(bf16[2,240,256]{2,1,0:T(8,128)(2,1)S(1)} %pad_maximum_fusion.rest_1_), channel_id=1, source_target_pairs={{0,96},{1,97},{2,98},{3,99},{4,100},{5,101},{6,102},{7,103},{8,104... | collective-permute-start | bytes 737288 | tf_op jit(solution)/shard_map/ppermute | solution.py:351
  20.2 8.5 %collective-permute-start.2 = (bf16[2,240,256]{2,1,0:T(8,128)(2,1)S(1)}, bf16[2,240,256]{2,1,0:T(8,128)(2,1)S(1)}, u32[]{:S(2)}, u32[]{:S(2)}) collective-permute-start(bf16[2,240,256]{2,1,0:T(8,128)(2,1)S(1)} %pad_maximum_fusion.1.rest_0_), channel_id=1, source_target_pairs={{0,6},{1,7},{2,0},{3,1},{4,2},{5,3},{6,4},{7,5},{8,14},{9,15},{10,... | collective-permute-start | bytes 737288 | tf_op jit(solution)/shard_map/ppermute | solution.py:344
  23.2 5.5 %collective-permute-start.8 = (bf16[2,240,256]{2,1,0:T(8,128)(2,1)S(1)}, bf16[2,240,256]{2,1,0:T(8,128)(2,1)S(1)}, u32[]{:S(2)}, u32[]{:S(2)}) collective-permute-start(bf16[2,240,256]{2,1,0:T(8,128)(2,1)S(1)} %pad_maximum_fusion.rest_1_), channel_id=1, source_target_pairs={{0,8},{8,0},{16,24},{24,16},{32,40},{40,32},{48,56},{56,48},{64,72... | collective-permute-start | bytes 737288 | tf_op jit(solution)/shard_map/ppermute | solution.py:340
  24.1 4.5 %collective-permute-start.11 = (bf16[2,240,256]{2,1,0:T(8,128)(2,1)S(1)}, bf16[2,240,256]{2,1,0:T(8,128)(2,1)S(1)}, u32[]{:S(2)}, u32[]{:S(2)}) collective-permute-start(bf16[2,240,256]{2,1,0:T(8,128)(2,1)S(1)} %collective-permute-done.7.rest_7_), channel_id=1, source_target_pairs={{0,8},{8,0},{16,24},{24,16},{32,40},{40,32},{48,56},{56,48},{64,72... | collective-permute-start | bytes 737288 | tf_op jit(solution)/shard_map/ppermute | solution.py:340
  28.1 1.5 %collective-permute-start.10 = (bf16[2,240,256]{2,1,0:T(8,128)(2,1)S(1)}, bf16[2,240,256]{2,1,0:T(8,128)(2,1)S(1)}, u32[]{:S(2)}, u32[]{:S(2)}) collective-permute-start(bf16[2,240,256]{2,1,0:T(8,128)(2,1)S(1)} %collective-permute-done.5.rest_5_), channel_id=1, source_target_pairs={{0,8},{8,0},{16,24},{24,16},{32,40},{40,32},{48,56},{56,48},{64,72... | collective-permute-start | bytes 737288 | tf_op jit(solution)/shard_map/ppermute | solution.py:340
  28.1 1.9 %collective-permute-start.9 = (bf16[2,240,256]{2,1,0:T(8,128)(2,1)S(1)}, bf16[2,240,256]{2,1,0:T(8,128)(2,1)S(1)}, u32[]{:S(2)}, u32[]{:S(2)}) collective-permute-start(bf16[2,240,256]{2,1,0:T(8,128)(2,1)S(1)} %collective-permute-done.3.rest_3_), channel_id=1, source_target_pairs={{0,8},{8,0},{16,24},{24,16},{32,40},{40,32},{48,56},{56,48},{64,72... | collective-permute-start | bytes 737288 | tf_op jit(solution)/shard_map/ppermute | solution.py:340
  56.0 11.6 %collective-permute-start.12 = (bf16[8,240,256]{2,1,0:T(8,128)(2,1)S(1)}, bf16[8,240,256]{2,1,0:T(8,128)(2,1)S(1)}, u32[]{:S(2)}, u32[]{:S(2)}) collective-permute-start(bf16[8,240,256]{2,1,0:T(8,128)(2,1)S(1)} %get-tuple-element.47), channel_id=1, source_target_pairs={{0,8},{8,0},{16,24},{24,16},{32,40},{40,32},{48,56},{56,48},{64,72... | collective-permute-start | bytes 2949128 | tf_op jit(solution)/shard_map/ppermute | solution.py:340
  56.1 11.5 %collective-permute-start.13 = (bf16[4,192,256]{2,1,0:T(8,128)(2,1)S(1)}, bf16[4,192,256]{2,1,0:T(8,128)(2,1)S(1)}, u32[]{:S(2)}, u32[]{:S(2)}) collective-permute-start(bf16[4,192,256]{2,1,0:T(8,128)(2,1)S(1)} %get-tuple-element.48), channel_id=1, source_target_pairs={{0,1},{1,0},{2,3},{3,2},{4,5},{5,4},{6,7},{7,6},{8,9},{9,8},{10,11... | collective-permute-start | bytes 1179656 | tf_op jit(solution)/shard_map/ppermute | solution.py:337
  68.8 20.8 %all-to-all-start.1 = ((bf16[8,240,256]{2,1,0:T(8,128)(2,1)}), bf16[8,240,256]{2,1,0:T(8,128)(2,1)S(1)}, u32[]{:S(2)}, u32[]{:S(2)}) async-start(bf16[8,240,256]{2,1,0:T(8,128)(2,1)} %join_cols.1.rest_4_), calls=%async_computation.1 | async-start | bytes 1966080 | tf_op jit(solution)/shard_map/all_to_all | solution.py:378
  73.9 4.6 %collective-permute-start.14 = (bf16[4,48,256]{2,1,0:T(8,128)(2,1)S(1)}, bf16[4,48,256]{2,1,0:T(8,128)(2,1)S(1)}, u32[]{:S(2)}, u32[]{:S(2)}) collective-permute-start(bf16[4,48,256]{2,1,0:T(8,128)(2,1)S(1)} %get-tuple-element.49), channel_id=1, source_target_pairs={{0,1},{1,0},{2,3},{3,2},{4,5},{5,4},{6,7},{7,6},{8,9},{9,8},{10,11... | collective-permute-start | bytes 294920 | tf_op jit(solution)/shard_map/ppermute | solution.py:337
  78.6 5.0 %collective-permute-start.15 = (bf16[240,256]{1,0:T(8,128)(2,1)S(1)}, bf16[240,256]{1,0:T(8,128)(2,1)S(1)}, u32[]{:S(2)}, u32[]{:S(2)}) collective-permute-start(bf16[240,256]{1,0:T(8,128)(2,1)S(1)} %get-tuple-element.55), channel_id=1, source_target_pairs={{0,2},{1,3},{2,0},{3,1},{4,6},{5,7},{6,4},{7,5},{8,10},{9,11},{10,... | collective-permute-start | bytes 368648 | tf_op jit(solution)/shard_map/ppermute | solution.py:337
  79.3 6.4 %collective-permute-start.16 = (bf16[240,256]{1,0:T(8,128)(2,1)S(1)}, bf16[240,256]{1,0:T(8,128)(2,1)S(1)}, u32[]{:S(2)}, u32[]{:S(2)}) collective-permute-start(bf16[240,256]{1,0:T(8,128)(2,1)S(1)} %get-tuple-element.56), channel_id=1, source_target_pairs={{0,4},{1,5},{2,6},{3,7},{4,0},{5,1},{6,2},{7,3},{8,12},{9,13},{10,... | collective-permute-start | bytes 368648 | tf_op jit(solution)/shard_map/ppermute | solution.py:337
  81.3 6.1 %collective-permute-start.17 = (bf16[240,256]{1,0:T(8,128)(2,1)S(1)}, bf16[240,256]{1,0:T(8,128)(2,1)S(1)}, u32[]{:S(2)}, u32[]{:S(2)}) collective-permute-start(bf16[240,256]{1,0:T(8,128)(2,1)S(1)} %get-tuple-element.57), channel_id=1, source_target_pairs={{0,6},{1,7},{2,4},{3,5},{4,2},{5,3},{6,0},{7,1},{8,14},{9,15},{10,... | collective-permute-start | bytes 368648 | tf_op jit(solution)/shard_map/ppermute | solution.py:337

commit v4 on v3

--- a/solution.py
+++ b/solution.py
@@ -64,10 +64,30 @@
     nodes_ref[...] = jnp.transpose(turned_ref[...])
 
 
-def stats_kernel(own, feat, place_ref, *rest):
+def rows_kernel(own, feat, place_ref, *rest):
+    a_refs, (a_pair, a_pair_t, a_src, a_src_t) = rest[: len(MOVES)], rest[len(MOVES) :]
+    assemble(own, a_refs, place_ref, 0, place_ref[8], a_pair, a_src_t, a_src)
+    a_pair_t[:feat] = jnp.transpose(a_pair[:, feat:])
+    a_pair_t[feat:] = jnp.transpose(a_pair[:, :feat])
+
+
+def row_arrays(place, a_parts, own, feat):
+    rows = own * sum(part.shape[0] for part in a_parts)
+    pair = 2 * feat
+    return pl.pallas_call(
+        functools.partial(rows_kernel, own, feat),
+        in_specs=[SMEM] + [pl.BlockSpec(memory_space=pltpu.VMEM)] * len(a_parts),
+        out_shape=shapes(((rows, pair), BF16), ((pair, rows), BF16), ((rows, LANES), BF16), ((LANES, rows), BF16)),
+        compiler_params=params(8),
+        cost_estimate=pl.CostEstimate(flops=1 << 30, bytes_accessed=1 << 20, transcendentals=0),
+        name="row_arrays",
+    )(place, *a_parts)
+
+
+def stats_kernel(own, feat, place_ref, a_pair, a_src, *rest):
     parts = len(MOVES)
-    a_refs, b0_refs, b1_refs = rest[0 : 2 * parts : 2], rest[1 : 2 * parts : 2], rest[2 * parts : 3 * parts]
-    scaled_ref, stats_ref, a_pair, a_pair_t, a_src, a_src_t, b_pair, b_dst, b_dst_t, scores, peaks = rest[3 * parts :]
+    b0_refs, b1_refs = rest[:parts], rest[parts : 2 * parts]
+    scaled_ref, stats_ref, b_pair, b_dst, b_dst_t, scores, peaks = rest[2 * parts :]
     step = pl.program_id(0)
     last = pl.num_programs(0) - 1
     count, cols = scores.shape
@@ -109,14 +129,11 @@
 
     @pl.when(step == 0)
     def _():
-        assemble(own, a_refs, place_ref, 0, place_ref[8], a_pair, a_src_t, a_src)
         half = b_pair.shape[0] // 2
         for index, b_refs in enumerate((b0_refs, b1_refs)):
             part = pl.ds(index * half, half)
             outs = (b_pair.at[part, :], b_dst_t.at[:, part], b_dst.at[part, :])
             assemble(own, b_refs, place_ref, 4, place_ref[9], *outs)
-        a_pair_t[:feat] = jnp.transpose(a_pair[:, feat:])
-        a_pair_t[feat:] = jnp.transpose(a_pair[:, :feat])
         work(True, False)
 
     @pl.when((step > 0) & (step < last))
@@ -128,15 +145,14 @@
         work(False, True)
 
 
-def row_stats(place, a_parts, b0_parts, b1_parts, own, feat):
-    mates = sum(part.shape[0] for part in a_parts)
-    rows = mates * own
+def row_stats(place, a_kept, b0_parts, b1_parts, own, feat):
+    rows = a_kept[0].shape[0]
+    mates = rows // own
     cols = 2 * own * sum(part.shape[0] for part in b0_parts)
     pair = 2 * feat
     step = pick(rows, LANES, 512)
-    kept = [((rows, pair), BF16), ((pair, rows), BF16), ((rows, LANES), BF16), ((LANES, rows), BF16)]
-    kept += [((cols, pair), BF16), ((cols, LANES), BF16), ((LANES, cols), BF16)]
-    parts = [part for both in zip(a_parts, b0_parts) for part in both] + b1_parts
+    kept = [((cols, pair), BF16), ((cols, LANES), BF16), ((LANES, cols), BF16)]
+    parts = (a_kept[0], a_kept[2], *b0_parts, *b1_parts)
     scaled, stats, *kept = pl.pallas_call(
         functools.partial(stats_kernel, own, feat),
         grid=(rows // step + 1,),
@@ -152,7 +168,7 @@
         cost_estimate=pl.CostEstimate(flops=2 * rows * cols * 512, bytes_accessed=8 << 20, transcendentals=rows * cols),
         name="row_stats",
     )(place, *parts)
-    return scaled, stats, kept
+    return scaled, stats, [*a_kept, *kept]
 
 
 def weigh_kernel(own, place_ref, stats_ref, scaled_ref, table_ref, mine_ref, given_ref, weights_ref):
@@ -363,7 +379,8 @@
     moved = [[along(array, -move, 0) for array, along in zip(near, alongs)] for move in MOVES[1:]]
     b_parts, a_parts = [[array, *[pair[index] for pair in moved]] for index, array in enumerate(near)]
     others = [swap(part) for part in b_parts]
-    scaled, stats, kept = row_stats(place, a_parts, b_parts, others, own, feat)
+    a_kept = row_arrays(place, a_parts, own, feat)
+    scaled, stats, kept = row_stats(place, a_kept, b_parts, others, own, feat)
     stats = lax.all_to_all(stats, "col", 0, 0)
 
     sizes = (own, feat, extra)

time: 90.7 us -> 90.8 us (level)
    ppermute x5, waiting for transfers between devices: 1.34 us -> 0.31 us  [swap(): return lax.ppermute(array, 'row', [(r, r ^ 1) for r in range(row_size)])]
    pallas_call x0 -> x1, Pallas kernels: none -> 1.01 us  [row_arrays(): pl.pallas_call(functools.partial(rows_kernel, own, feat), in_specs=[SMEM]...]
  transfers between devices with their start and end apart: 19 -> 19, of which waited for: 13 -> 12; matrix products, arithmetic and copies ran while one was open for 1% -> 1% of each run, Pallas kernels for 8% -> 9%
where the time goes in v4:
time: 90.8 us; the launch traced here: 90.6 us
  starting transfers between devices  28.5 us (31%)
  Pallas kernels  26.8 us (30%)
  waiting for transfers between devices  23.4 us (26%)
  blocking collectives  9.44 us (10%)
  other arithmetic  0.93 us (1%)
    pallas_call x2, Pallas kernels, tile_sums(): pl.pallas_call(functools.partial(tile_kernel, own, feat, half), in_specs=...  14.1 us
    ppermute x5, waiting for transfers between devices, mate(): return lax.ppermute(array, 'col', [(c, c ^ bits) for c in range(col_size)])  11.2 us
    all_to_all x1, blocking collectives, local(): stats = lax.all_to_all(stats, 'col', 0, 0)  9.44 us
    ppermute x4, starting transfers between devices, along_z(): return lax.ppermute(array, both, pairs)  8.69 us
    pallas_call x1, Pallas kernels, row_stats(): pl.pallas_call(functools.partial(stats_kernel, own, feat), grid=(rows //...  8.44 us
    ppermute x4, waiting for transfers between devices, along_z(): return lax.ppermute(array, both, pairs)  7.68 us
    ppermute x4, starting transfers between devices, along_x(): return lax.ppermute(array, 'col', pairs)  7.46 us
    ppermute x5, starting transfers between devices, mate(): return lax.ppermute(array, 'col', [(c, c ^ bits) for c in range(col_size)])  6.36 us
  transfers between devices with their start and end apart: 19, of which 12 were waited for; matrix products, arithmetic and copies ran while one was open for 1% of the time, Pallas kernels for 9%

profile of v4, /device:TPU:0, one launch (start us, length us, event | category | flops | bytes accessed | tf_op | source)
XLA Modules:
  0.0 90.6 jit_solution(2314828347942114166)
XLA Ops:
  0.6 0.9 fusion.1
  1.5 1.7 %collective-permute-start.1 = (bf16[240,256]{1,0:T(8,128)(2,1)S(1)}, bf16[240,256]{1,0:T(8,128)(2,1)S(1)}, u32[]{:S(2)}, u32[]{:S(2)}) collective-permute-start(bf16[240,256]{1,0:T(8,128)(2,1)S(1)} %get-tuple-element.59), channel_id=1, source_target_pairs={{0,1},{1,0},{2,3},{3,2},{4,5},{5,4},{6,7},{7,6},{8,9},{9,8},{10,11... | collective-permute-start | bytes 368648 | tf_op jit(solution)/shard_map/ppermute | solution.py:360
  3.3 2.2 %collective-permute-start = (bf16[240,256]{1,0:T(8,128)(2,1)S(1)}, bf16[240,256]{1,0:T(8,128)(2,1)S(1)}, u32[]{:S(2)}, u32[]{:S(2)}) collective-permute-start(bf16[240,256]{1,0:T(8,128)(2,1)S(1)} %get-tuple-element.62), channel_id=1, source_target_pairs={{0,17},{1,16},{2,19},{3,18},{4,21},{5,20},{6,23},{7,22},{8,25},{9,... | collective-permute-start | bytes 368648 | tf_op jit(solution)/shard_map/ppermute | solution.py:367
  5.4 0.7 dynamic-slice_bitcast_fusion.place_ref
  6.1 0.4 collective-permute-done.1
  6.6 2.7 %collective-permute-done = bf16[240,256]{1,0:T(8,128)(2,1)S(1)} collective-permute-done((bf16[240,256]{1,0:T(8,128)(2,1)S(1)}, bf16[240,256]{1,0:T(8,128)(2,1)S(1)}, u32[]{:S(2)}, u32[]{:S(2)}) %collective-permute-start) | collective-permute-done | bytes 122912 | tf_op jit(solution)/shard_map/ppermute | solution.py:367
  9.4 1.6 %collective-permute-start.4 = (bf16[2,240,256]{2,1,0:T(8,128)(2,1)S(1)}, bf16[2,240,256]{2,1,0:T(8,128)(2,1)S(1)}, u32[]{:S(2)}, u32[]{:S(2)}) collective-permute-start(bf16[2,240,256]{2,1,0:T(8,128)(2,1)S(1)} %pad_maximum_fusion.1.rest_0_), channel_id=1, source_target_pairs={{0,2},{1,3},{2,4},{3,5},{4,6},{5,7},{6,0},{7,1},{8,10},{9,11},{10,... | collective-permute-start | bytes 737288 | tf_op jit(solution)/shard_map/ppermute | solution.py:360
  10.9 2.7 %collective-permute-start.3 = (bf16[2,240,256]{2,1,0:T(8,128)(2,1)S(1)}, bf16[2,240,256]{2,1,0:T(8,128)(2,1)S(1)}, u32[]{:S(2)}, u32[]{:S(2)}) collective-permute-start(bf16[2,240,256]{2,1,0:T(8,128)(2,1)S(1)} %pad_maximum_fusion.1.rest_0_), channel_id=1, source_target_pairs={{0,4},{1,5},{2,6},{3,7},{4,0},{5,1},{6,2},{7,3},{8,12},{9,13},{10,... | collective-permute-start | bytes 737288 | tf_op jit(solution)/shard_map/ppermute | solution.py:360
  13.7 1.9 %collective-permute-start.7 = (bf16[2,240,256]{2,1,0:T(8,128)(2,1)S(1)}, bf16[2,240,256]{2,1,0:T(8,128)(2,1)S(1)}, u32[]{:S(2)}, u32[]{:S(2)}) collective-permute-start(bf16[2,240,256]{2,1,0:T(8,128)(2,1)S(1)} %pad_maximum_fusion.rest_0_), channel_id=1, source_target_pairs={{0,32},{1,33},{2,34},{3,35},{4,36},{5,37},{6,38},{7,39},{8,40},{9,... | collective-permute-start | bytes 737288 | tf_op jit(solution)/shard_map/ppermute | solution.py:367
  15.6 3.6 %collective-permute-start.6 = (bf16[2,240,256]{2,1,0:T(8,128)(2,1)S(1)}, bf16[2,240,256]{2,1,0:T(8,128)(2,1)S(1)}, u32[]{:S(2)}, u32[]{:S(2)}) collective-permute-start(bf16[2,240,256]{2,1,0:T(8,128)(2,1)S(1)} %pad_maximum_fusion.rest_0_), channel_id=1, source_target_pairs={{0,64},{1,65},{2,66},{3,67},{4,68},{5,69},{6,70},{7,71},{8,72},{9,... | collective-permute-start | bytes 737288 | tf_op jit(solution)/shard_map/ppermute | solution.py:367
  19.2 1.0 %collective-permute-start.5 = (bf16[2,240,256]{2,1,0:T(8,128)(2,1)S(1)}, bf16[2,240,256]{2,1,0:T(8,128)(2,1)S(1)}, u32[]{:S(2)}, u32[]{:S(2)}) collective-permute-start(bf16[2,240,256]{2,1,0:T(8,128)(2,1)S(1)} %pad_maximum_fusion.rest_0_), channel_id=1, source_target_pairs={{0,96},{1,97},{2,98},{3,99},{4,100},{5,101},{6,102},{7,103},{8,104... | collective-permute-start | bytes 737288 | tf_op jit(solution)/shard_map/ppermute | solution.py:367
  20.2 0.0 collective-permute-done.4.rest_3_
  20.2 1.4 %collective-permute-start.2 = (bf16[2,240,256]{2,1,0:T(8,128)(2,1)S(1)}, bf16[2,240,256]{2,1,0:T(8,128)(2,1)S(1)}, u32[]{:S(2)}, u32[]{:S(2)}) collective-permute-start(bf16[2,240,256]{2,1,0:T(8,128)(2,1)S(1)} %pad_maximum_fusion.1.rest_0_), channel_id=1, source_target_pairs={{0,6},{1,7},{2,0},{3,1},{4,2},{5,3},{6,4},{7,5},{8,14},{9,15},{10,... | collective-permute-start | bytes 737288 | tf_op jit(solution)/shard_map/ppermute | solution.py:360
  21.6 1.6 %collective-permute-done.3.rest_2_ = bf16[2,240,256]{2,1,0:T(8,128)(2,1)S(1)} collective-permute-done((bf16[2,240,256]{2,1,0:T(8,128)(2,1)S(1)}, bf16[2,240,256]{2,1,0:T(8,128)(2,1)S(1)}, u32[]{:S(2)}, u32[]{:S(2)}) %collective-permute-start.3) | collective-permute-done | bytes 245792 | tf_op jit(solution)/shard_map/ppermute | solution.py:360
  23.2 0.0 collective-permute-start.8
  23.2 0.9 %collective-permute-done.7.rest_3_ = bf16[2,240,256]{2,1,0:T(8,128)(2,1)S(1)} collective-permute-done((bf16[2,240,256]{2,1,0:T(8,128)(2,1)S(1)}, bf16[2,240,256]{2,1,0:T(8,128)(2,1)S(1)}, u32[]{:S(2)}, u32[]{:S(2)}) %collective-permute-start.7) | collective-permute-done | bytes 245792 | tf_op jit(solution)/shard_map/ppermute | solution.py:367
  24.1 0.0 collective-permute-start.11
  24.1 4.0 %collective-permute-done.6.rest_2_ = bf16[2,240,256]{2,1,0:T(8,128)(2,1)S(1)} collective-permute-done((bf16[2,240,256]{2,1,0:T(8,128)(2,1)S(1)}, bf16[2,240,256]{2,1,0:T(8,128)(2,1)S(1)}, u32[]{:S(2)}, u32[]{:S(2)}) %collective-permute-start.6) | collective-permute-done | bytes 245792 | tf_op jit(solution)/shard_map/ppermute | solution.py:367
  28.1 0.0 collective-permute-start.10
  28.1 0.0 collective-permute-done.5.rest_1_
  28.1 0.5 collective-permute-start.9
  28.6 0.0 collective-permute-done.2.rest_1_
  28.6 1.0 %row_arrays.1 = (bf16[1536,256]{1,0:T(8,128)(2,1)S(1)}, bf16[256,1536]{1,0:T(8,128)(2,1)S(1)}, bf16[1536,128]{1,0:T(8,128)(2,1)S(1)}, bf16[128,1536]{1,0:T(8,128)(2,1)S(1)}) custom-call(s32[16]{0:T(128)S(1)} %dynamic-slice_bitcast_fusion.place_ref, bf16[2,240,256]{2,1,0:T(8,128)(2,1)S(1)} %pad_maximum_fusion.1.rest_0_, ...), custom_call_target="tpu_custom_call" | custom-call | flops 1073741824 | bytes 1048576 | tf_op jit(solution)/shard_map/row_arrays/pallas_call | solution.py:77
  29.7 0.0 collective-permute-done.11.rest_7_
  29.7 0.0 collective-permute-done.10.rest_6_
  29.7 0.3 collective-permute-done.9.rest_5_
  30.0 8.4 %row_stats.1 = (bf16[1536,256]{1,0:T(8,128)(2,1)S(1)}, f32[8,4,1536]{2,1,0:T(4,128)S(1)}, bf16[3072,256]{1,0:T(8,128)(2,1)S(1)}, bf16[3072,128]{1,0:T(8,128)(2,1)S(1)}, bf16[128,3072]{1,0:T(8,128)(2,1)S(1)}) custom-call(s32[16]{0:T(128)S(1)} %dynamic-slice_bitcast_fusion.place_ref, bf16[1536,256]{1,0:T(8,128)(2,1)S(1)} %get-tuple-element.33.a_pair, ...), custom_call_target="tpu_custom_call" | custom-call | flops 4831838208 | bytes 8388608 | tf_op jit(solution)/shard_map/row_stats/pallas_call | solution.py:156
  38.4 9.4 %all_to_all.10.stats_ref = f32[8,4,1536]{2,1,0:T(4,128)S(1)} all-to-all(f32[8,4,1536]{2,1,0:T(4,128)S(1)} %get-tuple-element.41), channel_id=1, replica_groups=mesh['row'=16,'col'=8] {'col'}, dimensions={0} | all-to-all | bytes 393216 | tf_op jit(solution)/shard_map/all_to_all | solution.py:384
  47.9 1.2 %weigh.1 = (f32[8,1536]{1,0:T(8,128)S(1)}, bf16[4,192,256]{2,1,0:T(8,128)(2,1)S(1)}, bf16[4,192,256]{2,1,0:T(8,128)(2,1)S(1)}) custom-call(s32[16]{0:T(128)S(1)} %dynamic-slice_bitcast_fusion.place_ref, f32[8,4,1536]{2,1,0:T(4,128)S(1)} %all_to_all.10.stats_ref, bf16[1536,256]{1,0:T(8,128)(2,1)S(1)} %get-tuple-element.42.scaled_ref), custom_call_target="tpu_custom_call" | custom-call | tf_op jit(solution)/shard_map/weigh/pallas_call | solution.py:197
  49.1 6.7 %other_tile.1 = (bf16[8,240,256]{2,1,0:T(8,128)(2,1)S(1)}, f32[48,1536]{1,0:T(8,128)S(1)}) custom-call(s32[16]{0:T(128)S(1)} %dynamic-slice_bitcast_fusion.place_ref, bf16[1536,256]{1,0:T(8,128)(2,1)S(1)} %get-tuple-element.33.a_pair, bf16[256,1536]{1,0:T(8,128)(2,1)S(1)} %get-tuple-element.34.a_pair_t, bf16[1536,128]{1,0:T(8,128)(2,1)S(1)} %get-tuple-element.35.a_src, ...), custom_call_target="tpu_custom_call" | custom-call | flops 6039797760 | bytes 1048576 | tf_op jit(solution)/shard_map/other_tile/pallas_call | solution.py:274
  55.8 0.1 collective-permute-start.12
  55.8 1.3 %collective-permute-start.13 = (bf16[4,192,256]{2,1,0:T(8,128)(2,1)S(1)}, bf16[4,192,256]{2,1,0:T(8,128)(2,1)S(1)}, u32[]{:S(2)}, u32[]{:S(2)}) collective-permute-start(bf16[4,192,256]{2,1,0:T(8,128)(2,1)S(1)} %get-tuple-element.48), channel_id=1, source_target_pairs={{0,1},{1,0},{2,3},{3,2},{4,5},{5,4},{6,7},{7,6},{8,9},{9,8},{10,11... | collective-permute-start | bytes 1179656 | tf_op jit(solution)/shard_map/ppermute | solution.py:353
  57.1 7.4 %own_tile.1 = (bf16[8,240,256]{2,1,0:T(8,128)(2,1)S(1)}, f32[48,1536]{1,0:T(8,128)}, bf16[240,256]{1,0:T(8,128)(2,1)S(1)}, bf16[240,256]{1,0:T(8,128)(2,1)S(1)},...) custom-call(s32[16]{0:T(128)S(1)} %dynamic-slice_bitcast_fusion.place_ref, ...), custom_call_target="tpu_custom_call" | custom-call | flops 1048576 | bytes 1048576 | tf_op jit(solution)/shard_map/own_tile/pallas_call | solution.py:274
  64.5 2.9 %collective-permute-done.13.unread_ref.given_ref = bf16[4,192,256]{2,1,0:T(8,128)(2,1)S(1)} collective-permute-done((bf16[4,192,256]{2,1,0:T(8,128)(2,1)S(1)}, bf16[4,192,256]{2,1,0:T(8,128)(2,1)S(1)}, u32[]{:S(2)}, u32[]{:S(2)}) %collective-permute-start.13) | collective-permute-done | bytes 393248 | tf_op jit(solution)/shard_map/ppermute | solution.py:353
  67.4 0.0 collective-permute-done.12.other_ref
  67.4 1.2 %join_cols.1.rest_4_ = bf16[8,240,256]{2,1,0:T(8,128)(2,1)} custom-call(bf16[8,240,256]{2,1,0:T(8,128)(2,1)S(1)} %get-tuple-element.46.own_ref, bf16[8,240,256]{2,1,0:T(8,128)(2,1)S(1)} %collective-permute-done.12.other_ref, bf16[4,192,256]{2,1,0:T(8,128)(2,1)S(1)} %collective-permute-done.13.unread_ref.given_ref), custom_call_target="tpu_custom_call" | custom-call | tf_op jit(solution)/shard_map/join_cols/pallas_call | solution.py:298
  68.6 5.4 %all-to-all-start.1 = ((bf16[8,240,256]{2,1,0:T(8,128)(2,1)}), bf16[8,240,256]{2,1,0:T(8,128)(2,1)S(1)}, u32[]{:S(2)}, u32[]{:S(2)}) async-start(bf16[8,240,256]{2,1,0:T(8,128)(2,1)} %join_cols.1.rest_4_), calls=%async_computation.1 | async-start | bytes 1966080 | tf_op jit(solution)/shard_map/all_to_all | solution.py:395
  74.0 0.3 collective-permute-start.14
  74.3 4.3 %collective-permute-done.14.twin_ref = bf16[4,48,256]{2,1,0:T(8,128)(2,1)S(1)} collective-permute-done((bf16[4,48,256]{2,1,0:T(8,128)(2,1)S(1)}, bf16[4,48,256]{2,1,0:T(8,128)(2,1)S(1)}, u32[]{:S(2)}, u32[]{:S(2)}) %collective-permute-start.14) | collective-permute-done | bytes 98336 | tf_op jit(solution)/shard_map/ppermute | solution.py:353
  78.6 0.1 join_rows.1
  78.7 0.6 collective-permute-start.15
  79.4 2.1 %collective-permute-start.16 = (bf16[240,256]{1,0:T(8,128)(2,1)S(1)}, bf16[240,256]{1,0:T(8,128)(2,1)S(1)}, u32[]{:S(2)}, u32[]{:S(2)}) collective-permute-start(bf16[240,256]{1,0:T(8,128)(2,1)S(1)} %get-tuple-element.56), channel_id=1, source_target_pairs={{0,4},{1,5},{2,6},{3,7},{4,0},{5,1},{6,2},{7,3},{8,12},{9,13},{10,... | collective-permute-start | bytes 368648 | tf_op jit(solution)/shard_map/ppermute | solution.py:353
  81.4 2.1 %collective-permute-start.17 = (bf16[240,256]{1,0:T(8,128)(2,1)S(1)}, bf16[240,256]{1,0:T(8,128)(2,1)S(1)}, u32[]{:S(2)}, u32[]{:S(2)}) collective-permute-start(bf16[240,256]{1,0:T(8,128)(2,1)S(1)} %get-tuple-element.57), channel_id=1, source_target_pairs={{0,6},{1,7},{2,4},{3,5},{4,2},{5,3},{6,0},{7,1},{8,14},{9,15},{10,... | collective-permute-start | bytes 368648 | tf_op jit(solution)/shard_map/ppermute | solution.py:353
  83.5 0.2 collective-permute-done.15.rest_1_
  83.7 2.1 %collective-permute-done.16.rest_2_ = bf16[240,256]{1,0:T(8,128)(2,1)S(1)} collective-permute-done((bf16[240,256]{1,0:T(8,128)(2,1)S(1)}, bf16[240,256]{1,0:T(8,128)(2,1)S(1)}, u32[]{:S(2)}, u32[]{:S(2)}) %collective-permute-start.16) | collective-permute-done | bytes 122912 | tf_op jit(solution)/shard_map/ppermute | solution.py:353
  85.7 1.8 %collective-permute-done.17.rest_3_ = bf16[240,256]{1,0:T(8,128)(2,1)S(1)} collective-permute-done((bf16[240,256]{1,0:T(8,128)(2,1)S(1)}, bf16[240,256]{1,0:T(8,128)(2,1)S(1)}, u32[]{:S(2)}, u32[]{:S(2)}) %collective-permute-start.17) | collective-permute-done | bytes 122912 | tf_op jit(solution)/shard_map/ppermute | solution.py:353
  87.5 2.2 %all-to-all-done.1.cols_ref = bf16[8,240,256]{2,1,0:T(8,128)(2,1)S(1)} async-done(((bf16[8,240,256]{2,1,0:T(8,128)(2,1)}), bf16[8,240,256]{2,1,0:T(8,128)(2,1)S(1)}, u32[]{:S(2)}, u32[]{:S(2)}) %all-to-all-start.1) | async-done | bytes 983072 | tf_op jit(solution)/shard_map/all_to_all | solution.py:395
  89.7 0.8 finish.1
  (3 shorter events, 0.1 us)
Async XLA Ops:
  1.5 5.1 %collective-permute-start.1 = (bf16[240,256]{1,0:T(8,128)(2,1)S(1)}, bf16[240,256]{1,0:T(8,128)(2,1)S(1)}, u32[]{:S(2)}, u32[]{:S(2)}) collective-permute-start(bf16[240,256]{1,0:T(8,128)(2,1)S(1)} %get-tuple-element.59), channel_id=1, source_target_pairs={{0,1},{1,0},{2,3},{3,2},{4,5},{5,4},{6,7},{7,6},{8,9},{9,8},{10,11... | collective-permute-start | bytes 368648 | tf_op jit(solution)/shard_map/ppermute | solution.py:360
  3.3 6.1 %collective-permute-start = (bf16[240,256]{1,0:T(8,128)(2,1)S(1)}, bf16[240,256]{1,0:T(8,128)(2,1)S(1)}, u32[]{:S(2)}, u32[]{:S(2)}) collective-permute-start(bf16[240,256]{1,0:T(8,128)(2,1)S(1)} %get-tuple-element.62), channel_id=1, source_target_pairs={{0,17},{1,16},{2,19},{3,18},{4,21},{5,20},{6,23},{7,22},{8,25},{9,... | collective-permute-start | bytes 368648 | tf_op jit(solution)/shard_map/ppermute | solution.py:367
  9.4 10.8 %collective-permute-start.4 = (bf16[2,240,256]{2,1,0:T(8,128)(2,1)S(1)}, bf16[2,240,256]{2,1,0:T(8,128)(2,1)S(1)}, u32[]{:S(2)}, u32[]{:S(2)}) collective-permute-start(bf16[2,240,256]{2,1,0:T(8,128)(2,1)S(1)} %pad_maximum_fusion.1.rest_0_), channel_id=1, source_target_pairs={{0,2},{1,3},{2,4},{3,5},{4,6},{5,7},{6,0},{7,1},{8,10},{9,11},{10,... | collective-permute-start | bytes 737288 | tf_op jit(solution)/shard_map/ppermute | solution.py:360
  10.9 12.2 %collective-permute-start.3 = (bf16[2,240,256]{2,1,0:T(8,128)(2,1)S(1)}, bf16[2,240,256]{2,1,0:T(8,128)(2,1)S(1)}, u32[]{:S(2)}, u32[]{:S(2)}) collective-permute-start(bf16[2,240,256]{2,1,0:T(8,128)(2,1)S(1)} %pad_maximum_fusion.1.rest_0_), channel_id=1, source_target_pairs={{0,4},{1,5},{2,6},{3,7},{4,0},{5,1},{6,2},{7,3},{8,12},{9,13},{10,... | collective-permute-start | bytes 737288 | tf_op jit(solution)/shard_map/ppermute | solution.py:360
  13.7 10.4 %collective-permute-start.7 = (bf16[2,240,256]{2,1,0:T(8,128)(2,1)S(1)}, bf16[2,240,256]{2,1,0:T(8,128)(2,1)S(1)}, u32[]{:S(2)}, u32[]{:S(2)}) collective-permute-start(bf16[2,240,256]{2,1,0:T(8,128)(2,1)S(1)} %pad_maximum_fusion.rest_0_), channel_id=1, source_target_pairs={{0,32},{1,33},{2,34},{3,35},{4,36},{5,37},{6,38},{7,39},{8,40},{9,... | collective-permute-start | bytes 737288 | tf_op jit(solution)/shard_map/ppermute | solution.py:367
  15.6 12.5 %collective-permute-start.6 = (bf16[2,240,256]{2,1,0:T(8,128)(2,1)S(1)}, bf16[2,240,256]{2,1,0:T(8,128)(2,1)S(1)}, u32[]{:S(2)}, u32[]{:S(2)}) collective-permute-start(bf16[2,240,256]{2,1,0:T(8,128)(2,1)S(1)} %pad_maximum_fusion.rest_0_), channel_id=1, source_target_pairs={{0,64},{1,65},{2,66},{3,67},{4,68},{5,69},{6,70},{7,71},{8,72},{9,... | collective-permute-start | bytes 737288 | tf_op jit(solution)/shard_map/ppermute | solution.py:367
  19.2 9.0 %collective-permute-start.5 = (bf16[2,240,256]{2,1,0:T(8,128)(2,1)S(1)}, bf16[2,240,256]{2,1,0:T(8,128)(2,1)S(1)}, u32[]{:S(2)}, u32[]{:S(2)}) collective-permute-start(bf16[2,240,256]{2,1,0:T(8,128)(2,1)S(1)} %pad_maximum_fusion.rest_0_), channel_id=1, source_target_pairs={{0,96},{1,97},{2,98},{3,99},{4,100},{5,101},{6,102},{7,103},{8,104... | collective-permute-start | bytes 737288 | tf_op jit(solution)/shard_map/ppermute | solution.py:367
  20.2 8.5 %collective-permute-start.2 = (bf16[2,240,256]{2,1,0:T(8,128)(2,1)S(1)}, bf16[2,240,256]{2,1,0:T(8,128)(2,1)S(1)}, u32[]{:S(2)}, u32[]{:S(2)}) collective-permute-start(bf16[2,240,256]{2,1,0:T(8,128)(2,1)S(1)} %pad_maximum_fusion.1.rest_0_), channel_id=1, source_target_pairs={{0,6},{1,7},{2,0},{3,1},{4,2},{5,3},{6,4},{7,5},{8,14},{9,15},{10,... | collective-permute-start | bytes 737288 | tf_op jit(solution)/shard_map/ppermute | solution.py:360
  23.2 6.5 %collective-permute-start.8 = (bf16[2,240,256]{2,1,0:T(8,128)(2,1)S(1)}, bf16[2,240,256]{2,1,0:T(8,128)(2,1)S(1)}, u32[]{:S(2)}, u32[]{:S(2)}) collective-permute-start(bf16[2,240,256]{2,1,0:T(8,128)(2,1)S(1)} %pad_maximum_fusion.rest_0_), channel_id=1, source_target_pairs={{0,8},{8,0},{16,24},{24,16},{32,40},{40,32},{48,56},{56,48},{64,72... | collective-permute-start | bytes 737288 | tf_op jit(solution)/shard_map/ppermute | solution.py:356
  24.1 5.6 %collective-permute-start.11 = (bf16[2,240,256]{2,1,0:T(8,128)(2,1)S(1)}, bf16[2,240,256]{2,1,0:T(8,128)(2,1)S(1)}, u32[]{:S(2)}, u32[]{:S(2)}) collective-permute-start(bf16[2,240,256]{2,1,0:T(8,128)(2,1)S(1)} %collective-permute-done.7.rest_3_), channel_id=1, source_target_pairs={{0,8},{8,0},{16,24},{24,16},{32,40},{40,32},{48,56},{56,48},{64,72... | collective-permute-start | bytes 737288 | tf_op jit(solution)/shard_map/ppermute | solution.py:356
  28.1 1.6 %collective-permute-start.10 = (bf16[2,240,256]{2,1,0:T(8,128)(2,1)S(1)}, bf16[2,240,256]{2,1,0:T(8,128)(2,1)S(1)}, u32[]{:S(2)}, u32[]{:S(2)}) collective-permute-start(bf16[2,240,256]{2,1,0:T(8,128)(2,1)S(1)} %collective-permute-done.6.rest_2_), channel_id=1, source_target_pairs={{0,8},{8,0},{16,24},{24,16},{32,40},{40,32},{48,56},{56,48},{64,72... | collective-permute-start | bytes 737288 | tf_op jit(solution)/shard_map/ppermute | solution.py:356
  28.1 1.9 %collective-permute-start.9 = (bf16[2,240,256]{2,1,0:T(8,128)(2,1)S(1)}, bf16[2,240,256]{2,1,0:T(8,128)(2,1)S(1)}, u32[]{:S(2)}, u32[]{:S(2)}) collective-permute-start(bf16[2,240,256]{2,1,0:T(8,128)(2,1)S(1)} %collective-permute-done.5.rest_1_), channel_id=1, source_target_pairs={{0,8},{8,0},{16,24},{24,16},{32,40},{40,32},{48,56},{56,48},{64,72... | collective-permute-start | bytes 737288 | tf_op jit(solution)/shard_map/ppermute | solution.py:356
  55.8 11.6 %collective-permute-start.12 = (bf16[8,240,256]{2,1,0:T(8,128)(2,1)S(1)}, bf16[8,240,256]{2,1,0:T(8,128)(2,1)S(1)}, u32[]{:S(2)}, u32[]{:S(2)}) collective-permute-start(bf16[8,240,256]{2,1,0:T(8,128)(2,1)S(1)} %get-tuple-element.47), channel_id=1, source_target_pairs={{0,8},{8,0},{16,24},{24,16},{32,40},{40,32},{48,56},{56,48},{64,72... | collective-permute-start | bytes 2949128 | tf_op jit(solution)/shard_map/ppermute | solution.py:356
  55.8 11.5 %collective-permute-start.13 = (bf16[4,192,256]{2,1,0:T(8,128)(2,1)S(1)}, bf16[4,192,256]{2,1,0:T(8,128)(2,1)S(1)}, u32[]{:S(2)}, u32[]{:S(2)}) collective-permute-start(bf16[4,192,256]{2,1,0:T(8,128)(2,1)S(1)} %get-tuple-element.48), channel_id=1, source_target_pairs={{0,1},{1,0},{2,3},{3,2},{4,5},{5,4},{6,7},{7,6},{8,9},{9,8},{10,11... | collective-permute-start | bytes 1179656 | tf_op jit(solution)/shard_map/ppermute | solution.py:353
  68.6 21.2 %all-to-all-start.1 = ((bf16[8,240,256]{2,1,0:T(8,128)(2,1)}), bf16[8,240,256]{2,1,0:T(8,128)(2,1)S(1)}, u32[]{:S(2)}, u32[]{:S(2)}) async-start(bf16[8,240,256]{2,1,0:T(8,128)(2,1)} %join_cols.1.rest_4_), calls=%async_computation.1 | async-start | bytes 1966080 | tf_op jit(solution)/shard_map/all_to_all | solution.py:395
  74.0 4.6 %collective-permute-start.14 = (bf16[4,48,256]{2,1,0:T(8,128)(2,1)S(1)}, bf16[4,48,256]{2,1,0:T(8,128)(2,1)S(1)}, u32[]{:S(2)}, u32[]{:S(2)}) collective-permute-start(bf16[4,48,256]{2,1,0:T(8,128)(2,1)S(1)} %get-tuple-element.49), channel_id=1, source_target_pairs={{0,1},{1,0},{2,3},{3,2},{4,5},{5,4},{6,7},{7,6},{8,9},{9,8},{10,11... | collective-permute-start | bytes 294920 | tf_op jit(solution)/shard_map/ppermute | solution.py:353
  78.7 5.0 %collective-permute-start.15 = (bf16[240,256]{1,0:T(8,128)(2,1)S(1)}, bf16[240,256]{1,0:T(8,128)(2,1)S(1)}, u32[]{:S(2)}, u32[]{:S(2)}) collective-permute-start(bf16[240,256]{1,0:T(8,128)(2,1)S(1)} %get-tuple-element.55), channel_id=1, source_target_pairs={{0,2},{1,3},{2,0},{3,1},{4,6},{5,7},{6,4},{7,5},{8,10},{9,11},{10,... | collective-permute-start | bytes 368648 | tf_op jit(solution)/shard_map/ppermute | solution.py:353
  79.4 6.4 %collective-permute-start.16 = (bf16[240,256]{1,0:T(8,128)(2,1)S(1)}, bf16[240,256]{1,0:T(8,128)(2,1)S(1)}, u32[]{:S(2)}, u32[]{:S(2)}) collective-permute-start(bf16[240,256]{1,0:T(8,128)(2,1)S(1)} %get-tuple-element.56), channel_id=1, source_target_pairs={{0,4},{1,5},{2,6},{3,7},{4,0},{5,1},{6,2},{7,3},{8,12},{9,13},{10,... | collective-permute-start | bytes 368648 | tf_op jit(solution)/shard_map/ppermute | solution.py:353
  81.4 6.1 %collective-permute-start.17 = (bf16[240,256]{1,0:T(8,128)(2,1)S(1)}, bf16[240,256]{1,0:T(8,128)(2,1)S(1)}, u32[]{:S(2)}, u32[]{:S(2)}) collective-permute-start(bf16[240,256]{1,0:T(8,128)(2,1)S(1)} %get-tuple-element.57), channel_id=1, source_target_pairs={{0,6},{1,7},{2,4},{3,5},{4,2},{5,3},{6,0},{7,1},{8,14},{9,15},{10,... | collective-permute-start | bytes 368648 | tf_op jit(solution)/shard_map/ppermute | solution.py:353

commit v5 on v3

--- a/solution.py
+++ b/solution.py
@@ -360,8 +360,10 @@
     chunks, alongs = (pack(target_embed), pack(source_embed)), (along_z, along_x)
     near = [jnp.stack([chunk, along(chunk, 0, 1)]) for chunk, along in zip(chunks, alongs)]
     near, place = lax.optimization_barrier((near, place))
-    moved = [[along(array, -move, 0) for array, along in zip(near, alongs)] for move in MOVES[1:]]
-    b_parts, a_parts = [[array, *[pair[index] for pair in moved]] for index, array in enumerate(near)]
+    right = [along(array, -1, 0) for array, along in zip(near, alongs)]
+    far = [along(array, -1, 0) for array, along in zip(right, alongs)]
+    left = [along(array, 1, 0) for array, along in zip(near, alongs)]
+    b_parts, a_parts = [list(parts) for parts in zip(near, right, far, left)]
     others = [swap(part) for part in b_parts]
     scaled, stats, kept = row_stats(place, a_parts, b_parts, others, own, feat)
     stats = lax.all_to_all(stats, "col", 0, 0)

time: 90.7 us -> 91.4 us (level)
  waiting for transfers between devices: 24.2 us -> 21.9 us
  blocking collectives: 9.44 us -> 11.4 us
  starting transfers between devices: 28.4 us -> 29.4 us
    ppermute x4, waiting for transfers between devices: 7.68 us -> 3.72 us  [along_z(): return lax.ppermute(array, both, pairs)]
    ppermute x4, waiting for transfers between devices: 2.01 us -> 5.38 us  [along_x(): return lax.ppermute(array, 'col', pairs)]
    all_to_all x1, blocking collectives: 9.44 us -> 11.4 us  [local(): stats = lax.all_to_all(stats, 'col', 0, 0)]
    ppermute x5, waiting for transfers between devices: 1.34 us -> 0.01 us  [swap(): return lax.ppermute(array, 'row', [(r, r ^ 1) for r in range(row_size)])]
    ppermute x4, starting transfers between devices: 8.69 us -> 9.98 us  [along_z(): return lax.ppermute(array, both, pairs)]
    all_to_all x1, starting transfers between devices: 5.08 us -> 4.02 us  [local(): cols = lax.all_to_all(cols, both, 0, 0, axis_index_groups=groups)]
  transfers between devices with their start and end apart: 19 -> 19, of which waited for: 13 -> 11; matrix products, arithmetic and copies ran while one was open for 1% -> 1% of each run, Pallas kernels for 8% -> 8%
where the time goes in v5:
time: 91.4 us; the launch traced here: 91.1 us
  starting transfers between devices  29.4 us (32%)
  Pallas kernels  26.1 us (29%)
  waiting for transfers between devices  21.9 us (24%)
  blocking collectives  11.4 us (12%)
  other arithmetic  0.93 us (1%)
    pallas_call x2, Pallas kernels, tile_sums(): pl.pallas_call(functools.partial(tile_kernel, own, feat, half), in_specs=...  14 us
    all_to_all x1, blocking collectives, local(): stats = lax.all_to_all(stats, 'col', 0, 0)  11.4 us
    ppermute x5, waiting for transfers between devices, mate(): return lax.ppermute(array, 'col', [(c, c ^ bits) for c in range(col_size)])  10.6 us
    ppermute x4, starting transfers between devices, along_z(): return lax.ppermute(array, both, pairs)  9.98 us
    pallas_call x1, Pallas kernels, row_stats(): pl.pallas_call(functools.partial(stats_kernel, own, feat), grid=(rows //...  8.73 us
    ppermute x4, starting transfers between devices, along_x(): return lax.ppermute(array, 'col', pairs)  7.73 us
    ppermute x5, starting transfers between devices, mate(): return lax.ppermute(array, 'col', [(c, c ^ bits) for c in range(col_size)])  6.97 us
    ppermute x4, waiting for transfers between devices, along_x(): return lax.ppermute(array, 'col', pairs)  5.38 us
  transfers between devices with their start and end apart: 19, of which 11 were waited for; matrix products, arithmetic and copies ran while one was open for 1% of the time, Pallas kernels for 8%

profile of v5, /device:TPU:0, one launch (start us, length us, event | category | flops | bytes accessed | tf_op | source)
XLA Modules:
  0.0 91.1 jit_solution(13455317135385214153)
XLA Ops:
  0.6 0.9 fusion.1
  1.5 1.7 %collective-permute-start.1 = (bf16[240,256]{1,0:T(8,128)(2,1)S(1)}, bf16[240,256]{1,0:T(8,128)(2,1)S(1)}, u32[]{:S(2)}, u32[]{:S(2)}) collective-permute-start(bf16[240,256]{1,0:T(8,128)(2,1)S(1)} %get-tuple-element.59), channel_id=1, source_target_pairs={{0,1},{1,0},{2,3},{3,2},{4,5},{5,4},{6,7},{7,6},{8,9},{9,8},{10,11... | collective-permute-start | bytes 368648 | tf_op jit(solution)/shard_map/ppermute | solution.py:344
  3.3 2.2 %collective-permute-start = (bf16[240,256]{1,0:T(8,128)(2,1)S(1)}, bf16[240,256]{1,0:T(8,128)(2,1)S(1)}, u32[]{:S(2)}, u32[]{:S(2)}) collective-permute-start(bf16[240,256]{1,0:T(8,128)(2,1)S(1)} %get-tuple-element.62), channel_id=1, source_target_pairs={{0,17},{1,16},{2,19},{3,18},{4,21},{5,20},{6,23},{7,22},{8,25},{9,... | collective-permute-start | bytes 368648 | tf_op jit(solution)/shard_map/ppermute | solution.py:351
  5.4 0.7 dynamic-slice_bitcast_fusion.place_ref
  6.1 0.4 collective-permute-done.1
  6.6 2.7 %collective-permute-done = bf16[240,256]{1,0:T(8,128)(2,1)S(1)} collective-permute-done((bf16[240,256]{1,0:T(8,128)(2,1)S(1)}, bf16[240,256]{1,0:T(8,128)(2,1)S(1)}, u32[]{:S(2)}, u32[]{:S(2)}) %collective-permute-start) | collective-permute-done | bytes 122912 | tf_op jit(solution)/shard_map/ppermute | solution.py:351
  9.4 4.1 %collective-permute-start.3 = (bf16[2,240,256]{2,1,0:T(8,128)(2,1)S(1)}, bf16[2,240,256]{2,1,0:T(8,128)(2,1)S(1)}, u32[]{:S(2)}, u32[]{:S(2)}) collective-permute-start(bf16[2,240,256]{2,1,0:T(8,128)(2,1)S(1)} %pad_maximum_fusion.rest_1_), channel_id=1, source_target_pairs={{0,96},{1,97},{2,98},{3,99},{4,100},{5,101},{6,102},{7,103},{8,104... | collective-permute-start | bytes 737288 | tf_op jit(solution)/shard_map/ppermute | solution.py:351
  13.5 1.5 %collective-permute-start.6 = (bf16[2,240,256]{2,1,0:T(8,128)(2,1)S(1)}, bf16[2,240,256]{2,1,0:T(8,128)(2,1)S(1)}, u32[]{:S(2)}, u32[]{:S(2)}) collective-permute-start(bf16[2,240,256]{2,1,0:T(8,128)(2,1)S(1)} %pad_maximum_fusion.1.rest_0_), channel_id=1, source_target_pairs={{0,2},{1,3},{2,4},{3,5},{4,6},{5,7},{6,0},{7,1},{8,10},{9,11},{10,... | collective-permute-start | bytes 737288 | tf_op jit(solution)/shard_map/ppermute | solution.py:344
  15.0 1.7 %collective-permute-start.2 = (bf16[2,240,256]{2,1,0:T(8,128)(2,1)S(1)}, bf16[2,240,256]{2,1,0:T(8,128)(2,1)S(1)}, u32[]{:S(2)}, u32[]{:S(2)}) collective-permute-start(bf16[2,240,256]{2,1,0:T(8,128)(2,1)S(1)} %pad_maximum_fusion.1.rest_0_), channel_id=1, source_target_pairs={{0,6},{1,7},{2,0},{3,1},{4,2},{5,3},{6,4},{7,5},{8,14},{9,15},{10,... | collective-permute-start | bytes 737288 | tf_op jit(solution)/shard_map/ppermute | solution.py:344
  16.7 0.0 collective-permute-start.7
  16.7 0.5 collective-permute-done.3.rest_3_
  17.3 3.7 %collective-permute-start.5 = (bf16[2,240,256]{2,1,0:T(8,128)(2,1)S(1)}, bf16[2,240,256]{2,1,0:T(8,128)(2,1)S(1)}, u32[]{:S(2)}, u32[]{:S(2)}) collective-permute-start(bf16[2,240,256]{2,1,0:T(8,128)(2,1)S(1)} %collective-permute-done.3.rest_3_), channel_id=1, source_target_pairs={{0,96},{1,97},{2,98},{3,99},{4,100},{5,101},{6,102},{7,103},{8,104... | collective-permute-start | bytes 737288 | tf_op jit(solution)/shard_map/ppermute | solution.py:351
  21.0 0.0 collective-permute-start.8
  21.0 0.0 collective-permute-done.6.rest_6_
  21.0 0.5 collective-permute-start.9
  21.5 0.0 collective-permute-done.2.rest_2_
  21.5 2.8 %collective-permute-start.4 = (bf16[2,240,256]{2,1,0:T(8,128)(2,1)S(1)}, bf16[2,240,256]{2,1,0:T(8,128)(2,1)S(1)}, u32[]{:S(2)}, u32[]{:S(2)}) collective-permute-start(bf16[2,240,256]{2,1,0:T(8,128)(2,1)S(1)} %collective-permute-done.2.rest_2_), channel_id=1, source_target_pairs={{0,6},{1,7},{2,0},{3,1},{4,2},{5,3},{6,4},{7,5},{8,14},{9,15},{10,... | collective-permute-start | bytes 737288 | tf_op jit(solution)/shard_map/ppermute | solution.py:344
  24.2 0.0 collective-permute-done.7.rest_7_
  24.2 0.0 collective-permute-start.11
  24.2 0.4 collective-permute-done.5.rest_5_
  24.7 0.1 collective-permute-start.10
  24.8 0.0 collective-permute-done.8.rest_8_
  24.8 4.9 %collective-permute-done.4.rest_4_ = bf16[2,240,256]{2,1,0:T(8,128)(2,1)S(1)} collective-permute-done((bf16[2,240,256]{2,1,0:T(8,128)(2,1)S(1)}, bf16[2,240,256]{2,1,0:T(8,128)(2,1)S(1)}, u32[]{:S(2)}, u32[]{:S(2)}) %collective-permute-start.4) | collective-permute-done | bytes 245792 | tf_op jit(solution)/shard_map/ppermute | solution.py:344
  29.7 0.0 collective-permute-done.11.rest_11_
  29.7 0.0 collective-permute-done.9.rest_9_
  29.7 0.0 collective-permute-done.10.rest_10_
  29.7 8.7 %row_stats.1 = (bf16[1536,256]{1,0:T(8,128)(2,1)S(1)}, f32[8,4,1536]{2,1,0:T(4,128)S(1)}, bf16[1536,256]{1,0:T(8,128)(2,1)S(1)}, bf16[256,1536]{1,0:T(8,128)(2,1...) custom-call(s32[16]{0:T(128)S(1)} %dynamic-slice_bitcast_fusion.plac, ...), custom_call_target="tpu_custom_call" | custom-call | flops 4831838208 | bytes 8388608 | tf_op jit(solution)/shard_map/row_stats/pallas_call | solution.py:140
  38.4 11.4 %all_to_all.10.stats_ref = f32[8,4,1536]{2,1,0:T(4,128)S(1)} all-to-all(f32[8,4,1536]{2,1,0:T(4,128)S(1)} %get-tuple-element.41), channel_id=1, replica_groups=mesh['row'=16,'col'=8] {'col'}, dimensions={0} | all-to-all | bytes 393216 | tf_op jit(solution)/shard_map/all_to_all | solution.py:369
  49.9 1.2 %weigh.1 = (f32[8,1536]{1,0:T(8,128)S(1)}, bf16[4,192,256]{2,1,0:T(8,128)(2,1)S(1)}, bf16[4,192,256]{2,1,0:T(8,128)(2,1)S(1)}) custom-call(s32[16]{0:T(128)S(1)} %dynamic-slice_bitcast_fusion.place_ref, f32[8,4,1536]{2,1,0:T(4,128)S(1)} %all_to_all.10.stats_ref, bf16[1536,256]{1,0:T(8,128)(2,1)S(1)} %get-tuple-element.42.scaled_ref), custom_call_target="tpu_custom_call" | custom-call | tf_op jit(solution)/shard_map/weigh/pallas_call | solution.py:181
  51.1 6.7 %other_tile.1 = (bf16[8,240,256]{2,1,0:T(8,128)(2,1)S(1)}, f32[48,1536]{1,0:T(8,128)S(1)}) custom-call(s32[16]{0:T(128)S(1)} %dynamic-slice_bitcast_fusion.place_ref, bf16[1536,256]{1,0:T(8,128)(2,1)S(1)} %get-tuple-element.34.a_pair, bf16[256,1536]{1,0:T(8,128)(2,1)S(1)} %get-tuple-element.35.a_pair_t, bf16[1536,128]{1,0:T(8,128)(2,1)S(1)} %get-tuple-element.36.a_src, ...), custom_call_target="tpu_custom_call" | custom-call | flops 6039797760 | bytes 1048576 | tf_op jit(solution)/shard_map/other_tile/pallas_call | solution.py:258
  57.8 0.1 collective-permute-start.12
  57.8 1.4 %collective-permute-start.13 = (bf16[4,192,256]{2,1,0:T(8,128)(2,1)S(1)}, bf16[4,192,256]{2,1,0:T(8,128)(2,1)S(1)}, u32[]{:S(2)}, u32[]{:S(2)}) collective-permute-start(bf16[4,192,256]{2,1,0:T(8,128)(2,1)S(1)} %get-tuple-element.48), channel_id=1, source_target_pairs={{0,1},{1,0},{2,3},{3,2},{4,5},{5,4},{6,7},{7,6},{8,9},{9,8},{10,11... | collective-permute-start | bytes 1179656 | tf_op jit(solution)/shard_map/ppermute | solution.py:337
  59.3 7.4 %own_tile.1 = (bf16[8,240,256]{2,1,0:T(8,128)(2,1)S(1)}, f32[48,1536]{1,0:T(8,128)}, bf16[240,256]{1,0:T(8,128)(2,1)S(1)}, bf16[240,256]{1,0:T(8,128)(2,1)S(1)},...) custom-call(s32[16]{0:T(128)S(1)} %dynamic-slice_bitcast_fusion.place_ref, ...), custom_call_target="tpu_custom_call" | custom-call | flops 1048576 | bytes 1048576 | tf_op jit(solution)/shard_map/own_tile/pallas_call | solution.py:258
  66.7 2.7 %collective-permute-done.13.unread_ref.given_ref = bf16[4,192,256]{2,1,0:T(8,128)(2,1)S(1)} collective-permute-done((bf16[4,192,256]{2,1,0:T(8,128)(2,1)S(1)}, bf16[4,192,256]{2,1,0:T(8,128)(2,1)S(1)}, u32[]{:S(2)}, u32[]{:S(2)}) %collective-permute-start.13) | collective-permute-done | bytes 393248 | tf_op jit(solution)/shard_map/ppermute | solution.py:337
  69.4 0.0 collective-permute-done.12.other_ref
  69.4 1.2 %join_cols.1.rest_4_ = bf16[8,240,256]{2,1,0:T(8,128)(2,1)} custom-call(bf16[8,240,256]{2,1,0:T(8,128)(2,1)S(1)} %get-tuple-element.46.own_ref, bf16[8,240,256]{2,1,0:T(8,128)(2,1)S(1)} %collective-permute-done.12.other_ref, bf16[4,192,256]{2,1,0:T(8,128)(2,1)S(1)} %collective-permute-done.13.unread_ref.given_ref), custom_call_target="tpu_custom_call" | custom-call | tf_op jit(solution)/shard_map/join_cols/pallas_call | solution.py:282
  70.6 4.0 %all-to-all-start.1 = ((bf16[8,240,256]{2,1,0:T(8,128)(2,1)}), bf16[8,240,256]{2,1,0:T(8,128)(2,1)S(1)}, u32[]{:S(2)}, u32[]{:S(2)}) async-start(bf16[8,240,256]{2,1,0:T(8,128)(2,1)} %join_cols.1.rest_4_), calls=%async_computation.1 | async-start | bytes 1966080 | tf_op jit(solution)/shard_map/all_to_all | solution.py:380
  74.6 0.8 collective-permute-start.14
  75.3 3.9 %collective-permute-done.14.twin_ref = bf16[4,48,256]{2,1,0:T(8,128)(2,1)S(1)} collective-permute-done((bf16[4,48,256]{2,1,0:T(8,128)(2,1)S(1)}, bf16[4,48,256]{2,1,0:T(8,128)(2,1)S(1)}, u32[]{:S(2)}, u32[]{:S(2)}) %collective-permute-start.14) | collective-permute-done | bytes 98336 | tf_op jit(solution)/shard_map/ppermute | solution.py:337
  79.2 0.1 join_rows.1
  79.3 0.6 collective-permute-start.15
  79.9 2.1 %collective-permute-start.16 = (bf16[240,256]{1,0:T(8,128)(2,1)S(1)}, bf16[240,256]{1,0:T(8,128)(2,1)S(1)}, u32[]{:S(2)}, u32[]{:S(2)}) collective-permute-start(bf16[240,256]{1,0:T(8,128)(2,1)S(1)} %get-tuple-element.56), channel_id=1, source_target_pairs={{0,4},{1,5},{2,6},{3,7},{4,0},{5,1},{6,2},{7,3},{8,12},{9,13},{10,... | collective-permute-start | bytes 368648 | tf_op jit(solution)/shard_map/ppermute | solution.py:337
  82.0 2.1 %collective-permute-start.17 = (bf16[240,256]{1,0:T(8,128)(2,1)S(1)}, bf16[240,256]{1,0:T(8,128)(2,1)S(1)}, u32[]{:S(2)}, u32[]{:S(2)}) collective-permute-start(bf16[240,256]{1,0:T(8,128)(2,1)S(1)} %get-tuple-element.57), channel_id=1, source_target_pairs={{0,6},{1,7},{2,4},{3,5},{4,2},{5,3},{6,0},{7,1},{8,14},{9,15},{10,... | collective-permute-start | bytes 368648 | tf_op jit(solution)/shard_map/ppermute | solution.py:337
  84.1 0.2 collective-permute-done.15.rest_1_
  84.3 2.1 %collective-permute-done.16.rest_2_ = bf16[240,256]{1,0:T(8,128)(2,1)S(1)} collective-permute-done((bf16[240,256]{1,0:T(8,128)(2,1)S(1)}, bf16[240,256]{1,0:T(8,128)(2,1)S(1)}, u32[]{:S(2)}, u32[]{:S(2)}) %collective-permute-start.16) | collective-permute-done | bytes 122912 | tf_op jit(solution)/shard_map/ppermute | solution.py:337
  86.3 1.8 %collective-permute-done.17.rest_3_ = bf16[240,256]{1,0:T(8,128)(2,1)S(1)} collective-permute-done((bf16[240,256]{1,0:T(8,128)(2,1)S(1)}, bf16[240,256]{1,0:T(8,128)(2,1)S(1)}, u32[]{:S(2)}, u32[]{:S(2)}) %collective-permute-start.17) | collective-permute-done | bytes 122912 | tf_op jit(solution)/shard_map/ppermute | solution.py:337
  88.1 2.2 %all-to-all-done.1.cols_ref = bf16[8,240,256]{2,1,0:T(8,128)(2,1)S(1)} async-done(((bf16[8,240,256]{2,1,0:T(8,128)(2,1)}), bf16[8,240,256]{2,1,0:T(8,128)(2,1)S(1)}, u32[]{:S(2)}, u32[]{:S(2)}) %all-to-all-start.1) | async-done | bytes 983072 | tf_op jit(solution)/shard_map/all_to_all | solution.py:380
  90.3 0.8 finish.1
  (2 shorter events, 0.1 us)
Async XLA Ops:
  1.5 5.1 %collective-permute-start.1 = (bf16[240,256]{1,0:T(8,128)(2,1)S(1)}, bf16[240,256]{1,0:T(8,128)(2,1)S(1)}, u32[]{:S(2)}, u32[]{:S(2)}) collective-permute-start(bf16[240,256]{1,0:T(8,128)(2,1)S(1)} %get-tuple-element.59), channel_id=1, source_target_pairs={{0,1},{1,0},{2,3},{3,2},{4,5},{5,4},{6,7},{7,6},{8,9},{9,8},{10,11... | collective-permute-start | bytes 368648 | tf_op jit(solution)/shard_map/ppermute | solution.py:344
  3.3 6.1 %collective-permute-start = (bf16[240,256]{1,0:T(8,128)(2,1)S(1)}, bf16[240,256]{1,0:T(8,128)(2,1)S(1)}, u32[]{:S(2)}, u32[]{:S(2)}) collective-permute-start(bf16[240,256]{1,0:T(8,128)(2,1)S(1)} %get-tuple-element.62), channel_id=1, source_target_pairs={{0,17},{1,16},{2,19},{3,18},{4,21},{5,20},{6,23},{7,22},{8,25},{9,... | collective-permute-start | bytes 368648 | tf_op jit(solution)/shard_map/ppermute | solution.py:351
  9.4 7.9 %collective-permute-start.3 = (bf16[2,240,256]{2,1,0:T(8,128)(2,1)S(1)}, bf16[2,240,256]{2,1,0:T(8,128)(2,1)S(1)}, u32[]{:S(2)}, u32[]{:S(2)}) collective-permute-start(bf16[2,240,256]{2,1,0:T(8,128)(2,1)S(1)} %pad_maximum_fusion.rest_1_), channel_id=1, source_target_pairs={{0,96},{1,97},{2,98},{3,99},{4,100},{5,101},{6,102},{7,103},{8,104... | collective-permute-start | bytes 737288 | tf_op jit(solution)/shard_map/ppermute | solution.py:351
  13.5 7.5 %collective-permute-start.6 = (bf16[2,240,256]{2,1,0:T(8,128)(2,1)S(1)}, bf16[2,240,256]{2,1,0:T(8,128)(2,1)S(1)}, u32[]{:S(2)}, u32[]{:S(2)}) collective-permute-start(bf16[2,240,256]{2,1,0:T(8,128)(2,1)S(1)} %pad_maximum_fusion.1.rest_0_), channel_id=1, source_target_pairs={{0,2},{1,3},{2,4},{3,5},{4,6},{5,7},{6,0},{7,1},{8,10},{9,11},{10,... | collective-permute-start | bytes 737288 | tf_op jit(solution)/shard_map/ppermute | solution.py:344
  15.0 6.5 %collective-permute-start.2 = (bf16[2,240,256]{2,1,0:T(8,128)(2,1)S(1)}, bf16[2,240,256]{2,1,0:T(8,128)(2,1)S(1)}, u32[]{:S(2)}, u32[]{:S(2)}) collective-permute-start(bf16[2,240,256]{2,1,0:T(8,128)(2,1)S(1)} %pad_maximum_fusion.1.rest_0_), channel_id=1, source_target_pairs={{0,6},{1,7},{2,0},{3,1},{4,2},{5,3},{6,4},{7,5},{8,14},{9,15},{10,... | collective-permute-start | bytes 737288 | tf_op jit(solution)/shard_map/ppermute | solution.py:344
  16.7 7.5 %collective-permute-start.7 = (bf16[2,240,256]{2,1,0:T(8,128)(2,1)S(1)}, bf16[2,240,256]{2,1,0:T(8,128)(2,1)S(1)}, u32[]{:S(2)}, u32[]{:S(2)}) collective-permute-start(bf16[2,240,256]{2,1,0:T(8,128)(2,1)S(1)} %pad_maximum_fusion.rest_1_), channel_id=1, source_target_pairs={{0,32},{1,33},{2,34},{3,35},{4,36},{5,37},{6,38},{7,39},{8,40},{9,... | collective-permute-start | bytes 737288 | tf_op jit(solution)/shard_map/ppermute | solution.py:351
  17.3 7.4 %collective-permute-start.5 = (bf16[2,240,256]{2,1,0:T(8,128)(2,1)S(1)}, bf16[2,240,256]{2,1,0:T(8,128)(2,1)S(1)}, u32[]{:S(2)}, u32[]{:S(2)}) collective-permute-start(bf16[2,240,256]{2,1,0:T(8,128)(2,1)S(1)} %collective-permute-done.3.rest_3_), channel_id=1, source_target_pairs={{0,96},{1,97},{2,98},{3,99},{4,100},{5,101},{6,102},{7,103},{8,104... | collective-permute-start | bytes 737288 | tf_op jit(solution)/shard_map/ppermute | solution.py:351
  21.0 3.8 %collective-permute-start.8 = (bf16[2,240,256]{2,1,0:T(8,128)(2,1)S(1)}, bf16[2,240,256]{2,1,0:T(8,128)(2,1)S(1)}, u32[]{:S(2)}, u32[]{:S(2)}) collective-permute-start(bf16[2,240,256]{2,1,0:T(8,128)(2,1)S(1)} %pad_maximum_fusion.rest_1_), channel_id=1, source_target_pairs={{0,8},{8,0},{16,24},{24,16},{32,40},{40,32},{48,56},{56,48},{64,72... | collective-permute-start | bytes 737288 | tf_op jit(solution)/shard_map/ppermute | solution.py:340
  21.0 8.7 %collective-permute-start.9 = (bf16[2,240,256]{2,1,0:T(8,128)(2,1)S(1)}, bf16[2,240,256]{2,1,0:T(8,128)(2,1)S(1)}, u32[]{:S(2)}, u32[]{:S(2)}) collective-permute-start(bf16[2,240,256]{2,1,0:T(8,128)(2,1)S(1)} %collective-permute-done.3.rest_3_), channel_id=1, source_target_pairs={{0,8},{8,0},{16,24},{24,16},{32,40},{40,32},{48,56},{56,48},{64,72... | collective-permute-start | bytes 737288 | tf_op jit(solution)/shard_map/ppermute | solution.py:340
  21.5 8.2 %collective-permute-start.4 = (bf16[2,240,256]{2,1,0:T(8,128)(2,1)S(1)}, bf16[2,240,256]{2,1,0:T(8,128)(2,1)S(1)}, u32[]{:S(2)}, u32[]{:S(2)}) collective-permute-start(bf16[2,240,256]{2,1,0:T(8,128)(2,1)S(1)} %collective-permute-done.2.rest_2_), channel_id=1, source_target_pairs={{0,6},{1,7},{2,0},{3,1},{4,2},{5,3},{6,4},{7,5},{8,14},{9,15},{10,... | collective-permute-start | bytes 737288 | tf_op jit(solution)/shard_map/ppermute | solution.py:344
  24.2 5.5 %collective-permute-start.11 = (bf16[2,240,256]{2,1,0:T(8,128)(2,1)S(1)}, bf16[2,240,256]{2,1,0:T(8,128)(2,1)S(1)}, u32[]{:S(2)}, u32[]{:S(2)}) collective-permute-start(bf16[2,240,256]{2,1,0:T(8,128)(2,1)S(1)} %collective-permute-done.7.rest_7_), channel_id=1, source_target_pairs={{0,8},{8,0},{16,24},{24,16},{32,40},{40,32},{48,56},{56,48},{64,72... | collective-permute-start | bytes 737288 | tf_op jit(solution)/shard_map/ppermute | solution.py:340
  24.7 5.0 %collective-permute-start.10 = (bf16[2,240,256]{2,1,0:T(8,128)(2,1)S(1)}, bf16[2,240,256]{2,1,0:T(8,128)(2,1)S(1)}, u32[]{:S(2)}, u32[]{:S(2)}) collective-permute-start(bf16[2,240,256]{2,1,0:T(8,128)(2,1)S(1)} %collective-permute-done.5.rest_5_), channel_id=1, source_target_pairs={{0,8},{8,0},{16,24},{24,16},{32,40},{40,32},{48,56},{56,48},{64,72... | collective-permute-start | bytes 737288 | tf_op jit(solution)/shard_map/ppermute | solution.py:340
  57.8 11.6 %collective-permute-start.12 = (bf16[8,240,256]{2,1,0:T(8,128)(2,1)S(1)}, bf16[8,240,256]{2,1,0:T(8,128)(2,1)S(1)}, u32[]{:S(2)}, u32[]{:S(2)}) collective-permute-start(bf16[8,240,256]{2,1,0:T(8,128)(2,1)S(1)} %get-tuple-element.47), channel_id=1, source_target_pairs={{0,8},{8,0},{16,24},{24,16},{32,40},{40,32},{48,56},{56,48},{64,72... | collective-permute-start | bytes 2949128 | tf_op jit(solution)/shard_map/ppermute | solution.py:340
  57.8 11.5 %collective-permute-start.13 = (bf16[4,192,256]{2,1,0:T(8,128)(2,1)S(1)}, bf16[4,192,256]{2,1,0:T(8,128)(2,1)S(1)}, u32[]{:S(2)}, u32[]{:S(2)}) collective-permute-start(bf16[4,192,256]{2,1,0:T(8,128)(2,1)S(1)} %get-tuple-element.48), channel_id=1, source_target_pairs={{0,1},{1,0},{2,3},{3,2},{4,5},{5,4},{6,7},{7,6},{8,9},{9,8},{10,11... | collective-permute-start | bytes 1179656 | tf_op jit(solution)/shard_map/ppermute | solution.py:337
  70.6 19.8 %all-to-all-start.1 = ((bf16[8,240,256]{2,1,0:T(8,128)(2,1)}), bf16[8,240,256]{2,1,0:T(8,128)(2,1)S(1)}, u32[]{:S(2)}, u32[]{:S(2)}) async-start(bf16[8,240,256]{2,1,0:T(8,128)(2,1)} %join_cols.1.rest_4_), calls=%async_computation.1 | async-start | bytes 1966080 | tf_op jit(solution)/shard_map/all_to_all | solution.py:380
  74.6 4.6 %collective-permute-start.14 = (bf16[4,48,256]{2,1,0:T(8,128)(2,1)S(1)}, bf16[4,48,256]{2,1,0:T(8,128)(2,1)S(1)}, u32[]{:S(2)}, u32[]{:S(2)}) collective-permute-start(bf16[4,48,256]{2,1,0:T(8,128)(2,1)S(1)} %get-tuple-element.49), channel_id=1, source_target_pairs={{0,1},{1,0},{2,3},{3,2},{4,5},{5,4},{6,7},{7,6},{8,9},{9,8},{10,11... | collective-permute-start | bytes 294920 | tf_op jit(solution)/shard_map/ppermute | solution.py:337
  79.3 5.0 %collective-permute-start.15 = (bf16[240,256]{1,0:T(8,128)(2,1)S(1)}, bf16[240,256]{1,0:T(8,128)(2,1)S(1)}, u32[]{:S(2)}, u32[]{:S(2)}) collective-permute-start(bf16[240,256]{1,0:T(8,128)(2,1)S(1)} %get-tuple-element.55), channel_id=1, source_target_pairs={{0,2},{1,3},{2,0},{3,1},{4,6},{5,7},{6,4},{7,5},{8,10},{9,11},{10,... | collective-permute-start | bytes 368648 | tf_op jit(solution)/shard_map/ppermute | solution.py:337
  79.9 6.4 %collective-permute-start.16 = (bf16[240,256]{1,0:T(8,128)(2,1)S(1)}, bf16[240,256]{1,0:T(8,128)(2,1)S(1)}, u32[]{:S(2)}, u32[]{:S(2)}) collective-permute-start(bf16[240,256]{1,0:T(8,128)(2,1)S(1)} %get-tuple-element.56), channel_id=1, source_target_pairs={{0,4},{1,5},{2,6},{3,7},{4,0},{5,1},{6,2},{7,3},{8,12},{9,13},{10,... | collective-permute-start | bytes 368648 | tf_op jit(solution)/shard_map/ppermute | solution.py:337
  82.0 6.1 %collective-permute-start.17 = (bf16[240,256]{1,0:T(8,128)(2,1)S(1)}, bf16[240,256]{1,0:T(8,128)(2,1)S(1)}, u32[]{:S(2)}, u32[]{:S(2)}) collective-permute-start(bf16[240,256]{1,0:T(8,128)(2,1)S(1)} %get-tuple-element.57), channel_id=1, source_target_pairs={{0,6},{1,7},{2,4},{3,5},{4,2},{5,3},{6,0},{7,1},{8,14},{9,15},{10,... | collective-permute-start | bytes 368648 | tf_op jit(solution)/shard_map/ppermute | solution.py:337

commit v6 on v3

--- a/solution.py
+++ b/solution.py
@@ -11,6 +11,7 @@
 F32 = jnp.float32
 BF16 = jnp.bfloat16
 LANES = 128
+FULL, KEPT = 48, 32
 VMEM_MIB = 24
 SMEM = pl.BlockSpec(memory_space=pltpu.SMEM)
 MOVES = (0, 1, 2, -1)
@@ -45,22 +46,70 @@
     return table
 
 
+def fold(block):
+    low, high = block[KEPT : KEPT + 8, :LANES], block[KEPT : KEPT + 8, LANES:]
+    turned = [pltpu.roll(low, 64, 1), low, pltpu.roll(high, 64, 1), jnp.zeros_like(low)]
+    lane = lax.broadcasted_iota(jnp.int32, (KEPT, LANES), 1)
+    spare = jnp.where(lane >= 64, jnp.concatenate(turned, axis=0), block[:KEPT, LANES:])
+    return jnp.concatenate([block[:KEPT, :LANES], spare], axis=1)
+
+
+def unfold(block):
+    lane = lax.broadcasted_iota(jnp.int32, (KEPT, LANES), 1)
+    last = block[:, LANES:]
+    spare = jnp.where(lane >= 64, last, 0.0)
+    top = jnp.concatenate([block[:, :LANES], jnp.where(lane >= 64, 0.0, last)], axis=1)
+    low = pltpu.roll(spare[0:8], 64, 1) + spare[8:16]
+    bottom = jnp.concatenate([low, pltpu.roll(spare[16:24], 64, 1)], axis=1)
+    return jnp.concatenate([top, bottom, jnp.zeros((FULL - KEPT - 8, block.shape[1]), F32)], axis=0)
+
+
+def pack_kernel(source_hbm, target_hbm, feat_hbm, cot_hbm, a_ref, b_ref, source, target, feat, cot, wide, arrived):
+    moves = ((source_hbm, source), (target_hbm, target), (feat_hbm, feat), (cot_hbm, cot))
+    copies = [pltpu.make_async_copy(src, dst, arrived.at[index]) for index, (src, dst) in enumerate(moves)]
+    for copy in copies:
+        copy.start()
+    for copy in copies:
+        copy.wait()
+    own, width = feat.shape
+    for embed, out_ref in ((source, a_ref), (target, b_ref)):
+        wide[...] = jnp.zeros(wide.shape, F32)
+        wide[: embed.shape[0], :own] = embed[...].astype(F32)
+        out_ref[:own, :width] = feat[...]
+        out_ref[:own, width:] = cot[...]
+        out_ref[own:, :] = fold(wide[...]).astype(BF16)
+
+
+def pack(source_embed, target_embed, features, cotangent):
+    own, feat = features.shape
+    shape = (own + KEPT, 2 * feat)
+    arrays = (source_embed, target_embed, features, cotangent)
+    return pl.pallas_call(
+        pack_kernel,
+        in_specs=[pl.BlockSpec(memory_space=pltpu.HBM)] * len(arrays),
+        out_shape=shapes((shape, BF16), (shape, BF16)),
+        scratch_shapes=[pltpu.VMEM(array.shape, BF16) for array in arrays]
+        + [pltpu.VMEM((FULL, 2 * feat), F32), pltpu.SemaphoreType.DMA((len(arrays),))],
+        compiler_params=params(8),
+        name="pack",
+    )(*arrays)
+
+
 def assemble(own, chunk_refs, place_ref, base, parity, pair_ref, turned_ref, nodes_ref):
-    extra = chunk_refs[0].shape[1] - own
     even = parity == 0
-    blank = jnp.zeros((extra, 2 * own - chunk_refs[0].shape[2]), F32)
+    blank = jnp.zeros((FULL, 2 * own - chunk_refs[0].shape[2]), F32)
     for slot, chunk_ref in enumerate(chunk_refs):
         start = place_ref[base + slot] * 2 * own
         for flip in range(2):
             rows = pl.ds(pl.multiple_of(start + (parity ^ flip) * own, 64), own)
             pair_ref[rows, :] = chunk_ref[flip, :own, :]
-        first = chunk_ref[0, own:, :].astype(F32)
-        second = chunk_ref[1, own:, :].astype(F32)
+        first = unfold(chunk_ref[0, own:, :].astype(F32))
+        second = unfold(chunk_ref[1, own:, :].astype(F32))
         left = jnp.concatenate([jnp.where(even, first, second), blank], axis=1)
         right = jnp.concatenate([blank, jnp.where(even, second, first)], axis=1)
         both = left + pltpu.roll(right, own - blank.shape[1], 1)
-        turned_ref[:extra, pl.ds(pl.multiple_of(start, LANES), 2 * own)] = both.astype(BF16)
-    turned_ref[extra:, :] = jnp.zeros((LANES - extra, turned_ref.shape[1]), BF16)
+        turned_ref[:FULL, pl.ds(pl.multiple_of(start, LANES), 2 * own)] = both.astype(BF16)
+    turned_ref[FULL:, :] = jnp.zeros((LANES - FULL, turned_ref.shape[1]), BF16)
     nodes_ref[...] = jnp.transpose(turned_ref[...])
 
 
@@ -196,7 +245,6 @@
         col_sums, target_sums, scores, outer, slots = rest[-5:]
     else:
         cols_ref, source_ref, col_sums, target_sums, scores, outer = rest
-    extra = cols_ref.shape[1] - own
     rows = a_pair.shape[0]
     cols = col_sums.shape[0]
     span = scores.shape[2]
@@ -216,7 +264,7 @@
         grad_half = grad.astype(BF16)
         more_cols = jnp.dot(soft_half, a_pair[part, :], preferred_element_type=F32)
         more_target = jnp.dot(grad_half, a_src[part, :], preferred_element_type=F32)
-        more_source = jnp.dot(b_dst_t[:extra, here], grad_half, preferred_element_type=F32)
+        more_source = jnp.dot(b_dst_t[:FULL, here], grad_half, preferred_element_type=F32)
         col_sums[...] = col_sums[...] + more_cols if index else more_cols
         target_sums[...] = target_sums[...] + more_target if index else more_target
         source_ref[:, part] = start_ref[:, part] + more_source if last else more_source
@@ -231,19 +279,19 @@
         chunk = slice(slot * own, (slot + 1) * own)
         cols_ref[slot, :own, :] = col_sums[chunk, :].astype(BF16)
         wide = jnp.concatenate([target_sums[chunk, :], jnp.zeros((pair - own, LANES), F32)], axis=0)
-        cols_ref[slot, own:, :] = jnp.transpose(wide)[:extra].astype(BF16)
+        cols_ref[slot, own:, :] = fold(jnp.transpose(wide)[:FULL]).astype(BF16)
     if last:
-        fill = jnp.zeros((extra, pair - own), F32)
+        fill = jnp.zeros((FULL, pair - own), F32)
         for chunk in range(slots.shape[0]):
             part = source_ref[:, chunk * own : (chunk + 1) * own]
-            slots[place_ref[10] ^ chunk] = jnp.concatenate([part, fill], axis=1)
+            slots[place_ref[10] ^ chunk] = fold(jnp.concatenate([part, fill], axis=1))
         for slot, piece_ref in enumerate(piece_refs):
             piece_ref[:own, :] = mine_ref[slot]
             piece_ref[own:, :] = slots[2 * slot].astype(BF16)
             twin_ref[slot] = slots[2 * slot + 1].astype(BF16)
 
 
-def tile_sums(place, kept, half, table, late, unread, own, feat, extra, name):
+def tile_sums(place, kept, half, table, late, unread, own, feat, name):
     rows, pair = kept[0].shape
     cols = kept[4].shape[0] // 2
     mates = rows // own
@@ -251,14 +299,14 @@
     scratch = [pltpu.VMEM((cols, pair), F32), pltpu.VMEM((cols, LANES), F32)] + [pltpu.VMEM((2, cols, span), F32)] * 2
     kinds = []
     if half == 0:
-        kinds = [((own + extra, pair), BF16)] * (mates // 2) + [((mates // 2, extra, pair), BF16)]
-        scratch += [pltpu.VMEM((mates, extra, pair), F32)]
+        kinds = [((own + KEPT, pair), BF16)] * (mates // 2) + [((mates // 2, KEPT, pair), BF16)]
+        scratch += [pltpu.VMEM((mates, KEPT, pair), F32)]
     vmem, anywhere = pl.BlockSpec(memory_space=pltpu.VMEM), pl.BlockSpec(memory_space=pl.ANY)
     work = 1 << 20 if half == 0 else 2 * rows * cols * 1280
     return pl.pallas_call(
         functools.partial(tile_kernel, own, feat, half),
         in_specs=[SMEM] + [vmem] * (len(kept) + 1 + len(late)) + [anywhere] * len(unread),
-        out_shape=shapes(((cols // own, own + extra, pair), BF16), ((extra, rows), F32), *kinds),
+        out_shape=shapes(((cols // own, own + KEPT, pair), BF16), ((FULL, rows), F32), *kinds),
         scratch_shapes=scratch,
         compiler_params=params(),
         cost_estimate=pl.CostEstimate(flops=work, bytes_accessed=1 << 20, transcendentals=work >> 11),
@@ -301,8 +349,8 @@
         extra = extra + cols_ref[slot, own:, :].astype(F32)
     hop_ref[...] = total[:, :feat].astype(BF16)
     grad_ref[...] = total[:, feat:].astype(BF16)
-    source_ref[...] = source[:emb_count, :own]
-    target_ref[...] = extra[:emb_count, :own]
+    source_ref[...] = unfold(source)[:emb_count, :own]
+    target_ref[...] = unfold(extra)[:emb_count, :own]
 
 
 def finish(cols, pieces, own, feat, emb_count):
@@ -321,7 +369,6 @@
     emb_count, own = source_embed.shape
     feat = features.shape[1]
     pair = 2 * feat
-    extra = -(-emb_count // 16) * 16
     depth, width = row_size // 4, col_size // 2
     both = ("row", "col")
 
@@ -350,14 +397,10 @@
         ]
         return lax.ppermute(array, both, pairs)
 
-    def pack(embed):
-        left = jnp.pad(features, ((0, extra), (0, feat)))
-        right = jnp.pad(cotangent, ((0, extra), (feat, 0)))
-        return left + right + jnp.pad(embed, ((own, extra - emb_count), (0, pair - own)))
-
     index = lax.axis_index(both)
     place = lax.dynamic_index_in_dim(jnp.asarray(places(row_size, col_size)), index, 0, keepdims=False)
-    chunks, alongs = (pack(target_embed), pack(source_embed)), (along_z, along_x)
+    pack_a, pack_b = pack(source_embed, target_embed, features, cotangent)
+    chunks, alongs = (pack_b, pack_a), (along_z, along_x)
     near = [jnp.stack([chunk, along(chunk, 0, 1)]) for chunk, along in zip(chunks, alongs)]
     near, place = lax.optimization_barrier((near, place))
     moved = [[along(array, -move, 0) for array, along in zip(near, alongs)] for move in MOVES[1:]]
@@ -366,7 +409,7 @@
     scaled, stats, kept = row_stats(place, a_parts, b_parts, others, own, feat)
     stats = lax.all_to_all(stats, "col", 0, 0)
 
-    sizes = (own, feat, extra)
+    sizes = (own, feat)
     table, mine, *given = weigh(place, stats, scaled, own)
     given = [mate(part, 1) for part in given]
     other_cols, start = tile_sums(place, kept, 1, table, (), (), *sizes, "other_tile")

time: 90.7 us -> 91.8 us (1.012)
  local copies, waits for them, and re-layouts: 0.69 us -> 3.73 us
    unnamed x0 -> x8, local copies, waits for them, and re-layouts: none -> 3.04 us
    ppermute x4, starting transfers between devices: 7.46 us -> 5.86 us  [along_x(): return lax.ppermute(array, 'col', pairs)]
    ppermute x4, starting transfers between devices: 8.69 us -> 9.69 us  [along_z(): return lax.ppermute(array, both, pairs)]
where the time goes in v6:
time: 91.8 us; the launch traced here: 91.4 us
  starting transfers between devices  27.6 us (30%)
  Pallas kernels  26.4 us (29%)
  waiting for transfers between devices  23.4 us (25%)
  blocking collectives  9.46 us (10%)
  local copies, waits for them, and re-layouts  3.73 us (4%)
    pallas_call x2, Pallas kernels, tile_sums(): pl.pallas_call(functools.partial(tile_kernel, own, feat, half), in_specs=...  14.1 us
    ppermute x5, waiting for transfers between devices, mate(): return lax.ppermute(array, 'col', [(c, c ^ bits) for c in range(col_size)])  10.4 us
    ppermute x4, starting transfers between devices, along_z(): return lax.ppermute(array, both, pairs)  9.69 us
    all_to_all x1, blocking collectives, local(): stats = lax.all_to_all(stats, 'col', 0, 0)  9.46 us
    pallas_call x1, Pallas kernels, row_stats(): pl.pallas_call(functools.partial(stats_kernel, own, feat), grid=(rows //...  8.73 us
    ppermute x4, waiting for transfers between devices, along_z(): return lax.ppermute(array, both, pairs)  7.25 us
    ppermute x5, starting transfers between devices, mate(): return lax.ppermute(array, 'col', [(c, c ^ bits) for c in range(col_size)])  6.66 us
    ppermute x4, starting transfers between devices, along_x(): return lax.ppermute(array, 'col', pairs)  5.86 us
  transfers between devices with their start and end apart: 19, of which 13 were waited for; matrix products, arithmetic and copies ran while one was open for 1% of the time, Pallas kernels for 8%

profile of v6, /device:TPU:0, one launch (start us, length us, event | category | flops | bytes accessed | tf_op | source)
XLA Modules:
  0.0 91.4 jit_solution(11685467106685475116)
XLA Ops:
  0.6 0.8 copy-done
  1.4 0.8 copy-done.1
  2.2 0.7 copy-done.2
  3.0 0.7 copy-done.3
  3.7 0.3 pack.1
  4.0 3.2 %collective-permute-start = (bf16[224,256]{1,0:T(8,128)(2,1)S(1)}, bf16[224,256]{1,0:T(8,128)(2,1)S(1)}, u32[]{:S(2)}, u32[]{:S(2)}) collective-permute-start(bf16[224,256]{1,0:T(8,128)(2,1)S(1)} %get-tuple-element.33), channel_id=1, source_target_pairs={{0,17},{1,16},{2,19},{3,18},{4,21},{5,20},{6,23},{7,22},{8,25},{9,... | collective-permute-start | bytes 344072 | tf_op jit(solution)/shard_map/ppermute | solution.py:398
  7.1 0.1 collective-permute-start.1
  7.3 0.7 dynamic-slice_bitcast_fusion.place_ref
  8.0 2.3 %collective-permute-done = bf16[224,256]{1,0:T(8,128)(2,1)S(1)} collective-permute-done((bf16[224,256]{1,0:T(8,128)(2,1)S(1)}, bf16[224,256]{1,0:T(8,128)(2,1)S(1)}, u32[]{:S(2)}, u32[]{:S(2)}) %collective-permute-start) | collective-permute-done | bytes 114720 | tf_op jit(solution)/shard_map/ppermute | solution.py:398
  10.3 1.6 %collective-permute-done.1 = bf16[224,256]{1,0:T(8,128)(2,1)S(1)} collective-permute-done((bf16[224,256]{1,0:T(8,128)(2,1)S(1)}, bf16[224,256]{1,0:T(8,128)(2,1)S(1)}, u32[]{:S(2)}, u32[]{:S(2)}) %collective-permute-start.1) | collective-permute-done | bytes 114720 | tf_op jit(solution)/shard_map/ppermute | solution.py:391
  12.0 1.6 %collective-permute-start.6 = (bf16[2,224,256]{2,1,0:T(8,128)(2,1)S(1)}, bf16[2,224,256]{2,1,0:T(8,128)(2,1)S(1)}, u32[]{:S(2)}, u32[]{:S(2)}) collective-permute-start(bf16[2,224,256]{2,1,0:T(8,128)(2,1)S(1)} %pad_maximum_fusion.1.rest_0_), channel_id=1, source_target_pairs={{0,2},{1,3},{2,4},{3,5},{4,6},{5,7},{6,0},{7,1},{8,10},{9,11},{10,... | collective-permute-start | bytes 688136 | tf_op jit(solution)/shard_map/ppermute | solution.py:391
  13.5 2.7 %collective-permute-start.4 = (bf16[2,224,256]{2,1,0:T(8,128)(2,1)S(1)}, bf16[2,224,256]{2,1,0:T(8,128)(2,1)S(1)}, u32[]{:S(2)}, u32[]{:S(2)}) collective-permute-start(bf16[2,224,256]{2,1,0:T(8,128)(2,1)S(1)} %pad_maximum_fusion.1.rest_0_), channel_id=1, source_target_pairs={{0,4},{1,5},{2,6},{3,7},{4,0},{5,1},{6,2},{7,3},{8,12},{9,13},{10,... | collective-permute-start | bytes 688136 | tf_op jit(solution)/shard_map/ppermute | solution.py:391
  16.3 1.9 %collective-permute-start.7 = (bf16[2,224,256]{2,1,0:T(8,128)(2,1)S(1)}, bf16[2,224,256]{2,1,0:T(8,128)(2,1)S(1)}, u32[]{:S(2)}, u32[]{:S(2)}) collective-permute-start(bf16[2,224,256]{2,1,0:T(8,128)(2,1)S(1)} %pad_maximum_fusion.rest_1_), channel_id=1, source_target_pairs={{0,32},{1,33},{2,34},{3,35},{4,36},{5,37},{6,38},{7,39},{8,40},{9,... | collective-permute-start | bytes 688136 | tf_op jit(solution)/shard_map/ppermute | solution.py:398
  18.2 3.6 %collective-permute-start.5 = (bf16[2,224,256]{2,1,0:T(8,128)(2,1)S(1)}, bf16[2,224,256]{2,1,0:T(8,128)(2,1)S(1)}, u32[]{:S(2)}, u32[]{:S(2)}) collective-permute-start(bf16[2,224,256]{2,1,0:T(8,128)(2,1)S(1)} %pad_maximum_fusion.rest_1_), channel_id=1, source_target_pairs={{0,64},{1,65},{2,66},{3,67},{4,68},{5,69},{6,70},{7,71},{8,72},{9,... | collective-permute-start | bytes 688136 | tf_op jit(solution)/shard_map/ppermute | solution.py:398
  21.8 1.0 %collective-permute-start.3 = (bf16[2,224,256]{2,1,0:T(8,128)(2,1)S(1)}, bf16[2,224,256]{2,1,0:T(8,128)(2,1)S(1)}, u32[]{:S(2)}, u32[]{:S(2)}) collective-permute-start(bf16[2,224,256]{2,1,0:T(8,128)(2,1)S(1)} %pad_maximum_fusion.rest_1_), channel_id=1, source_target_pairs={{0,96},{1,97},{2,98},{3,99},{4,100},{5,101},{6,102},{7,103},{8,104... | collective-permute-start | bytes 688136 | tf_op jit(solution)/shard_map/ppermute | solution.py:398
  22.8 0.0 collective-permute-done.6.rest_6_
  22.8 1.4 %collective-permute-start.2 = (bf16[2,224,256]{2,1,0:T(8,128)(2,1)S(1)}, bf16[2,224,256]{2,1,0:T(8,128)(2,1)S(1)}, u32[]{:S(2)}, u32[]{:S(2)}) collective-permute-start(bf16[2,224,256]{2,1,0:T(8,128)(2,1)S(1)} %pad_maximum_fusion.1.rest_0_), channel_id=1, source_target_pairs={{0,6},{1,7},{2,0},{3,1},{4,2},{5,3},{6,4},{7,5},{8,14},{9,15},{10,... | collective-permute-start | bytes 688136 | tf_op jit(solution)/shard_map/ppermute | solution.py:391
  24.2 0.9 %collective-permute-done.4.rest_4_ = bf16[2,224,256]{2,1,0:T(8,128)(2,1)S(1)} collective-permute-done((bf16[2,224,256]{2,1,0:T(8,128)(2,1)S(1)}, bf16[2,224,256]{2,1,0:T(8,128)(2,1)S(1)}, u32[]{:S(2)}, u32[]{:S(2)}) %collective-permute-start.4) | collective-permute-done | bytes 229408 | tf_op jit(solution)/shard_map/ppermute | solution.py:391
  25.1 0.0 collective-permute-start.8
  25.1 1.4 %collective-permute-done.7.rest_7_ = bf16[2,224,256]{2,1,0:T(8,128)(2,1)S(1)} collective-permute-done((bf16[2,224,256]{2,1,0:T(8,128)(2,1)S(1)}, bf16[2,224,256]{2,1,0:T(8,128)(2,1)S(1)}, u32[]{:S(2)}, u32[]{:S(2)}) %collective-permute-start.7) | collective-permute-done | bytes 229408 | tf_op jit(solution)/shard_map/ppermute | solution.py:398
  26.6 0.0 collective-permute-start.11
  26.6 3.5 %collective-permute-done.5.rest_5_ = bf16[2,224,256]{2,1,0:T(8,128)(2,1)S(1)} collective-permute-done((bf16[2,224,256]{2,1,0:T(8,128)(2,1)S(1)}, bf16[2,224,256]{2,1,0:T(8,128)(2,1)S(1)}, u32[]{:S(2)}, u32[]{:S(2)}) %collective-permute-start.5) | collective-permute-done | bytes 229408 | tf_op jit(solution)/shard_map/ppermute | solution.py:398
  30.1 0.0 collective-permute-start.10
  30.1 0.5 collective-permute-start.9
  30.6 1.0 %collective-permute-done.10.rest_10_ = bf16[2,224,256]{2,1,0:T(8,128)(2,1)S(1)} collective-permute-done((bf16[2,224,256]{2,1,0:T(8,128)(2,1)S(1)}, bf16[2,224,256]{2,1,0:T(8,128)(2,1)S(1)}, u32[]{:S(2)}, u32[]{:S(2)}) %collective-permute-start.10) | collective-permute-done | bytes 229408 | tf_op jit(solution)/shard_map/ppermute | solution.py:387
  31.6 0.3 collective-permute-done.9.rest_9_
  31.9 8.7 %row_stats.1 = (bf16[1536,256]{1,0:T(8,128)(2,1)S(1)}, f32[8,4,1536]{2,1,0:T(4,128)S(1)}, bf16[1536,256]{1,0:T(8,128)(2,1)S(1)}, bf16[256,1536]{1,0:T(8,128)(2,1...) custom-call(s32[16]{0:T(128)S(1)} %dynamic-slice_bitcast_fusion.plac, ...), custom_call_target="tpu_custom_call" | custom-call | flops 4831838208 | bytes 8388608 | tf_op jit(solution)/shard_map/row_stats/pallas_call | solution.py:189
  40.6 9.5 %all_to_all.10.stats_ref = f32[8,4,1536]{2,1,0:T(4,128)S(1)} all-to-all(f32[8,4,1536]{2,1,0:T(4,128)S(1)} %get-tuple-element.45), channel_id=1, replica_groups=mesh['row'=16,'col'=8] {'col'}, dimensions={0} | all-to-all | bytes 393216 | tf_op jit(solution)/shard_map/all_to_all | solution.py:410
  50.1 1.2 %weigh.1 = (f32[8,1536]{1,0:T(8,128)S(1)}, bf16[4,192,256]{2,1,0:T(8,128)(2,1)S(1)}, bf16[4,192,256]{2,1,0:T(8,128)(2,1)S(1)}) custom-call(s32[16]{0:T(128)S(1)} %dynamic-slice_bitcast_fusion.place_ref, f32[8,4,1536]{2,1,0:T(4,128)S(1)} %all_to_all.10.stats_ref, bf16[1536,256]{1,0:T(8,128)(2,1)S(1)} %get-tuple-element.46.scaled_ref), custom_call_target="tpu_custom_call" | custom-call | tf_op jit(solution)/shard_map/weigh/pallas_call | solution.py:230
  51.3 6.7 %other_tile.1 = (bf16[8,224,256]{2,1,0:T(8,128)(2,1)S(1)}, f32[48,1536]{1,0:T(8,128)S(1)}) custom-call(s32[16]{0:T(128)S(1)} %dynamic-slice_bitcast_fusion.place_ref, bf16[1536,256]{1,0:T(8,128)(2,1)S(1)} %get-tuple-element.38.a_pair, bf16[256,1536]{1,0:T(8,128)(2,1)S(1)} %get-tuple-element.39.a_pair_t, bf16[1536,128]{1,0:T(8,128)(2,1)S(1)} %get-tuple-element.40.a_src, ...), custom_call_target="tpu_custom_call" | custom-call | flops 6039797760 | bytes 1048576 | tf_op jit(solution)/shard_map/other_tile/pallas_call | solution.py:306
  58.0 0.1 collective-permute-start.12
  58.0 1.3 %collective-permute-start.13 = (bf16[4,192,256]{2,1,0:T(8,128)(2,1)S(1)}, bf16[4,192,256]{2,1,0:T(8,128)(2,1)S(1)}, u32[]{:S(2)}, u32[]{:S(2)}) collective-permute-start(bf16[4,192,256]{2,1,0:T(8,128)(2,1)S(1)} %get-tuple-element.52), channel_id=1, source_target_pairs={{0,1},{1,0},{2,3},{3,2},{4,5},{5,4},{6,7},{7,6},{8,9},{9,8},{10,11... | collective-permute-start | bytes 1179656 | tf_op jit(solution)/shard_map/ppermute | solution.py:384
  59.4 7.5 %own_tile.1 = (bf16[8,224,256]{2,1,0:T(8,128)(2,1)S(1)}, f32[48,1536]{1,0:T(8,128)}, bf16[224,256]{1,0:T(8,128)(2,1)S(1)}, bf16[224,256]{1,0:T(8,128)(2,1)S(1)},...) custom-call(s32[16]{0:T(128)S(1)} %dynamic-slice_bitcast_fusion.place_ref, ...), custom_call_target="tpu_custom_call" | custom-call | flops 1048576 | bytes 1048576 | tf_op jit(solution)/shard_map/own_tile/pallas_call | solution.py:306
  66.9 2.7 %collective-permute-done.13.unread_ref.given_ref = bf16[4,192,256]{2,1,0:T(8,128)(2,1)S(1)} collective-permute-done((bf16[4,192,256]{2,1,0:T(8,128)(2,1)S(1)}, bf16[4,192,256]{2,1,0:T(8,128)(2,1)S(1)}, u32[]{:S(2)}, u32[]{:S(2)}) %collective-permute-start.13) | collective-permute-done | bytes 393248 | tf_op jit(solution)/shard_map/ppermute | solution.py:384
  69.6 0.0 collective-permute-done.12.other_ref
  69.6 1.1 %join_cols.1.rest_4_ = bf16[8,224,256]{2,1,0:T(8,128)(2,1)} custom-call(bf16[8,224,256]{2,1,0:T(8,128)(2,1)S(1)} %get-tuple-element.50.own_ref, bf16[8,224,256]{2,1,0:T(8,128)(2,1)S(1)} %collective-permute-done.12.other_ref, bf16[4,192,256]{2,1,0:T(8,128)(2,1)S(1)} %collective-permute-done.13.unread_ref.given_ref), custom_call_target="tpu_custom_call" | custom-call | tf_op jit(solution)/shard_map/join_cols/pallas_call | solution.py:330
  70.7 4.8 %all-to-all-start.1 = ((bf16[8,224,256]{2,1,0:T(8,128)(2,1)}), bf16[8,224,256]{2,1,0:T(8,128)(2,1)S(1)}, u32[]{:S(2)}, u32[]{:S(2)}) async-start(bf16[8,224,256]{2,1,0:T(8,128)(2,1)} %join_cols.1.rest_4_), calls=%async_computation.1 | async-start | bytes 1835008 | tf_op jit(solution)/shard_map/all_to_all | solution.py:421
  75.5 0.5 collective-permute-start.14
  76.0 3.7 %collective-permute-done.14.twin_ref = bf16[4,32,256]{2,1,0:T(8,128)(2,1)S(1)} collective-permute-done((bf16[4,32,256]{2,1,0:T(8,128)(2,1)S(1)}, bf16[4,32,256]{2,1,0:T(8,128)(2,1)S(1)}, u32[]{:S(2)}, u32[]{:S(2)}) %collective-permute-start.14) | collective-permute-done | bytes 65568 | tf_op jit(solution)/shard_map/ppermute | solution.py:384
  79.7 0.1 join_rows.1
  79.8 0.7 collective-permute-start.15
  80.5 2.1 %collective-permute-start.16 = (bf16[224,256]{1,0:T(8,128)(2,1)S(1)}, bf16[224,256]{1,0:T(8,128)(2,1)S(1)}, u32[]{:S(2)}, u32[]{:S(2)}) collective-permute-start(bf16[224,256]{1,0:T(8,128)(2,1)S(1)} %get-tuple-element.60), channel_id=1, source_target_pairs={{0,4},{1,5},{2,6},{3,7},{4,0},{5,1},{6,2},{7,3},{8,12},{9,13},{10,... | collective-permute-start | bytes 344072 | tf_op jit(solution)/shard_map/ppermute | solution.py:384
  82.6 2.1 %collective-permute-start.17 = (bf16[224,256]{1,0:T(8,128)(2,1)S(1)}, bf16[224,256]{1,0:T(8,128)(2,1)S(1)}, u32[]{:S(2)}, u32[]{:S(2)}) collective-permute-start(bf16[224,256]{1,0:T(8,128)(2,1)S(1)} %get-tuple-element.61), channel_id=1, source_target_pairs={{0,6},{1,7},{2,4},{3,5},{4,2},{5,3},{6,0},{7,1},{8,14},{9,15},{10,... | collective-permute-start | bytes 344072 | tf_op jit(solution)/shard_map/ppermute | solution.py:384
  84.6 0.1 collective-permute-done.15.rest_1_
  84.7 2.1 %collective-permute-done.16.rest_2_ = bf16[224,256]{1,0:T(8,128)(2,1)S(1)} collective-permute-done((bf16[224,256]{1,0:T(8,128)(2,1)S(1)}, bf16[224,256]{1,0:T(8,128)(2,1)S(1)}, u32[]{:S(2)}, u32[]{:S(2)}) %collective-permute-start.16) | collective-permute-done | bytes 114720 | tf_op jit(solution)/shard_map/ppermute | solution.py:384
  86.8 1.8 %collective-permute-done.17.rest_3_ = bf16[224,256]{1,0:T(8,128)(2,1)S(1)} collective-permute-done((bf16[224,256]{1,0:T(8,128)(2,1)S(1)}, bf16[224,256]{1,0:T(8,128)(2,1)S(1)}, u32[]{:S(2)}, u32[]{:S(2)}) %collective-permute-start.17) | collective-permute-done | bytes 114720 | tf_op jit(solution)/shard_map/ppermute | solution.py:384
  88.6 1.9 %all-to-all-done.1.cols_ref = bf16[8,224,256]{2,1,0:T(8,128)(2,1)S(1)} async-done(((bf16[8,224,256]{2,1,0:T(8,128)(2,1)}), bf16[8,224,256]{2,1,0:T(8,128)(2,1)S(1)}, u32[]{:S(2)}, u32[]{:S(2)}) %all-to-all-start.1) | async-done | bytes 917536 | tf_op jit(solution)/shard_map/all_to_all | solution.py:421
  90.5 0.8 finish.1
  (10 shorter events, 0.1 us)
Async XLA Ops:
  0.6 0.8 copy-start
  1.4 0.8 copy-start.1
  2.2 0.7 copy-start.2
  3.0 0.7 copy-start.3
  4.0 6.3 %collective-permute-start = (bf16[224,256]{1,0:T(8,128)(2,1)S(1)}, bf16[224,256]{1,0:T(8,128)(2,1)S(1)}, u32[]{:S(2)}, u32[]{:S(2)}) collective-permute-start(bf16[224,256]{1,0:T(8,128)(2,1)S(1)} %get-tuple-element.33), channel_id=1, source_target_pairs={{0,17},{1,16},{2,19},{3,18},{4,21},{5,20},{6,23},{7,22},{8,25},{9,... | collective-permute-start | bytes 344072 | tf_op jit(solution)/shard_map/ppermute | solution.py:398
  7.1 4.8 %collective-permute-start.1 = (bf16[224,256]{1,0:T(8,128)(2,1)S(1)}, bf16[224,256]{1,0:T(8,128)(2,1)S(1)}, u32[]{:S(2)}, u32[]{:S(2)}) collective-permute-start(bf16[224,256]{1,0:T(8,128)(2,1)S(1)} %get-tuple-element.34), channel_id=1, source_target_pairs={{0,1},{1,0},{2,3},{3,2},{4,5},{5,4},{6,7},{7,6},{8,9},{9,8},{10,11... | collective-permute-start | bytes 344072 | tf_op jit(solution)/shard_map/ppermute | solution.py:391
  12.0 10.8 %collective-permute-start.6 = (bf16[2,224,256]{2,1,0:T(8,128)(2,1)S(1)}, bf16[2,224,256]{2,1,0:T(8,128)(2,1)S(1)}, u32[]{:S(2)}, u32[]{:S(2)}) collective-permute-start(bf16[2,224,256]{2,1,0:T(8,128)(2,1)S(1)} %pad_maximum_fusion.1.rest_0_), channel_id=1, source_target_pairs={{0,2},{1,3},{2,4},{3,5},{4,6},{5,7},{6,0},{7,1},{8,10},{9,11},{10,... | collective-permute-start | bytes 688136 | tf_op jit(solution)/shard_map/ppermute | solution.py:391
  13.5 11.6 %collective-permute-start.4 = (bf16[2,224,256]{2,1,0:T(8,128)(2,1)S(1)}, bf16[2,224,256]{2,1,0:T(8,128)(2,1)S(1)}, u32[]{:S(2)}, u32[]{:S(2)}) collective-permute-start(bf16[2,224,256]{2,1,0:T(8,128)(2,1)S(1)} %pad_maximum_fusion.1.rest_0_), channel_id=1, source_target_pairs={{0,4},{1,5},{2,6},{3,7},{4,0},{5,1},{6,2},{7,3},{8,12},{9,13},{10,... | collective-permute-start | bytes 688136 | tf_op jit(solution)/shard_map/ppermute | solution.py:391
  16.3 10.3 %collective-permute-start.7 = (bf16[2,224,256]{2,1,0:T(8,128)(2,1)S(1)}, bf16[2,224,256]{2,1,0:T(8,128)(2,1)S(1)}, u32[]{:S(2)}, u32[]{:S(2)}) collective-permute-start(bf16[2,224,256]{2,1,0:T(8,128)(2,1)S(1)} %pad_maximum_fusion.rest_1_), channel_id=1, source_target_pairs={{0,32},{1,33},{2,34},{3,35},{4,36},{5,37},{6,38},{7,39},{8,40},{9,... | collective-permute-start | bytes 688136 | tf_op jit(solution)/shard_map/ppermute | solution.py:398
  18.2 11.9 %collective-permute-start.5 = (bf16[2,224,256]{2,1,0:T(8,128)(2,1)S(1)}, bf16[2,224,256]{2,1,0:T(8,128)(2,1)S(1)}, u32[]{:S(2)}, u32[]{:S(2)}) collective-permute-start(bf16[2,224,256]{2,1,0:T(8,128)(2,1)S(1)} %pad_maximum_fusion.rest_1_), channel_id=1, source_target_pairs={{0,64},{1,65},{2,66},{3,67},{4,68},{5,69},{6,70},{7,71},{8,72},{9,... | collective-permute-start | bytes 688136 | tf_op jit(solution)/shard_map/ppermute | solution.py:398
  21.8 8.3 %collective-permute-start.3 = (bf16[2,224,256]{2,1,0:T(8,128)(2,1)S(1)}, bf16[2,224,256]{2,1,0:T(8,128)(2,1)S(1)}, u32[]{:S(2)}, u32[]{:S(2)}) collective-permute-start(bf16[2,224,256]{2,1,0:T(8,128)(2,1)S(1)} %pad_maximum_fusion.rest_1_), channel_id=1, source_target_pairs={{0,96},{1,97},{2,98},{3,99},{4,100},{5,101},{6,102},{7,103},{8,104... | collective-permute-start | bytes 688136 | tf_op jit(solution)/shard_map/ppermute | solution.py:398
  22.8 7.8 %collective-permute-start.2 = (bf16[2,224,256]{2,1,0:T(8,128)(2,1)S(1)}, bf16[2,224,256]{2,1,0:T(8,128)(2,1)S(1)}, u32[]{:S(2)}, u32[]{:S(2)}) collective-permute-start(bf16[2,224,256]{2,1,0:T(8,128)(2,1)S(1)} %pad_maximum_fusion.1.rest_0_), channel_id=1, source_target_pairs={{0,6},{1,7},{2,0},{3,1},{4,2},{5,3},{6,4},{7,5},{8,14},{9,15},{10,... | collective-permute-start | bytes 688136 | tf_op jit(solution)/shard_map/ppermute | solution.py:391
  25.1 5.5 %collective-permute-start.8 = (bf16[2,224,256]{2,1,0:T(8,128)(2,1)S(1)}, bf16[2,224,256]{2,1,0:T(8,128)(2,1)S(1)}, u32[]{:S(2)}, u32[]{:S(2)}) collective-permute-start(bf16[2,224,256]{2,1,0:T(8,128)(2,1)S(1)} %pad_maximum_fusion.rest_1_), channel_id=1, source_target_pairs={{0,8},{8,0},{16,24},{24,16},{32,40},{40,32},{48,56},{56,48},{64,72... | collective-permute-start | bytes 688136 | tf_op jit(solution)/shard_map/ppermute | solution.py:387
  26.6 4.0 %collective-permute-start.11 = (bf16[2,224,256]{2,1,0:T(8,128)(2,1)S(1)}, bf16[2,224,256]{2,1,0:T(8,128)(2,1)S(1)}, u32[]{:S(2)}, u32[]{:S(2)}) collective-permute-start(bf16[2,224,256]{2,1,0:T(8,128)(2,1)S(1)} %collective-permute-done.7.rest_7_), channel_id=1, source_target_pairs={{0,8},{8,0},{16,24},{24,16},{32,40},{40,32},{48,56},{56,48},{64,72... | collective-permute-start | bytes 688136 | tf_op jit(solution)/shard_map/ppermute | solution.py:387
  30.1 1.5 %collective-permute-start.10 = (bf16[2,224,256]{2,1,0:T(8,128)(2,1)S(1)}, bf16[2,224,256]{2,1,0:T(8,128)(2,1)S(1)}, u32[]{:S(2)}, u32[]{:S(2)}) collective-permute-start(bf16[2,224,256]{2,1,0:T(8,128)(2,1)S(1)} %collective-permute-done.5.rest_5_), channel_id=1, source_target_pairs={{0,8},{8,0},{16,24},{24,16},{32,40},{40,32},{48,56},{56,48},{64,72... | collective-permute-start | bytes 688136 | tf_op jit(solution)/shard_map/ppermute | solution.py:387
  30.1 1.8 %collective-permute-start.9 = (bf16[2,224,256]{2,1,0:T(8,128)(2,1)S(1)}, bf16[2,224,256]{2,1,0:T(8,128)(2,1)S(1)}, u32[]{:S(2)}, u32[]{:S(2)}) collective-permute-start(bf16[2,224,256]{2,1,0:T(8,128)(2,1)S(1)} %collective-permute-done.3.rest_3_), channel_id=1, source_target_pairs={{0,8},{8,0},{16,24},{24,16},{32,40},{40,32},{48,56},{56,48},{64,72... | collective-permute-start | bytes 688136 | tf_op jit(solution)/shard_map/ppermute | solution.py:387
  58.0 11.6 %collective-permute-start.12 = (bf16[8,224,256]{2,1,0:T(8,128)(2,1)S(1)}, bf16[8,224,256]{2,1,0:T(8,128)(2,1)S(1)}, u32[]{:S(2)}, u32[]{:S(2)}) collective-permute-start(bf16[8,224,256]{2,1,0:T(8,128)(2,1)S(1)} %get-tuple-element.51), channel_id=1, source_target_pairs={{0,8},{8,0},{16,24},{24,16},{32,40},{40,32},{48,56},{56,48},{64,72... | collective-permute-start | bytes 2752520 | tf_op jit(solution)/shard_map/ppermute | solution.py:387
  58.0 11.5 %collective-permute-start.13 = (bf16[4,192,256]{2,1,0:T(8,128)(2,1)S(1)}, bf16[4,192,256]{2,1,0:T(8,128)(2,1)S(1)}, u32[]{:S(2)}, u32[]{:S(2)}) collective-permute-start(bf16[4,192,256]{2,1,0:T(8,128)(2,1)S(1)} %get-tuple-element.52), channel_id=1, source_target_pairs={{0,1},{1,0},{2,3},{3,2},{4,5},{5,4},{6,7},{7,6},{8,9},{9,8},{10,11... | collective-permute-start | bytes 1179656 | tf_op jit(solution)/shard_map/ppermute | solution.py:384
  70.7 19.8 %all-to-all-start.1 = ((bf16[8,224,256]{2,1,0:T(8,128)(2,1)}), bf16[8,224,256]{2,1,0:T(8,128)(2,1)S(1)}, u32[]{:S(2)}, u32[]{:S(2)}) async-start(bf16[8,224,256]{2,1,0:T(8,128)(2,1)} %join_cols.1.rest_4_), calls=%async_computation.1 | async-start | bytes 1835008 | tf_op jit(solution)/shard_map/all_to_all | solution.py:421
  75.5 4.3 %collective-permute-start.14 = (bf16[4,32,256]{2,1,0:T(8,128)(2,1)S(1)}, bf16[4,32,256]{2,1,0:T(8,128)(2,1)S(1)}, u32[]{:S(2)}, u32[]{:S(2)}) collective-permute-start(bf16[4,32,256]{2,1,0:T(8,128)(2,1)S(1)} %get-tuple-element.53), channel_id=1, source_target_pairs={{0,1},{1,0},{2,3},{3,2},{4,5},{5,4},{6,7},{7,6},{8,9},{9,8},{10,11... | collective-permute-start | bytes 196616 | tf_op jit(solution)/shard_map/ppermute | solution.py:384
  79.8 4.9 %collective-permute-start.15 = (bf16[224,256]{1,0:T(8,128)(2,1)S(1)}, bf16[224,256]{1,0:T(8,128)(2,1)S(1)}, u32[]{:S(2)}, u32[]{:S(2)}) collective-permute-start(bf16[224,256]{1,0:T(8,128)(2,1)S(1)} %get-tuple-element.59), channel_id=1, source_target_pairs={{0,2},{1,3},{2,0},{3,1},{4,6},{5,7},{6,4},{7,5},{8,10},{9,11},{10,... | collective-permute-start | bytes 344072 | tf_op jit(solution)/shard_map/ppermute | solution.py:384
  80.5 6.3 %collective-permute-start.16 = (bf16[224,256]{1,0:T(8,128)(2,1)S(1)}, bf16[224,256]{1,0:T(8,128)(2,1)S(1)}, u32[]{:S(2)}, u32[]{:S(2)}) collective-permute-start(bf16[224,256]{1,0:T(8,128)(2,1)S(1)} %get-tuple-element.60), channel_id=1, source_target_pairs={{0,4},{1,5},{2,6},{3,7},{4,0},{5,1},{6,2},{7,3},{8,12},{9,13},{10,... | collective-permute-start | bytes 344072 | tf_op jit(solution)/shard_map/ppermute | solution.py:384
  82.6 6.0 %collective-permute-start.17 = (bf16[224,256]{1,0:T(8,128)(2,1)S(1)}, bf16[224,256]{1,0:T(8,128)(2,1)S(1)}, u32[]{:S(2)}, u32[]{:S(2)}) collective-permute-start(bf16[224,256]{1,0:T(8,128)(2,1)S(1)} %get-tuple-element.61), channel_id=1, source_target_pairs={{0,6},{1,7},{2,4},{3,5},{4,2},{5,3},{6,0},{7,1},{8,14},{9,15},{10,... | collective-permute-start | bytes 344072 | tf_op jit(solution)/shard_map/ppermute | solution.py:384

commit v7 on v6

--- a/solution.py
+++ b/solution.py
@@ -62,37 +62,6 @@
     low = pltpu.roll(spare[0:8], 64, 1) + spare[8:16]
     bottom = jnp.concatenate([low, pltpu.roll(spare[16:24], 64, 1)], axis=1)
     return jnp.concatenate([top, bottom, jnp.zeros((FULL - KEPT - 8, block.shape[1]), F32)], axis=0)
-
-
-def pack_kernel(source_hbm, target_hbm, feat_hbm, cot_hbm, a_ref, b_ref, source, target, feat, cot, wide, arrived):
-    moves = ((source_hbm, source), (target_hbm, target), (feat_hbm, feat), (cot_hbm, cot))
-    copies = [pltpu.make_async_copy(src, dst, arrived.at[index]) for index, (src, dst) in enumerate(moves)]
-    for copy in copies:
-        copy.start()
-    for copy in copies:
-        copy.wait()
-    own, width = feat.shape
-    for embed, out_ref in ((source, a_ref), (target, b_ref)):
-        wide[...] = jnp.zeros(wide.shape, F32)
-        wide[: embed.shape[0], :own] = embed[...].astype(F32)
-        out_ref[:own, :width] = feat[...]
-        out_ref[:own, width:] = cot[...]
-        out_ref[own:, :] = fold(wide[...]).astype(BF16)
-
-
-def pack(source_embed, target_embed, features, cotangent):
-    own, feat = features.shape
-    shape = (own + KEPT, 2 * feat)
-    arrays = (source_embed, target_embed, features, cotangent)
-    return pl.pallas_call(
-        pack_kernel,
-        in_specs=[pl.BlockSpec(memory_space=pltpu.HBM)] * len(arrays),
-        out_shape=shapes((shape, BF16), (shape, BF16)),
-        scratch_shapes=[pltpu.VMEM(array.shape, BF16) for array in arrays]
-        + [pltpu.VMEM((FULL, 2 * feat), F32), pltpu.SemaphoreType.DMA((len(arrays),))],
-        compiler_params=params(8),
-        name="pack",
-    )(*arrays)
 
 
 def assemble(own, chunk_refs, place_ref, base, parity, pair_ref, turned_ref, nodes_ref):
@@ -397,10 +366,25 @@
         ]
         return lax.ppermute(array, both, pairs)
 
+    row = lax.broadcasted_iota(jnp.int32, (own + KEPT, pair), 0)
+    lane = lax.broadcasted_iota(jnp.int32, (own + KEPT, pair), 1)
+
+    def pack(embed):
+        def place(down, right):
+            room = ((down, own + KEPT - emb_count - down, 0), (right, pair - own - right, 0))
+            return lax.pad(embed, jnp.zeros((), BF16), room)
+
+        total = jnp.pad(features, ((0, KEPT), (0, feat))) + jnp.pad(cotangent, ((0, KEPT), (feat, 0)))
+        total = total + place(own, 0)
+        for part in range(3):
+            top = own + 8 * part
+            here = (row >= top) & (row < top + 8) & (lane >= own)
+            total = jnp.where(here, place(top - KEPT, own - 64 * part), total)
+        return total
+
     index = lax.axis_index(both)
     place = lax.dynamic_index_in_dim(jnp.asarray(places(row_size, col_size)), index, 0, keepdims=False)
-    pack_a, pack_b = pack(source_embed, target_embed, features, cotangent)
-    chunks, alongs = (pack_b, pack_a), (along_z, along_x)
+    chunks, alongs = (pack(target_embed), pack(source_embed)), (along_z, along_x)
     near = [jnp.stack([chunk, along(chunk, 0, 1)]) for chunk, along in zip(chunks, alongs)]
     near, place = lax.optimization_barrier((near, place))
     moved = [[along(array, -move, 0) for array, along in zip(near, alongs)] for move in MOVES[1:]]

time: 91.8 us -> 89.5 us (0.975)
  local copies, waits for them, and re-layouts: 3.73 us -> 0.69 us
  other arithmetic: 0.05 us -> 1.15 us
    unnamed x8 -> x0, local copies, waits for them, and re-layouts: 3.04 us -> none
    ppermute x4, starting transfers between devices: 5.86 us -> 7.46 us  [along_x(): return lax.ppermute(array, 'col', pairs)]
    ppermute x4, waiting for transfers between devices: 2.54 us -> 1.13 us  [along_x(): return lax.ppermute(array, 'col', pairs)]
    select_n x0 -> x1, other arithmetic: none -> 1.08 us  [pack(): total = jnp.where(here, place(top - KEPT, own - 64 * part), total)]
    ppermute x4, starting transfers between devices: 9.69 us -> 8.69 us  [along_z(): return lax.ppermute(array, both, pairs)]
where the time goes in v7:
time: 89.5 us; the launch traced here: 89.2 us
  starting transfers between devices  28.5 us (32%)
  Pallas kernels  26.2 us (29%)
  waiting for transfers between devices  22.5 us (25%)
  blocking collectives  9.44 us (11%)
  other arithmetic  1.15 us (1%)
    pallas_call x2, Pallas kernels, tile_sums(): pl.pallas_call(functools.partial(tile_kernel, own, feat, half), in_specs=...  14.1 us
    ppermute x5, waiting for transfers between devices, mate(): return lax.ppermute(array, 'col', [(c, c ^ bits) for c in range(col_size)])  10.4 us
    all_to_all x1, blocking collectives, local(): stats = lax.all_to_all(stats, 'col', 0, 0)  9.44 us
    pallas_call x1, Pallas kernels, row_stats(): pl.pallas_call(functools.partial(stats_kernel, own, feat), grid=(rows //...  8.74 us
    ppermute x4, starting transfers between devices, along_z(): return lax.ppermute(array, both, pairs)  8.69 us
    ppermute x4, waiting for transfers between devices, along_z(): return lax.ppermute(array, both, pairs)  7.77 us
    ppermute x4, starting transfers between devices, along_x(): return lax.ppermute(array, 'col', pairs)  7.46 us
    ppermute x5, starting transfers between devices, mate(): return lax.ppermute(array, 'col', [(c, c ^ bits) for c in range(col_size)])  6.63 us
  transfers between devices with their start and end apart: 19, of which 13 were waited for; matrix products, arithmetic and copies ran while one was open for 1% of the time, Pallas kernels for 8%

profile of v7, /device:TPU:0, one launch (start us, length us, event | category | flops | bytes accessed | tf_op | source)
XLA Modules:
  0.0 89.2 jit_solution(1383341060866091019)
XLA Ops:
  0.7 1.1 %and_select_fusion.4 = (bf16[224,256]{1,0:T(8,128)(2,1)S(1)}, bf16[224,256]{1,0:T(8,128)(2,1)S(1)}) fusion(bf16[40,192]{1,0:T(8,128)(2,1)} %param.5, pred[256]{0:T(512)(128)(4,1)S(1)} %iota_compare_fusion, pred[224]{0:T(512)(128)(4,1)S(1)} %get-tuple-element.60, pred[224]{0:T(512)(128)(4,1)S(1)} %get-tuple-element.61, ...), kind=kLoop, calls=%fused_computation.4 | loop fusion | flops 1032192 | bytes 359328 | tf_op jit(solution)/shard_map/jit(_where)/select_n | solution.py:382
  1.8 1.7 %collective-permute-start.1 = (bf16[224,256]{1,0:T(8,128)(2,1)S(1)}, bf16[224,256]{1,0:T(8,128)(2,1)S(1)}, u32[]{:S(2)}, u32[]{:S(2)}) collective-permute-start(bf16[224,256]{1,0:T(8,128)(2,1)S(1)} %get-tuple-element.58), channel_id=1, source_target_pairs={{0,1},{1,0},{2,3},{3,2},{4,5},{5,4},{6,7},{7,6},{8,9},{9,8},{10,11... | collective-permute-start | bytes 344072 | tf_op jit(solution)/shard_map/ppermute | solution.py:360
  3.5 2.2 %collective-permute-start = (bf16[224,256]{1,0:T(8,128)(2,1)S(1)}, bf16[224,256]{1,0:T(8,128)(2,1)S(1)}, u32[]{:S(2)}, u32[]{:S(2)}) collective-permute-start(bf16[224,256]{1,0:T(8,128)(2,1)S(1)} %get-tuple-element.59), channel_id=1, source_target_pairs={{0,17},{1,16},{2,19},{3,18},{4,21},{5,20},{6,23},{7,22},{8,25},{9,... | collective-permute-start | bytes 344072 | tf_op jit(solution)/shard_map/ppermute | solution.py:367
  5.7 0.7 dynamic-slice_bitcast_fusion.place_ref
  6.4 0.3 collective-permute-done.1
  6.7 2.8 %collective-permute-done = bf16[224,256]{1,0:T(8,128)(2,1)S(1)} collective-permute-done((bf16[224,256]{1,0:T(8,128)(2,1)S(1)}, bf16[224,256]{1,0:T(8,128)(2,1)S(1)}, u32[]{:S(2)}, u32[]{:S(2)}) %collective-permute-start) | collective-permute-done | bytes 114720 | tf_op jit(solution)/shard_map/ppermute | solution.py:367
  9.5 1.6 %collective-permute-start.6 = (bf16[2,224,256]{2,1,0:T(8,128)(2,1)S(1)}, bf16[2,224,256]{2,1,0:T(8,128)(2,1)S(1)}, u32[]{:S(2)}, u32[]{:S(2)}) collective-permute-start(bf16[2,224,256]{2,1,0:T(8,128)(2,1)S(1)} %pad_maximum_fusion.1.rest_0_), channel_id=1, source_target_pairs={{0,2},{1,3},{2,4},{3,5},{4,6},{5,7},{6,0},{7,1},{8,10},{9,11},{10,... | collective-permute-start | bytes 688136 | tf_op jit(solution)/shard_map/ppermute | solution.py:360
  11.1 2.7 %collective-permute-start.4 = (bf16[2,224,256]{2,1,0:T(8,128)(2,1)S(1)}, bf16[2,224,256]{2,1,0:T(8,128)(2,1)S(1)}, u32[]{:S(2)}, u32[]{:S(2)}) collective-permute-start(bf16[2,224,256]{2,1,0:T(8,128)(2,1)S(1)} %pad_maximum_fusion.1.rest_0_), channel_id=1, source_target_pairs={{0,4},{1,5},{2,6},{3,7},{4,0},{5,1},{6,2},{7,3},{8,12},{9,13},{10,... | collective-permute-start | bytes 688136 | tf_op jit(solution)/shard_map/ppermute | solution.py:360
  13.8 1.9 %collective-permute-start.7 = (bf16[2,224,256]{2,1,0:T(8,128)(2,1)S(1)}, bf16[2,224,256]{2,1,0:T(8,128)(2,1)S(1)}, u32[]{:S(2)}, u32[]{:S(2)}) collective-permute-start(bf16[2,224,256]{2,1,0:T(8,128)(2,1)S(1)} %pad_maximum_fusion.rest_1_), channel_id=1, source_target_pairs={{0,32},{1,33},{2,34},{3,35},{4,36},{5,37},{6,38},{7,39},{8,40},{9,... | collective-permute-start | bytes 688136 | tf_op jit(solution)/shard_map/ppermute | solution.py:367
  15.7 3.6 %collective-permute-start.5 = (bf16[2,224,256]{2,1,0:T(8,128)(2,1)S(1)}, bf16[2,224,256]{2,1,0:T(8,128)(2,1)S(1)}, u32[]{:S(2)}, u32[]{:S(2)}) collective-permute-start(bf16[2,224,256]{2,1,0:T(8,128)(2,1)S(1)} %pad_maximum_fusion.rest_1_), channel_id=1, source_target_pairs={{0,64},{1,65},{2,66},{3,67},{4,68},{5,69},{6,70},{7,71},{8,72},{9,... | collective-permute-start | bytes 688136 | tf_op jit(solution)/shard_map/ppermute | solution.py:367
  19.3 1.0 %collective-permute-start.3 = (bf16[2,224,256]{2,1,0:T(8,128)(2,1)S(1)}, bf16[2,224,256]{2,1,0:T(8,128)(2,1)S(1)}, u32[]{:S(2)}, u32[]{:S(2)}) collective-permute-start(bf16[2,224,256]{2,1,0:T(8,128)(2,1)S(1)} %pad_maximum_fusion.rest_1_), channel_id=1, source_target_pairs={{0,96},{1,97},{2,98},{3,99},{4,100},{5,101},{6,102},{7,103},{8,104... | collective-permute-start | bytes 688136 | tf_op jit(solution)/shard_map/ppermute | solution.py:367
  20.3 0.0 collective-permute-done.6.rest_6_
  20.3 1.4 %collective-permute-start.2 = (bf16[2,224,256]{2,1,0:T(8,128)(2,1)S(1)}, bf16[2,224,256]{2,1,0:T(8,128)(2,1)S(1)}, u32[]{:S(2)}, u32[]{:S(2)}) collective-permute-start(bf16[2,224,256]{2,1,0:T(8,128)(2,1)S(1)} %pad_maximum_fusion.1.rest_0_), channel_id=1, source_target_pairs={{0,6},{1,7},{2,0},{3,1},{4,2},{5,3},{6,4},{7,5},{8,14},{9,15},{10,... | collective-permute-start | bytes 688136 | tf_op jit(solution)/shard_map/ppermute | solution.py:360
  21.8 0.9 collective-permute-done.4.rest_4_
  22.6 0.0 collective-permute-start.8
  22.6 1.6 %collective-permute-done.7.rest_7_ = bf16[2,224,256]{2,1,0:T(8,128)(2,1)S(1)} collective-permute-done((bf16[2,224,256]{2,1,0:T(8,128)(2,1)S(1)}, bf16[2,224,256]{2,1,0:T(8,128)(2,1)S(1)}, u32[]{:S(2)}, u32[]{:S(2)}) %collective-permute-start.7) | collective-permute-done | bytes 229408 | tf_op jit(solution)/shard_map/ppermute | solution.py:367
  24.2 0.0 collective-permute-start.11
  24.2 3.3 %collective-permute-done.5.rest_5_ = bf16[2,224,256]{2,1,0:T(8,128)(2,1)S(1)} collective-permute-done((bf16[2,224,256]{2,1,0:T(8,128)(2,1)S(1)}, bf16[2,224,256]{2,1,0:T(8,128)(2,1)S(1)}, u32[]{:S(2)}, u32[]{:S(2)}) %collective-permute-start.5) | collective-permute-done | bytes 229408 | tf_op jit(solution)/shard_map/ppermute | solution.py:367
  27.6 0.0 collective-permute-start.10
  27.6 0.0 collective-permute-done.3.rest_3_
  27.6 0.5 collective-permute-start.9
  28.1 0.0 collective-permute-done.2.rest_2_
  28.1 0.0 collective-permute-done.8.rest_8_
  28.1 0.0 collective-permute-done.11.rest_11_
  28.1 1.0 %collective-permute-done.10.rest_10_ = bf16[2,224,256]{2,1,0:T(8,128)(2,1)S(1)} collective-permute-done((bf16[2,224,256]{2,1,0:T(8,128)(2,1)S(1)}, bf16[2,224,256]{2,1,0:T(8,128)(2,1)S(1)}, u32[]{:S(2)}, u32[]{:S(2)}) %collective-permute-start.10) | collective-permute-done | bytes 229408 | tf_op jit(solution)/shard_map/ppermute | solution.py:356
  29.0 0.3 collective-permute-done.9.rest_9_
  29.4 8.7 %row_stats.1 = (bf16[1536,256]{1,0:T(8,128)(2,1)S(1)}, f32[8,4,1536]{2,1,0:T(4,128)S(1)}, bf16[1536,256]{1,0:T(8,128)(2,1)S(1)}, bf16[256,1536]{1,0:T(8,128)(2,1...) custom-call(s32[16]{0:T(128)S(1)} %dynamic-slice_bitcast_fusion.plac, ...), custom_call_target="tpu_custom_call" | custom-call | flops 4831838208 | bytes 8388608 | tf_op jit(solution)/shard_map/row_stats/pallas_call | solution.py:158
  38.1 9.4 %all_to_all.10.stats_ref = f32[8,4,1536]{2,1,0:T(4,128)S(1)} all-to-all(f32[8,4,1536]{2,1,0:T(4,128)S(1)} %get-tuple-element.41), channel_id=1, replica_groups=mesh['row'=16,'col'=8] {'col'}, dimensions={0} | all-to-all | bytes 393216 | tf_op jit(solution)/shard_map/all_to_all | solution.py:394
  47.6 1.2 %weigh.1 = (f32[8,1536]{1,0:T(8,128)S(1)}, bf16[4,192,256]{2,1,0:T(8,128)(2,1)S(1)}, bf16[4,192,256]{2,1,0:T(8,128)(2,1)S(1)}) custom-call(s32[16]{0:T(128)S(1)} %dynamic-slice_bitcast_fusion.place_ref, f32[8,4,1536]{2,1,0:T(4,128)S(1)} %all_to_all.10.stats_ref, bf16[1536,256]{1,0:T(8,128)(2,1)S(1)} %get-tuple-element.42.scaled_ref), custom_call_target="tpu_custom_call" | custom-call | tf_op jit(solution)/shard_map/weigh/pallas_call | solution.py:199
  48.8 6.7 %other_tile.1 = (bf16[8,224,256]{2,1,0:T(8,128)(2,1)S(1)}, f32[48,1536]{1,0:T(8,128)S(1)}) custom-call(s32[16]{0:T(128)S(1)} %dynamic-slice_bitcast_fusion.place_ref, bf16[1536,256]{1,0:T(8,128)(2,1)S(1)} %get-tuple-element.34.a_pair, bf16[256,1536]{1,0:T(8,128)(2,1)S(1)} %get-tuple-element.35.a_pair_t, bf16[1536,128]{1,0:T(8,128)(2,1)S(1)} %get-tuple-element.36.a_src, ...), custom_call_target="tpu_custom_call" | custom-call | flops 6039797760 | bytes 1048576 | tf_op jit(solution)/shard_map/other_tile/pallas_call | solution.py:275
  55.4 0.1 collective-permute-start.12
  55.5 1.3 %collective-permute-start.13 = (bf16[4,192,256]{2,1,0:T(8,128)(2,1)S(1)}, bf16[4,192,256]{2,1,0:T(8,128)(2,1)S(1)}, u32[]{:S(2)}, u32[]{:S(2)}) collective-permute-start(bf16[4,192,256]{2,1,0:T(8,128)(2,1)S(1)} %get-tuple-element.48), channel_id=1, source_target_pairs={{0,1},{1,0},{2,3},{3,2},{4,5},{5,4},{6,7},{7,6},{8,9},{9,8},{10,11... | collective-permute-start | bytes 1179656 | tf_op jit(solution)/shard_map/ppermute | solution.py:353
  56.9 7.5 %own_tile.1 = (bf16[8,224,256]{2,1,0:T(8,128)(2,1)S(1)}, f32[48,1536]{1,0:T(8,128)}, bf16[224,256]{1,0:T(8,128)(2,1)S(1)}, bf16[224,256]{1,0:T(8,128)(2,1)S(1)},...) custom-call(s32[16]{0:T(128)S(1)} %dynamic-slice_bitcast_fusion.place_ref, ...), custom_call_target="tpu_custom_call" | custom-call | flops 1048576 | bytes 1048576 | tf_op jit(solution)/shard_map/own_tile/pallas_call | solution.py:275
  64.3 2.7 %collective-permute-done.13.unread_ref.given_ref = bf16[4,192,256]{2,1,0:T(8,128)(2,1)S(1)} collective-permute-done((bf16[4,192,256]{2,1,0:T(8,128)(2,1)S(1)}, bf16[4,192,256]{2,1,0:T(8,128)(2,1)S(1)}, u32[]{:S(2)}, u32[]{:S(2)}) %collective-permute-start.13) | collective-permute-done | bytes 393248 | tf_op jit(solution)/shard_map/ppermute | solution.py:353
  67.1 0.0 collective-permute-done.12.other_ref
  67.1 1.2 %join_cols.1.rest_4_ = bf16[8,224,256]{2,1,0:T(8,128)(2,1)} custom-call(bf16[8,224,256]{2,1,0:T(8,128)(2,1)S(1)} %get-tuple-element.46.own_ref, bf16[8,224,256]{2,1,0:T(8,128)(2,1)S(1)} %collective-permute-done.12.other_ref, bf16[4,192,256]{2,1,0:T(8,128)(2,1)S(1)} %collective-permute-done.13.unread_ref.given_ref), custom_call_target="tpu_custom_call" | custom-call | tf_op jit(solution)/shard_map/join_cols/pallas_call | solution.py:299
  68.2 5.1 %all-to-all-start.1 = ((bf16[8,224,256]{2,1,0:T(8,128)(2,1)}), bf16[8,224,256]{2,1,0:T(8,128)(2,1)S(1)}, u32[]{:S(2)}, u32[]{:S(2)}) async-start(bf16[8,224,256]{2,1,0:T(8,128)(2,1)} %join_cols.1.rest_4_), calls=%async_computation.1 | async-start | bytes 1835008 | tf_op jit(solution)/shard_map/all_to_all | solution.py:405
  73.4 0.5 collective-permute-start.14
  73.9 3.7 %collective-permute-done.14.twin_ref = bf16[4,32,256]{2,1,0:T(8,128)(2,1)S(1)} collective-permute-done((bf16[4,32,256]{2,1,0:T(8,128)(2,1)S(1)}, bf16[4,32,256]{2,1,0:T(8,128)(2,1)S(1)}, u32[]{:S(2)}, u32[]{:S(2)}) %collective-permute-start.14) | collective-permute-done | bytes 65568 | tf_op jit(solution)/shard_map/ppermute | solution.py:353
  77.6 0.1 join_rows.1
  77.7 0.6 collective-permute-start.15
  78.4 2.1 %collective-permute-start.16 = (bf16[224,256]{1,0:T(8,128)(2,1)S(1)}, bf16[224,256]{1,0:T(8,128)(2,1)S(1)}, u32[]{:S(2)}, u32[]{:S(2)}) collective-permute-start(bf16[224,256]{1,0:T(8,128)(2,1)S(1)} %get-tuple-element.56), channel_id=1, source_target_pairs={{0,4},{1,5},{2,6},{3,7},{4,0},{5,1},{6,2},{7,3},{8,12},{9,13},{10,... | collective-permute-start | bytes 344072 | tf_op jit(solution)/shard_map/ppermute | solution.py:353
  80.4 2.1 %collective-permute-start.17 = (bf16[224,256]{1,0:T(8,128)(2,1)S(1)}, bf16[224,256]{1,0:T(8,128)(2,1)S(1)}, u32[]{:S(2)}, u32[]{:S(2)}) collective-permute-start(bf16[224,256]{1,0:T(8,128)(2,1)S(1)} %get-tuple-element.57), channel_id=1, source_target_pairs={{0,6},{1,7},{2,4},{3,5},{4,2},{5,3},{6,0},{7,1},{8,14},{9,15},{10,... | collective-permute-start | bytes 344072 | tf_op jit(solution)/shard_map/ppermute | solution.py:353
  82.5 0.1 collective-permute-done.15.rest_1_
  82.6 2.1 %collective-permute-done.16.rest_2_ = bf16[224,256]{1,0:T(8,128)(2,1)S(1)} collective-permute-done((bf16[224,256]{1,0:T(8,128)(2,1)S(1)}, bf16[224,256]{1,0:T(8,128)(2,1)S(1)}, u32[]{:S(2)}, u32[]{:S(2)}) %collective-permute-start.16) | collective-permute-done | bytes 114720 | tf_op jit(solution)/shard_map/ppermute | solution.py:353
  84.7 1.8 %collective-permute-done.17.rest_3_ = bf16[224,256]{1,0:T(8,128)(2,1)S(1)} collective-permute-done((bf16[224,256]{1,0:T(8,128)(2,1)S(1)}, bf16[224,256]{1,0:T(8,128)(2,1)S(1)}, u32[]{:S(2)}, u32[]{:S(2)}) %collective-permute-start.17) | collective-permute-done | bytes 114720 | tf_op jit(solution)/shard_map/ppermute | solution.py:353
  86.4 2.0 %all-to-all-done.1.cols_ref = bf16[8,224,256]{2,1,0:T(8,128)(2,1)S(1)} async-done(((bf16[8,224,256]{2,1,0:T(8,128)(2,1)}), bf16[8,224,256]{2,1,0:T(8,128)(2,1)S(1)}, u32[]{:S(2)}, u32[]{:S(2)}) %all-to-all-start.1) | async-done | bytes 917536 | tf_op jit(solution)/shard_map/all_to_all | solution.py:405
  88.4 0.8 finish.1
  (5 shorter events, 0.1 us)
Async XLA Ops:
  1.8 4.9 %collective-permute-start.1 = (bf16[224,256]{1,0:T(8,128)(2,1)S(1)}, bf16[224,256]{1,0:T(8,128)(2,1)S(1)}, u32[]{:S(2)}, u32[]{:S(2)}) collective-permute-start(bf16[224,256]{1,0:T(8,128)(2,1)S(1)} %get-tuple-element.58), channel_id=1, source_target_pairs={{0,1},{1,0},{2,3},{3,2},{4,5},{5,4},{6,7},{7,6},{8,9},{9,8},{10,11... | collective-permute-start | bytes 344072 | tf_op jit(solution)/shard_map/ppermute | solution.py:360
  3.5 6.0 %collective-permute-start = (bf16[224,256]{1,0:T(8,128)(2,1)S(1)}, bf16[224,256]{1,0:T(8,128)(2,1)S(1)}, u32[]{:S(2)}, u32[]{:S(2)}) collective-permute-start(bf16[224,256]{1,0:T(8,128)(2,1)S(1)} %get-tuple-element.59), channel_id=1, source_target_pairs={{0,17},{1,16},{2,19},{3,18},{4,21},{5,20},{6,23},{7,22},{8,25},{9,... | collective-permute-start | bytes 344072 | tf_op jit(solution)/shard_map/ppermute | solution.py:367
  9.5 10.8 %collective-permute-start.6 = (bf16[2,224,256]{2,1,0:T(8,128)(2,1)S(1)}, bf16[2,224,256]{2,1,0:T(8,128)(2,1)S(1)}, u32[]{:S(2)}, u32[]{:S(2)}) collective-permute-start(bf16[2,224,256]{2,1,0:T(8,128)(2,1)S(1)} %pad_maximum_fusion.1.rest_0_), channel_id=1, source_target_pairs={{0,2},{1,3},{2,4},{3,5},{4,6},{5,7},{6,0},{7,1},{8,10},{9,11},{10,... | collective-permute-start | bytes 688136 | tf_op jit(solution)/shard_map/ppermute | solution.py:360
  11.1 11.5 %collective-permute-start.4 = (bf16[2,224,256]{2,1,0:T(8,128)(2,1)S(1)}, bf16[2,224,256]{2,1,0:T(8,128)(2,1)S(1)}, u32[]{:S(2)}, u32[]{:S(2)}) collective-permute-start(bf16[2,224,256]{2,1,0:T(8,128)(2,1)S(1)} %pad_maximum_fusion.1.rest_0_), channel_id=1, source_target_pairs={{0,4},{1,5},{2,6},{3,7},{4,0},{5,1},{6,2},{7,3},{8,12},{9,13},{10,... | collective-permute-start | bytes 688136 | tf_op jit(solution)/shard_map/ppermute | solution.py:360
  13.8 10.4 %collective-permute-start.7 = (bf16[2,224,256]{2,1,0:T(8,128)(2,1)S(1)}, bf16[2,224,256]{2,1,0:T(8,128)(2,1)S(1)}, u32[]{:S(2)}, u32[]{:S(2)}) collective-permute-start(bf16[2,224,256]{2,1,0:T(8,128)(2,1)S(1)} %pad_maximum_fusion.rest_1_), channel_id=1, source_target_pairs={{0,32},{1,33},{2,34},{3,35},{4,36},{5,37},{6,38},{7,39},{8,40},{9,... | collective-permute-start | bytes 688136 | tf_op jit(solution)/shard_map/ppermute | solution.py:367
  15.7 11.8 %collective-permute-start.5 = (bf16[2,224,256]{2,1,0:T(8,128)(2,1)S(1)}, bf16[2,224,256]{2,1,0:T(8,128)(2,1)S(1)}, u32[]{:S(2)}, u32[]{:S(2)}) collective-permute-start(bf16[2,224,256]{2,1,0:T(8,128)(2,1)S(1)} %pad_maximum_fusion.rest_1_), channel_id=1, source_target_pairs={{0,64},{1,65},{2,66},{3,67},{4,68},{5,69},{6,70},{7,71},{8,72},{9,... | collective-permute-start | bytes 688136 | tf_op jit(solution)/shard_map/ppermute | solution.py:367
  19.3 8.2 %collective-permute-start.3 = (bf16[2,224,256]{2,1,0:T(8,128)(2,1)S(1)}, bf16[2,224,256]{2,1,0:T(8,128)(2,1)S(1)}, u32[]{:S(2)}, u32[]{:S(2)}) collective-permute-start(bf16[2,224,256]{2,1,0:T(8,128)(2,1)S(1)} %pad_maximum_fusion.rest_1_), channel_id=1, source_target_pairs={{0,96},{1,97},{2,98},{3,99},{4,100},{5,101},{6,102},{7,103},{8,104... | collective-permute-start | bytes 688136 | tf_op jit(solution)/shard_map/ppermute | solution.py:367
  20.3 7.7 %collective-permute-start.2 = (bf16[2,224,256]{2,1,0:T(8,128)(2,1)S(1)}, bf16[2,224,256]{2,1,0:T(8,128)(2,1)S(1)}, u32[]{:S(2)}, u32[]{:S(2)}) collective-permute-start(bf16[2,224,256]{2,1,0:T(8,128)(2,1)S(1)} %pad_maximum_fusion.1.rest_0_), channel_id=1, source_target_pairs={{0,6},{1,7},{2,0},{3,1},{4,2},{5,3},{6,4},{7,5},{8,14},{9,15},{10,... | collective-permute-start | bytes 688136 | tf_op jit(solution)/shard_map/ppermute | solution.py:360
  22.6 5.5 %collective-permute-start.8 = (bf16[2,224,256]{2,1,0:T(8,128)(2,1)S(1)}, bf16[2,224,256]{2,1,0:T(8,128)(2,1)S(1)}, u32[]{:S(2)}, u32[]{:S(2)}) collective-permute-start(bf16[2,224,256]{2,1,0:T(8,128)(2,1)S(1)} %pad_maximum_fusion.rest_1_), channel_id=1, source_target_pairs={{0,8},{8,0},{16,24},{24,16},{32,40},{40,32},{48,56},{56,48},{64,72... | collective-permute-start | bytes 688136 | tf_op jit(solution)/shard_map/ppermute | solution.py:356
  24.2 3.8 %collective-permute-start.11 = (bf16[2,224,256]{2,1,0:T(8,128)(2,1)S(1)}, bf16[2,224,256]{2,1,0:T(8,128)(2,1)S(1)}, u32[]{:S(2)}, u32[]{:S(2)}) collective-permute-start(bf16[2,224,256]{2,1,0:T(8,128)(2,1)S(1)} %collective-permute-done.7.rest_7_), channel_id=1, source_target_pairs={{0,8},{8,0},{16,24},{24,16},{32,40},{40,32},{48,56},{56,48},{64,72... | collective-permute-start | bytes 688136 | tf_op jit(solution)/shard_map/ppermute | solution.py:356
  27.6 1.5 %collective-permute-start.10 = (bf16[2,224,256]{2,1,0:T(8,128)(2,1)S(1)}, bf16[2,224,256]{2,1,0:T(8,128)(2,1)S(1)}, u32[]{:S(2)}, u32[]{:S(2)}) collective-permute-start(bf16[2,224,256]{2,1,0:T(8,128)(2,1)S(1)} %collective-permute-done.5.rest_5_), channel_id=1, source_target_pairs={{0,8},{8,0},{16,24},{24,16},{32,40},{40,32},{48,56},{56,48},{64,72... | collective-permute-start | bytes 688136 | tf_op jit(solution)/shard_map/ppermute | solution.py:356
  27.6 1.8 %collective-permute-start.9 = (bf16[2,224,256]{2,1,0:T(8,128)(2,1)S(1)}, bf16[2,224,256]{2,1,0:T(8,128)(2,1)S(1)}, u32[]{:S(2)}, u32[]{:S(2)}) collective-permute-start(bf16[2,224,256]{2,1,0:T(8,128)(2,1)S(1)} %collective-permute-done.3.rest_3_), channel_id=1, source_target_pairs={{0,8},{8,0},{16,24},{24,16},{32,40},{40,32},{48,56},{56,48},{64,72... | collective-permute-start | bytes 688136 | tf_op jit(solution)/shard_map/ppermute | solution.py:356
  55.4 11.6 %collective-permute-start.12 = (bf16[8,224,256]{2,1,0:T(8,128)(2,1)S(1)}, bf16[8,224,256]{2,1,0:T(8,128)(2,1)S(1)}, u32[]{:S(2)}, u32[]{:S(2)}) collective-permute-start(bf16[8,224,256]{2,1,0:T(8,128)(2,1)S(1)} %get-tuple-element.47), channel_id=1, source_target_pairs={{0,8},{8,0},{16,24},{24,16},{32,40},{40,32},{48,56},{56,48},{64,72... | collective-permute-start | bytes 2752520 | tf_op jit(solution)/shard_map/ppermute | solution.py:356
  55.5 11.5 %collective-permute-start.13 = (bf16[4,192,256]{2,1,0:T(8,128)(2,1)S(1)}, bf16[4,192,256]{2,1,0:T(8,128)(2,1)S(1)}, u32[]{:S(2)}, u32[]{:S(2)}) collective-permute-start(bf16[4,192,256]{2,1,0:T(8,128)(2,1)S(1)} %get-tuple-element.48), channel_id=1, source_target_pairs={{0,1},{1,0},{2,3},{3,2},{4,5},{5,4},{6,7},{7,6},{8,9},{9,8},{10,11... | collective-permute-start | bytes 1179656 | tf_op jit(solution)/shard_map/ppermute | solution.py:353
  68.2 20.2 %all-to-all-start.1 = ((bf16[8,224,256]{2,1,0:T(8,128)(2,1)}), bf16[8,224,256]{2,1,0:T(8,128)(2,1)S(1)}, u32[]{:S(2)}, u32[]{:S(2)}) async-start(bf16[8,224,256]{2,1,0:T(8,128)(2,1)} %join_cols.1.rest_4_), calls=%async_computation.1 | async-start | bytes 1835008 | tf_op jit(solution)/shard_map/all_to_all | solution.py:405
  73.4 4.3 %collective-permute-start.14 = (bf16[4,32,256]{2,1,0:T(8,128)(2,1)S(1)}, bf16[4,32,256]{2,1,0:T(8,128)(2,1)S(1)}, u32[]{:S(2)}, u32[]{:S(2)}) collective-permute-start(bf16[4,32,256]{2,1,0:T(8,128)(2,1)S(1)} %get-tuple-element.49), channel_id=1, source_target_pairs={{0,1},{1,0},{2,3},{3,2},{4,5},{5,4},{6,7},{7,6},{8,9},{9,8},{10,11... | collective-permute-start | bytes 196616 | tf_op jit(solution)/shard_map/ppermute | solution.py:353
  77.7 4.9 %collective-permute-start.15 = (bf16[224,256]{1,0:T(8,128)(2,1)S(1)}, bf16[224,256]{1,0:T(8,128)(2,1)S(1)}, u32[]{:S(2)}, u32[]{:S(2)}) collective-permute-start(bf16[224,256]{1,0:T(8,128)(2,1)S(1)} %get-tuple-element.55), channel_id=1, source_target_pairs={{0,2},{1,3},{2,0},{3,1},{4,6},{5,7},{6,4},{7,5},{8,10},{9,11},{10,... | collective-permute-start | bytes 344072 | tf_op jit(solution)/shard_map/ppermute | solution.py:353
  78.4 6.3 %collective-permute-start.16 = (bf16[224,256]{1,0:T(8,128)(2,1)S(1)}, bf16[224,256]{1,0:T(8,128)(2,1)S(1)}, u32[]{:S(2)}, u32[]{:S(2)}) collective-permute-start(bf16[224,256]{1,0:T(8,128)(2,1)S(1)} %get-tuple-element.56), channel_id=1, source_target_pairs={{0,4},{1,5},{2,6},{3,7},{4,0},{5,1},{6,2},{7,3},{8,12},{9,13},{10,... | collective-permute-start | bytes 344072 | tf_op jit(solution)/shard_map/ppermute | solution.py:353
  80.4 6.0 %collective-permute-start.17 = (bf16[224,256]{1,0:T(8,128)(2,1)S(1)}, bf16[224,256]{1,0:T(8,128)(2,1)S(1)}, u32[]{:S(2)}, u32[]{:S(2)}) collective-permute-start(bf16[224,256]{1,0:T(8,128)(2,1)S(1)} %get-tuple-element.57), channel_id=1, source_target_pairs={{0,6},{1,7},{2,4},{3,5},{4,2},{5,3},{6,0},{7,1},{8,14},{9,15},{10,... | collective-permute-start | bytes 344072 | tf_op jit(solution)/shard_map/ppermute | solution.py:353

commit v8 on v7

--- a/solution.py
+++ b/solution.py
@@ -151,7 +151,7 @@
     rows = mates * own
     cols = 2 * own * sum(part.shape[0] for part in b0_parts)
     pair = 2 * feat
-    step = pick(rows, LANES, 512)
+    step = pick(rows, LANES, 768)
     kept = [((rows, pair), BF16), ((pair, rows), BF16), ((rows, LANES), BF16), ((LANES, rows), BF16)]
     kept += [((cols, pair), BF16), ((cols, LANES), BF16), ((LANES, cols), BF16)]
     parts = [part for both in zip(a_parts, b0_parts) for part in both] + b1_parts

time: 89.5 us -> 89.3 us (level)
  transfers between devices with their start and end apart: 19 -> 19, of which waited for: 13 -> 13; matrix products, arithmetic and copies ran while one was open for 1% -> 1% of each run, Pallas kernels for 8% -> 9%
where the time goes in v8:
time: 89.3 us; the launch traced here: 89 us
  starting transfers between devices  28.5 us (32%)
  Pallas kernels  26 us (29%)
  waiting for transfers between devices  22.6 us (25%)
  blocking collectives  9.44 us (11%)
  other arithmetic  1.15 us (1%)
    pallas_call x2, Pallas kernels, tile_sums(): pl.pallas_call(functools.partial(tile_kernel, own, feat, half), in_specs=...  14.2 us
    ppermute x5, waiting for transfers between devices, mate(): return lax.ppermute(array, 'col', [(c, c ^ bits) for c in range(col_size)])  10.4 us
    all_to_all x1, blocking collectives, local(): stats = lax.all_to_all(stats, 'col', 0, 0)  9.44 us
    ppermute x4, starting transfers between devices, along_z(): return lax.ppermute(array, both, pairs)  8.69 us
    pallas_call x1, Pallas kernels, row_stats(): pl.pallas_call(functools.partial(stats_kernel, own, feat), grid=(rows //...  8.51 us
    ppermute x4, waiting for transfers between devices, along_z(): return lax.ppermute(array, both, pairs)  7.77 us
    ppermute x4, starting transfers between devices, along_x(): return lax.ppermute(array, 'col', pairs)  7.46 us
    ppermute x5, starting transfers between devices, mate(): return lax.ppermute(array, 'col', [(c, c ^ bits) for c in range(col_size)])  6.62 us
  transfers between devices with their start and end apart: 19, of which 13 were waited for; matrix products, arithmetic and copies ran while one was open for 1% of the time, Pallas kernels for 9%

profile of v8, /device:TPU:0, one launch (start us, length us, event | category | flops | bytes accessed | tf_op | source)
XLA Modules:
  0.0 89.0 jit_solution(427022376006168950)
XLA Ops:
  0.7 1.1 %and_select_fusion.4 = (bf16[224,256]{1,0:T(8,128)(2,1)S(1)}, bf16[224,256]{1,0:T(8,128)(2,1)S(1)}) fusion(bf16[40,192]{1,0:T(8,128)(2,1)} %param.5, pred[256]{0:T(512)(128)(4,1)S(1)} %iota_compare_fusion, pred[224]{0:T(512)(128)(4,1)S(1)} %get-tuple-element.60, pred[224]{0:T(512)(128)(4,1)S(1)} %get-tuple-element.61, ...), kind=kLoop, calls=%fused_computation.4 | loop fusion | flops 1032192 | bytes 359328 | tf_op jit(solution)/shard_map/jit(_where)/select_n | solution.py:382
  1.8 1.7 %collective-permute-start.1 = (bf16[224,256]{1,0:T(8,128)(2,1)S(1)}, bf16[224,256]{1,0:T(8,128)(2,1)S(1)}, u32[]{:S(2)}, u32[]{:S(2)}) collective-permute-start(bf16[224,256]{1,0:T(8,128)(2,1)S(1)} %get-tuple-element.58), channel_id=1, source_target_pairs={{0,1},{1,0},{2,3},{3,2},{4,5},{5,4},{6,7},{7,6},{8,9},{9,8},{10,11... | collective-permute-start | bytes 344072 | tf_op jit(solution)/shard_map/ppermute | solution.py:360
  3.5 2.2 %collective-permute-start = (bf16[224,256]{1,0:T(8,128)(2,1)S(1)}, bf16[224,256]{1,0:T(8,128)(2,1)S(1)}, u32[]{:S(2)}, u32[]{:S(2)}) collective-permute-start(bf16[224,256]{1,0:T(8,128)(2,1)S(1)} %get-tuple-element.59), channel_id=1, source_target_pairs={{0,17},{1,16},{2,19},{3,18},{4,21},{5,20},{6,23},{7,22},{8,25},{9,... | collective-permute-start | bytes 344072 | tf_op jit(solution)/shard_map/ppermute | solution.py:367
  5.7 0.7 dynamic-slice_bitcast_fusion.place_ref
  6.4 0.3 collective-permute-done.1
  6.7 2.8 %collective-permute-done = bf16[224,256]{1,0:T(8,128)(2,1)S(1)} collective-permute-done((bf16[224,256]{1,0:T(8,128)(2,1)S(1)}, bf16[224,256]{1,0:T(8,128)(2,1)S(1)}, u32[]{:S(2)}, u32[]{:S(2)}) %collective-permute-start) | collective-permute-done | bytes 114720 | tf_op jit(solution)/shard_map/ppermute | solution.py:367
  9.5 1.6 %collective-permute-start.6 = (bf16[2,224,256]{2,1,0:T(8,128)(2,1)S(1)}, bf16[2,224,256]{2,1,0:T(8,128)(2,1)S(1)}, u32[]{:S(2)}, u32[]{:S(2)}) collective-permute-start(bf16[2,224,256]{2,1,0:T(8,128)(2,1)S(1)} %pad_maximum_fusion.1.rest_0_), channel_id=1, source_target_pairs={{0,2},{1,3},{2,4},{3,5},{4,6},{5,7},{6,0},{7,1},{8,10},{9,11},{10,... | collective-permute-start | bytes 688136 | tf_op jit(solution)/shard_map/ppermute | solution.py:360
  11.1 2.7 %collective-permute-start.4 = (bf16[2,224,256]{2,1,0:T(8,128)(2,1)S(1)}, bf16[2,224,256]{2,1,0:T(8,128)(2,1)S(1)}, u32[]{:S(2)}, u32[]{:S(2)}) collective-permute-start(bf16[2,224,256]{2,1,0:T(8,128)(2,1)S(1)} %pad_maximum_fusion.1.rest_0_), channel_id=1, source_target_pairs={{0,4},{1,5},{2,6},{3,7},{4,0},{5,1},{6,2},{7,3},{8,12},{9,13},{10,... | collective-permute-start | bytes 688136 | tf_op jit(solution)/shard_map/ppermute | solution.py:360
  13.8 1.9 %collective-permute-start.7 = (bf16[2,224,256]{2,1,0:T(8,128)(2,1)S(1)}, bf16[2,224,256]{2,1,0:T(8,128)(2,1)S(1)}, u32[]{:S(2)}, u32[]{:S(2)}) collective-permute-start(bf16[2,224,256]{2,1,0:T(8,128)(2,1)S(1)} %pad_maximum_fusion.rest_1_), channel_id=1, source_target_pairs={{0,32},{1,33},{2,34},{3,35},{4,36},{5,37},{6,38},{7,39},{8,40},{9,... | collective-permute-start | bytes 688136 | tf_op jit(solution)/shard_map/ppermute | solution.py:367
  15.7 3.6 %collective-permute-start.5 = (bf16[2,224,256]{2,1,0:T(8,128)(2,1)S(1)}, bf16[2,224,256]{2,1,0:T(8,128)(2,1)S(1)}, u32[]{:S(2)}, u32[]{:S(2)}) collective-permute-start(bf16[2,224,256]{2,1,0:T(8,128)(2,1)S(1)} %pad_maximum_fusion.rest_1_), channel_id=1, source_target_pairs={{0,64},{1,65},{2,66},{3,67},{4,68},{5,69},{6,70},{7,71},{8,72},{9,... | collective-permute-start | bytes 688136 | tf_op jit(solution)/shard_map/ppermute | solution.py:367
  19.3 1.0 %collective-permute-start.3 = (bf16[2,224,256]{2,1,0:T(8,128)(2,1)S(1)}, bf16[2,224,256]{2,1,0:T(8,128)(2,1)S(1)}, u32[]{:S(2)}, u32[]{:S(2)}) collective-permute-start(bf16[2,224,256]{2,1,0:T(8,128)(2,1)S(1)} %pad_maximum_fusion.rest_1_), channel_id=1, source_target_pairs={{0,96},{1,97},{2,98},{3,99},{4,100},{5,101},{6,102},{7,103},{8,104... | collective-permute-start | bytes 688136 | tf_op jit(solution)/shard_map/ppermute | solution.py:367
  20.3 0.0 collective-permute-done.6.rest_6_
  20.3 1.4 %collective-permute-start.2 = (bf16[2,224,256]{2,1,0:T(8,128)(2,1)S(1)}, bf16[2,224,256]{2,1,0:T(8,128)(2,1)S(1)}, u32[]{:S(2)}, u32[]{:S(2)}) collective-permute-start(bf16[2,224,256]{2,1,0:T(8,128)(2,1)S(1)} %pad_maximum_fusion.1.rest_0_), channel_id=1, source_target_pairs={{0,6},{1,7},{2,0},{3,1},{4,2},{5,3},{6,4},{7,5},{8,14},{9,15},{10,... | collective-permute-start | bytes 688136 | tf_op jit(solution)/shard_map/ppermute | solution.py:360
  21.8 0.9 collective-permute-done.4.rest_4_
  22.6 0.0 collective-permute-start.8
  22.6 1.6 %collective-permute-done.7.rest_7_ = bf16[2,224,256]{2,1,0:T(8,128)(2,1)S(1)} collective-permute-done((bf16[2,224,256]{2,1,0:T(8,128)(2,1)S(1)}, bf16[2,224,256]{2,1,0:T(8,128)(2,1)S(1)}, u32[]{:S(2)}, u32[]{:S(2)}) %collective-permute-start.7) | collective-permute-done | bytes 229408 | tf_op jit(solution)/shard_map/ppermute | solution.py:367
  24.2 0.0 collective-permute-start.11
  24.2 3.3 %collective-permute-done.5.rest_5_ = bf16[2,224,256]{2,1,0:T(8,128)(2,1)S(1)} collective-permute-done((bf16[2,224,256]{2,1,0:T(8,128)(2,1)S(1)}, bf16[2,224,256]{2,1,0:T(8,128)(2,1)S(1)}, u32[]{:S(2)}, u32[]{:S(2)}) %collective-permute-start.5) | collective-permute-done | bytes 229408 | tf_op jit(solution)/shard_map/ppermute | solution.py:367
  27.6 0.0 collective-permute-start.10
  27.6 0.0 collective-permute-done.3.rest_3_
  27.6 0.5 collective-permute-start.9
  28.1 0.0 collective-permute-done.2.rest_2_
  28.1 0.0 collective-permute-done.8.rest_8_
  28.1 0.0 collective-permute-done.11.rest_11_
  28.1 1.0 %collective-permute-done.10.rest_10_ = bf16[2,224,256]{2,1,0:T(8,128)(2,1)S(1)} collective-permute-done((bf16[2,224,256]{2,1,0:T(8,128)(2,1)S(1)}, bf16[2,224,256]{2,1,0:T(8,128)(2,1)S(1)}, u32[]{:S(2)}, u32[]{:S(2)}) %collective-permute-start.10) | collective-permute-done | bytes 229408 | tf_op jit(solution)/shard_map/ppermute | solution.py:356
  29.0 0.3 collective-permute-done.9.rest_9_
  29.4 8.5 %row_stats.1 = (bf16[1536,256]{1,0:T(8,128)(2,1)S(1)}, f32[8,4,1536]{2,1,0:T(4,128)S(1)}, bf16[1536,256]{1,0:T(8,128)(2,1)S(1)}, bf16[256,1536]{1,0:T(8,128)(2,1...) custom-call(s32[16]{0:T(128)S(1)} %dynamic-slice_bitcast_fusion.plac, ...), custom_call_target="tpu_custom_call" | custom-call | flops 4831838208 | bytes 8388608 | tf_op jit(solution)/shard_map/row_stats/pallas_call | solution.py:158
  37.9 9.4 %all_to_all.10.stats_ref = f32[8,4,1536]{2,1,0:T(4,128)S(1)} all-to-all(f32[8,4,1536]{2,1,0:T(4,128)S(1)} %get-tuple-element.41), channel_id=1, replica_groups=mesh['row'=16,'col'=8] {'col'}, dimensions={0} | all-to-all | bytes 393216 | tf_op jit(solution)/shard_map/all_to_all | solution.py:394
  47.3 1.2 %weigh.1 = (f32[8,1536]{1,0:T(8,128)S(1)}, bf16[4,192,256]{2,1,0:T(8,128)(2,1)S(1)}, bf16[4,192,256]{2,1,0:T(8,128)(2,1)S(1)}) custom-call(s32[16]{0:T(128)S(1)} %dynamic-slice_bitcast_fusion.place_ref, f32[8,4,1536]{2,1,0:T(4,128)S(1)} %all_to_all.10.stats_ref, bf16[1536,256]{1,0:T(8,128)(2,1)S(1)} %get-tuple-element.42.scaled_ref), custom_call_target="tpu_custom_call" | custom-call | tf_op jit(solution)/shard_map/weigh/pallas_call | solution.py:199
  48.5 6.7 %other_tile.1 = (bf16[8,224,256]{2,1,0:T(8,128)(2,1)S(1)}, f32[48,1536]{1,0:T(8,128)S(1)}) custom-call(s32[16]{0:T(128)S(1)} %dynamic-slice_bitcast_fusion.place_ref, bf16[1536,256]{1,0:T(8,128)(2,1)S(1)} %get-tuple-element.34.a_pair, bf16[256,1536]{1,0:T(8,128)(2,1)S(1)} %get-tuple-element.35.a_pair_t, bf16[1536,128]{1,0:T(8,128)(2,1)S(1)} %get-tuple-element.36.a_src, ...), custom_call_target="tpu_custom_call" | custom-call | flops 6039797760 | bytes 1048576 | tf_op jit(solution)/shard_map/other_tile/pallas_call | solution.py:275
  55.2 0.1 collective-permute-start.12
  55.3 1.3 %collective-permute-start.13 = (bf16[4,192,256]{2,1,0:T(8,128)(2,1)S(1)}, bf16[4,192,256]{2,1,0:T(8,128)(2,1)S(1)}, u32[]{:S(2)}, u32[]{:S(2)}) collective-permute-start(bf16[4,192,256]{2,1,0:T(8,128)(2,1)S(1)} %get-tuple-element.48), channel_id=1, source_target_pairs={{0,1},{1,0},{2,3},{3,2},{4,5},{5,4},{6,7},{7,6},{8,9},{9,8},{10,11... | collective-permute-start | bytes 1179656 | tf_op jit(solution)/shard_map/ppermute | solution.py:353
  56.6 7.5 %own_tile.1 = (bf16[8,224,256]{2,1,0:T(8,128)(2,1)S(1)}, f32[48,1536]{1,0:T(8,128)}, bf16[224,256]{1,0:T(8,128)(2,1)S(1)}, bf16[224,256]{1,0:T(8,128)(2,1)S(1)},...) custom-call(s32[16]{0:T(128)S(1)} %dynamic-slice_bitcast_fusion.place_ref, ...), custom_call_target="tpu_custom_call" | custom-call | flops 1048576 | bytes 1048576 | tf_op jit(solution)/shard_map/own_tile/pallas_call | solution.py:275
  64.1 2.7 %collective-permute-done.13.unread_ref.given_ref = bf16[4,192,256]{2,1,0:T(8,128)(2,1)S(1)} collective-permute-done((bf16[4,192,256]{2,1,0:T(8,128)(2,1)S(1)}, bf16[4,192,256]{2,1,0:T(8,128)(2,1)S(1)}, u32[]{:S(2)}, u32[]{:S(2)}) %collective-permute-start.13) | collective-permute-done | bytes 393248 | tf_op jit(solution)/shard_map/ppermute | solution.py:353
  66.8 0.0 collective-permute-done.12.other_ref
  66.8 1.2 %join_cols.1.rest_4_ = bf16[8,224,256]{2,1,0:T(8,128)(2,1)} custom-call(bf16[8,224,256]{2,1,0:T(8,128)(2,1)S(1)} %get-tuple-element.46.own_ref, bf16[8,224,256]{2,1,0:T(8,128)(2,1)S(1)} %collective-permute-done.12.other_ref, bf16[4,192,256]{2,1,0:T(8,128)(2,1)S(1)} %collective-permute-done.13.unread_ref.given_ref), custom_call_target="tpu_custom_call" | custom-call | tf_op jit(solution)/shard_map/join_cols/pallas_call | solution.py:299
  68.0 5.1 %all-to-all-start.1 = ((bf16[8,224,256]{2,1,0:T(8,128)(2,1)}), bf16[8,224,256]{2,1,0:T(8,128)(2,1)S(1)}, u32[]{:S(2)}, u32[]{:S(2)}) async-start(bf16[8,224,256]{2,1,0:T(8,128)(2,1)} %join_cols.1.rest_4_), calls=%async_computation.1 | async-start | bytes 1835008 | tf_op jit(solution)/shard_map/all_to_all | solution.py:405
  73.1 0.5 collective-permute-start.14
  73.7 3.7 %collective-permute-done.14.twin_ref = bf16[4,32,256]{2,1,0:T(8,128)(2,1)S(1)} collective-permute-done((bf16[4,32,256]{2,1,0:T(8,128)(2,1)S(1)}, bf16[4,32,256]{2,1,0:T(8,128)(2,1)S(1)}, u32[]{:S(2)}, u32[]{:S(2)}) %collective-permute-start.14) | collective-permute-done | bytes 65568 | tf_op jit(solution)/shard_map/ppermute | solution.py:353
  77.4 0.1 join_rows.1
  77.5 0.6 collective-permute-start.15
  78.2 2.1 %collective-permute-start.16 = (bf16[224,256]{1,0:T(8,128)(2,1)S(1)}, bf16[224,256]{1,0:T(8,128)(2,1)S(1)}, u32[]{:S(2)}, u32[]{:S(2)}) collective-permute-start(bf16[224,256]{1,0:T(8,128)(2,1)S(1)} %get-tuple-element.56), channel_id=1, source_target_pairs={{0,4},{1,5},{2,6},{3,7},{4,0},{5,1},{6,2},{7,3},{8,12},{9,13},{10,... | collective-permute-start | bytes 344072 | tf_op jit(solution)/shard_map/ppermute | solution.py:353
  80.2 2.1 %collective-permute-start.17 = (bf16[224,256]{1,0:T(8,128)(2,1)S(1)}, bf16[224,256]{1,0:T(8,128)(2,1)S(1)}, u32[]{:S(2)}, u32[]{:S(2)}) collective-permute-start(bf16[224,256]{1,0:T(8,128)(2,1)S(1)} %get-tuple-element.57), channel_id=1, source_target_pairs={{0,6},{1,7},{2,4},{3,5},{4,2},{5,3},{6,0},{7,1},{8,14},{9,15},{10,... | collective-permute-start | bytes 344072 | tf_op jit(solution)/shard_map/ppermute | solution.py:353
  82.3 0.1 collective-permute-done.15.rest_1_
  82.4 2.1 %collective-permute-done.16.rest_2_ = bf16[224,256]{1,0:T(8,128)(2,1)S(1)} collective-permute-done((bf16[224,256]{1,0:T(8,128)(2,1)S(1)}, bf16[224,256]{1,0:T(8,128)(2,1)S(1)}, u32[]{:S(2)}, u32[]{:S(2)}) %collective-permute-start.16) | collective-permute-done | bytes 114720 | tf_op jit(solution)/shard_map/ppermute | solution.py:353
  84.5 1.8 %collective-permute-done.17.rest_3_ = bf16[224,256]{1,0:T(8,128)(2,1)S(1)} collective-permute-done((bf16[224,256]{1,0:T(8,128)(2,1)S(1)}, bf16[224,256]{1,0:T(8,128)(2,1)S(1)}, u32[]{:S(2)}, u32[]{:S(2)}) %collective-permute-start.17) | collective-permute-done | bytes 114720 | tf_op jit(solution)/shard_map/ppermute | solution.py:353
  86.2 2.0 %all-to-all-done.1.cols_ref = bf16[8,224,256]{2,1,0:T(8,128)(2,1)S(1)} async-done(((bf16[8,224,256]{2,1,0:T(8,128)(2,1)}), bf16[8,224,256]{2,1,0:T(8,128)(2,1)S(1)}, u32[]{:S(2)}, u32[]{:S(2)}) %all-to-all-start.1) | async-done | bytes 917536 | tf_op jit(solution)/shard_map/all_to_all | solution.py:405
  88.2 0.8 finish.1
  (5 shorter events, 0.1 us)
Async XLA Ops:
  1.8 4.9 %collective-permute-start.1 = (bf16[224,256]{1,0:T(8,128)(2,1)S(1)}, bf16[224,256]{1,0:T(8,128)(2,1)S(1)}, u32[]{:S(2)}, u32[]{:S(2)}) collective-permute-start(bf16[224,256]{1,0:T(8,128)(2,1)S(1)} %get-tuple-element.58), channel_id=1, source_target_pairs={{0,1},{1,0},{2,3},{3,2},{4,5},{5,4},{6,7},{7,6},{8,9},{9,8},{10,11... | collective-permute-start | bytes 344072 | tf_op jit(solution)/shard_map/ppermute | solution.py:360
  3.5 6.0 %collective-permute-start = (bf16[224,256]{1,0:T(8,128)(2,1)S(1)}, bf16[224,256]{1,0:T(8,128)(2,1)S(1)}, u32[]{:S(2)}, u32[]{:S(2)}) collective-permute-start(bf16[224,256]{1,0:T(8,128)(2,1)S(1)} %get-tuple-element.59), channel_id=1, source_target_pairs={{0,17},{1,16},{2,19},{3,18},{4,21},{5,20},{6,23},{7,22},{8,25},{9,... | collective-permute-start | bytes 344072 | tf_op jit(solution)/shard_map/ppermute | solution.py:367
  9.5 10.8 %collective-permute-start.6 = (bf16[2,224,256]{2,1,0:T(8,128)(2,1)S(1)}, bf16[2,224,256]{2,1,0:T(8,128)(2,1)S(1)}, u32[]{:S(2)}, u32[]{:S(2)}) collective-permute-start(bf16[2,224,256]{2,1,0:T(8,128)(2,1)S(1)} %pad_maximum_fusion.1.rest_0_), channel_id=1, source_target_pairs={{0,2},{1,3},{2,4},{3,5},{4,6},{5,7},{6,0},{7,1},{8,10},{9,11},{10,... | collective-permute-start | bytes 688136 | tf_op jit(solution)/shard_map/ppermute | solution.py:360
  11.1 11.5 %collective-permute-start.4 = (bf16[2,224,256]{2,1,0:T(8,128)(2,1)S(1)}, bf16[2,224,256]{2,1,0:T(8,128)(2,1)S(1)}, u32[]{:S(2)}, u32[]{:S(2)}) collective-permute-start(bf16[2,224,256]{2,1,0:T(8,128)(2,1)S(1)} %pad_maximum_fusion.1.rest_0_), channel_id=1, source_target_pairs={{0,4},{1,5},{2,6},{3,7},{4,0},{5,1},{6,2},{7,3},{8,12},{9,13},{10,... | collective-permute-start | bytes 688136 | tf_op jit(solution)/shard_map/ppermute | solution.py:360
  13.8 10.4 %collective-permute-start.7 = (bf16[2,224,256]{2,1,0:T(8,128)(2,1)S(1)}, bf16[2,224,256]{2,1,0:T(8,128)(2,1)S(1)}, u32[]{:S(2)}, u32[]{:S(2)}) collective-permute-start(bf16[2,224,256]{2,1,0:T(8,128)(2,1)S(1)} %pad_maximum_fusion.rest_1_), channel_id=1, source_target_pairs={{0,32},{1,33},{2,34},{3,35},{4,36},{5,37},{6,38},{7,39},{8,40},{9,... | collective-permute-start | bytes 688136 | tf_op jit(solution)/shard_map/ppermute | solution.py:367
  15.7 11.8 %collective-permute-start.5 = (bf16[2,224,256]{2,1,0:T(8,128)(2,1)S(1)}, bf16[2,224,256]{2,1,0:T(8,128)(2,1)S(1)}, u32[]{:S(2)}, u32[]{:S(2)}) collective-permute-start(bf16[2,224,256]{2,1,0:T(8,128)(2,1)S(1)} %pad_maximum_fusion.rest_1_), channel_id=1, source_target_pairs={{0,64},{1,65},{2,66},{3,67},{4,68},{5,69},{6,70},{7,71},{8,72},{9,... | collective-permute-start | bytes 688136 | tf_op jit(solution)/shard_map/ppermute | solution.py:367
  19.3 8.2 %collective-permute-start.3 = (bf16[2,224,256]{2,1,0:T(8,128)(2,1)S(1)}, bf16[2,224,256]{2,1,0:T(8,128)(2,1)S(1)}, u32[]{:S(2)}, u32[]{:S(2)}) collective-permute-start(bf16[2,224,256]{2,1,0:T(8,128)(2,1)S(1)} %pad_maximum_fusion.rest_1_), channel_id=1, source_target_pairs={{0,96},{1,97},{2,98},{3,99},{4,100},{5,101},{6,102},{7,103},{8,104... | collective-permute-start | bytes 688136 | tf_op jit(solution)/shard_map/ppermute | solution.py:367
  20.3 7.7 %collective-permute-start.2 = (bf16[2,224,256]{2,1,0:T(8,128)(2,1)S(1)}, bf16[2,224,256]{2,1,0:T(8,128)(2,1)S(1)}, u32[]{:S(2)}, u32[]{:S(2)}) collective-permute-start(bf16[2,224,256]{2,1,0:T(8,128)(2,1)S(1)} %pad_maximum_fusion.1.rest_0_), channel_id=1, source_target_pairs={{0,6},{1,7},{2,0},{3,1},{4,2},{5,3},{6,4},{7,5},{8,14},{9,15},{10,... | collective-permute-start | bytes 688136 | tf_op jit(solution)/shard_map/ppermute | solution.py:360
  22.6 5.5 %collective-permute-start.8 = (bf16[2,224,256]{2,1,0:T(8,128)(2,1)S(1)}, bf16[2,224,256]{2,1,0:T(8,128)(2,1)S(1)}, u32[]{:S(2)}, u32[]{:S(2)}) collective-permute-start(bf16[2,224,256]{2,1,0:T(8,128)(2,1)S(1)} %pad_maximum_fusion.rest_1_), channel_id=1, source_target_pairs={{0,8},{8,0},{16,24},{24,16},{32,40},{40,32},{48,56},{56,48},{64,72... | collective-permute-start | bytes 688136 | tf_op jit(solution)/shard_map/ppermute | solution.py:356
  24.2 3.8 %collective-permute-start.11 = (bf16[2,224,256]{2,1,0:T(8,128)(2,1)S(1)}, bf16[2,224,256]{2,1,0:T(8,128)(2,1)S(1)}, u32[]{:S(2)}, u32[]{:S(2)}) collective-permute-start(bf16[2,224,256]{2,1,0:T(8,128)(2,1)S(1)} %collective-permute-done.7.rest_7_), channel_id=1, source_target_pairs={{0,8},{8,0},{16,24},{24,16},{32,40},{40,32},{48,56},{56,48},{64,72... | collective-permute-start | bytes 688136 | tf_op jit(solution)/shard_map/ppermute | solution.py:356
  27.6 1.5 %collective-permute-start.10 = (bf16[2,224,256]{2,1,0:T(8,128)(2,1)S(1)}, bf16[2,224,256]{2,1,0:T(8,128)(2,1)S(1)}, u32[]{:S(2)}, u32[]{:S(2)}) collective-permute-start(bf16[2,224,256]{2,1,0:T(8,128)(2,1)S(1)} %collective-permute-done.5.rest_5_), channel_id=1, source_target_pairs={{0,8},{8,0},{16,24},{24,16},{32,40},{40,32},{48,56},{56,48},{64,72... | collective-permute-start | bytes 688136 | tf_op jit(solution)/shard_map/ppermute | solution.py:356
  27.6 1.8 %collective-permute-start.9 = (bf16[2,224,256]{2,1,0:T(8,128)(2,1)S(1)}, bf16[2,224,256]{2,1,0:T(8,128)(2,1)S(1)}, u32[]{:S(2)}, u32[]{:S(2)}) collective-permute-start(bf16[2,224,256]{2,1,0:T(8,128)(2,1)S(1)} %collective-permute-done.3.rest_3_), channel_id=1, source_target_pairs={{0,8},{8,0},{16,24},{24,16},{32,40},{40,32},{48,56},{56,48},{64,72... | collective-permute-start | bytes 688136 | tf_op jit(solution)/shard_map/ppermute | solution.py:356
  55.2 11.6 %collective-permute-start.12 = (bf16[8,224,256]{2,1,0:T(8,128)(2,1)S(1)}, bf16[8,224,256]{2,1,0:T(8,128)(2,1)S(1)}, u32[]{:S(2)}, u32[]{:S(2)}) collective-permute-start(bf16[8,224,256]{2,1,0:T(8,128)(2,1)S(1)} %get-tuple-element.47), channel_id=1, source_target_pairs={{0,8},{8,0},{16,24},{24,16},{32,40},{40,32},{48,56},{56,48},{64,72... | collective-permute-start | bytes 2752520 | tf_op jit(solution)/shard_map/ppermute | solution.py:356
  55.3 11.5 %collective-permute-start.13 = (bf16[4,192,256]{2,1,0:T(8,128)(2,1)S(1)}, bf16[4,192,256]{2,1,0:T(8,128)(2,1)S(1)}, u32[]{:S(2)}, u32[]{:S(2)}) collective-permute-start(bf16[4,192,256]{2,1,0:T(8,128)(2,1)S(1)} %get-tuple-element.48), channel_id=1, source_target_pairs={{0,1},{1,0},{2,3},{3,2},{4,5},{5,4},{6,7},{7,6},{8,9},{9,8},{10,11... | collective-permute-start | bytes 1179656 | tf_op jit(solution)/shard_map/ppermute | solution.py:353
  68.0 20.2 %all-to-all-start.1 = ((bf16[8,224,256]{2,1,0:T(8,128)(2,1)}), bf16[8,224,256]{2,1,0:T(8,128)(2,1)S(1)}, u32[]{:S(2)}, u32[]{:S(2)}) async-start(bf16[8,224,256]{2,1,0:T(8,128)(2,1)} %join_cols.1.rest_4_), calls=%async_computation.1 | async-start | bytes 1835008 | tf_op jit(solution)/shard_map/all_to_all | solution.py:405
  73.1 4.3 %collective-permute-start.14 = (bf16[4,32,256]{2,1,0:T(8,128)(2,1)S(1)}, bf16[4,32,256]{2,1,0:T(8,128)(2,1)S(1)}, u32[]{:S(2)}, u32[]{:S(2)}) collective-permute-start(bf16[4,32,256]{2,1,0:T(8,128)(2,1)S(1)} %get-tuple-element.49), channel_id=1, source_target_pairs={{0,1},{1,0},{2,3},{3,2},{4,5},{5,4},{6,7},{7,6},{8,9},{9,8},{10,11... | collective-permute-start | bytes 196616 | tf_op jit(solution)/shard_map/ppermute | solution.py:353
  77.5 4.9 %collective-permute-start.15 = (bf16[224,256]{1,0:T(8,128)(2,1)S(1)}, bf16[224,256]{1,0:T(8,128)(2,1)S(1)}, u32[]{:S(2)}, u32[]{:S(2)}) collective-permute-start(bf16[224,256]{1,0:T(8,128)(2,1)S(1)} %get-tuple-element.55), channel_id=1, source_target_pairs={{0,2},{1,3},{2,0},{3,1},{4,6},{5,7},{6,4},{7,5},{8,10},{9,11},{10,... | collective-permute-start | bytes 344072 | tf_op jit(solution)/shard_map/ppermute | solution.py:353
  78.2 6.3 %collective-permute-start.16 = (bf16[224,256]{1,0:T(8,128)(2,1)S(1)}, bf16[224,256]{1,0:T(8,128)(2,1)S(1)}, u32[]{:S(2)}, u32[]{:S(2)}) collective-permute-start(bf16[224,256]{1,0:T(8,128)(2,1)S(1)} %get-tuple-element.56), channel_id=1, source_target_pairs={{0,4},{1,5},{2,6},{3,7},{4,0},{5,1},{6,2},{7,3},{8,12},{9,13},{10,... | collective-permute-start | bytes 344072 | tf_op jit(solution)/shard_map/ppermute | solution.py:353
  80.2 6.0 %collective-permute-start.17 = (bf16[224,256]{1,0:T(8,128)(2,1)S(1)}, bf16[224,256]{1,0:T(8,128)(2,1)S(1)}, u32[]{:S(2)}, u32[]{:S(2)}) collective-permute-start(bf16[224,256]{1,0:T(8,128)(2,1)S(1)} %get-tuple-element.57), channel_id=1, source_target_pairs={{0,6},{1,7},{2,4},{3,5},{4,2},{5,3},{6,0},{7,1},{8,14},{9,15},{10,... | collective-permute-start | bytes 344072 | tf_op jit(solution)/shard_map/ppermute | solution.py:353
